TPU v7x, 128 devices: a whole 4x4x4 slice. The times are simulated.
128 devices in a mesh: gx: 8 (over y, core), gy: 16 (over x, z).
Axes of the slice: x: 4, y: 4, z: 4, core: 2. Of those that a mesh axis runs over, the one named last changes fastest.
Arguments:
- density_blocks: bfloat16 [8192, 128, 128], P(('gx', 'gy')), may hold values from -0.01171875 to 0.01171875
- send_table: int32 [128, 3, 3, 8], P(('gx', 'gy')), may hold values from -1 to 63, as said below
- batch_pairs: int32 [32, 192, 4, 4], P('gx', 'gy'), may hold values from -1 to 71, as said below
- basis_values: bfloat16 [32, 192, 4, 256, 128], P('gx', 'gy'), may hold values from -6 to 6
- previous_hartree: float32 [32, 192, 256], P('gx', 'gy'), may hold values from -6 to 6
- external_potential: float32 [32, 192, 256], P('gx', 'gy'), may hold values from -6 to 6
Outputs:
- density: float32 [32, 192, 256], P('gx', 'gy')
- hartree: float32 [32, 192, 256], P('gx', 'gy')
- potential_blocks: float32 [8192, 128, 128], P(('gx', 'gy'))
Inputs may be any that keep to these rules, and one draw needn't show every extreme that they name: send_table[s, i, j, c] is owner s's local index of the pair block in slot c for the brick at mesh offset (i - 1, j - 1) from s, or -1; an entry is filled exactly when some batch of that brick names the slot, is -1 toward bricks outside the mesh, and in every draw some brick has all 72 of its slots filled. `batch_pairs`: entry [n, a, b] is the received slot (k * 3 + l) * 8 + c of the density block for orbital blocks a and b of batch n, naming the owner at mesh offset (k - 1, l - 1) from the batch's brick, never one outside the mesh; -1 where the pair has no block; the share of pairs with a block varies from brick to brick.
All inputs are finite; a program needn't handle non-finite values.
Results may differ from a plain program's by a relative error of at most 0.0029.
Values may be sent and summed in bfloat16 or wider, within the bound.
No kernel may reach another device: no remote copies, remote signals or barrier semaphores. Data moves between devices by JAX's collectives and lax.ppermute only.
A program may use at most 256 MiB of HBM per device.

v0:
```python
import jax
import jax.numpy as jnp
from jax import lax
from jax.sharding import PartitionSpec as P

SWEEPS = 3


cell_volume = 0.0625


def padded(value, sides, width):
    for axis, dim in sides:
        count, length = (lax.axis_size(axis), value.shape[dim])
        up = [(i, (i + 1) % count) for i in range(count - 1)]
        down = [(j, i) for i, j in up]
        last = lax.slice_in_dim(value, length - width, length, axis=dim)
        initial = lax.slice_in_dim(value, 0, width, axis=dim)
        before = lax.ppermute(last, axis, up)
        after = lax.ppermute(initial, axis, down)
        value = jnp.concatenate([before, value, after], axis=dim)
    return value


def stencil(extended, charge):
    z_padded = jnp.pad(extended, ((0, 0), (0, 0), (1, 1)))
    beside = z_padded[2:, 1:-1, 1:-1] + z_padded[:-2, 1:-1, 1:-1]
    beside = beside + z_padded[1:-1, 2:, 1:-1] + z_padded[1:-1, :-2, 1:-1]
    beside = beside + z_padded[1:-1, 1:-1, 2:] + z_padded[1:-1, 1:-1, :-2]
    return (beside + charge) / 6.0


def blocks_around(outgoing):
    extended = padded(outgoing, (("gx", 0), ("gy", 1)), 1)
    return extended[0::2, 0::2]


def partials_around(partial_value):
    extended = padded(partial_value, (("gx", 0), ("gy", 1)), 1)
    return extended[0::2, 0::2]


def per_device(
    density_blocks, send_table, batch_pairs, basis_values, previous_hartree, external_potential
):
    block_width = density_blocks.shape[1]
    owned_count = density_blocks.shape[0]
    rows_sent = send_table[0]
    slot_depth = rows_sent.shape[2]
    slot_count = 9 * slot_depth
    chosen = jnp.clip(rows_sent, 0, owned_count - 1)
    outgoing = jnp.where(
        (rows_sent >= 0)[..., None, None], density_blocks[chosen], jnp.zeros((), jnp.bfloat16)
    )
    arrived = blocks_around(outgoing).reshape(slot_count, block_width, block_width)
    brick_x, brick_y, block_count, column_len = (
        basis_values.shape[0],
        basis_values.shape[1],
        basis_values.shape[2],
        basis_values.shape[3],
    )
    batch_count = brick_x * brick_y
    basis_cols = basis_values.reshape(batch_count, block_count, column_len, block_width)
    pair_slots = batch_pairs.reshape(batch_count, block_count, block_count)
    live_mask = pair_slots >= 0
    picked = jnp.where(
        live_mask[..., None, None],
        arrived[jnp.clip(pair_slots, 0, slot_count - 1)],
        jnp.zeros((), jnp.bfloat16),
    )
    mixed_rows = jnp.einsum(
        "nbzv,nabuv->nazu", basis_cols, picked, preferred_element_type=jnp.float32
    )
    density = jnp.sum(basis_cols.astype(jnp.float32) * mixed_rows, axis=(1, 3)).reshape(
        brick_x, brick_y, column_len
    )
    hartree = previous_hartree
    for sweep_index in range(SWEEPS):
        extended = padded(hartree, (("gx", 0), ("gy", 1)), 1)
        hartree = stencil(extended, density)
    total_field = (hartree + external_potential).reshape(batch_count, column_len)
    weighted = (total_field[:, None, :, None] * basis_cols).astype(jnp.bfloat16)
    integrals = cell_volume * jnp.einsum(
        "nazu,nbzv->nabuv", basis_cols, weighted, preferred_element_type=jnp.float32
    )
    flat_integrals = integrals.reshape(-1, block_width * block_width)
    slot_target = jnp.where(live_mask, pair_slots, slot_count).reshape(-1)
    slot_onehot = (slot_target[None, :] == jnp.arange(slot_count)[:, None]).astype(jnp.float32)
    partial_value = jnp.dot(
        slot_onehot,
        flat_integrals,
        precision=lax.Precision.HIGHEST,
        preferred_element_type=jnp.float32,
    )
    returned = partials_around(partial_value.reshape(3, 3, slot_depth, block_width, block_width))
    owner_rows = jnp.where(rows_sent >= 0, rows_sent, owned_count).reshape(-1)
    owner_onehot = (jnp.arange(owned_count)[:, None] == owner_rows[None, :]).astype(jnp.float32)
    potential = jnp.dot(
        owner_onehot,
        returned.reshape(-1, block_width * block_width),
        precision=lax.Precision.HIGHEST,
        preferred_element_type=jnp.float32,
    )
    return (density, hartree, potential.reshape(owned_count, block_width, block_width))


def solution(mesh):
    in_specs = (
        P(("gx", "gy"), None, None),
        P(("gx", "gy"), None, None, None),
        P("gx", "gy", None, None),
        P("gx", "gy", None, None, None),
        P("gx", "gy", None),
        P("gx", "gy", None),
    )
    out_specs = (P("gx", "gy", None), P("gx", "gy", None), P(("gx", "gy"), None, None))
    return jax.shard_map(
        per_device, mesh=mesh, in_specs=in_specs, out_specs=out_specs, check_vma=False
    )
```

profile of v0, /device:TPU:13, one launch (start us, length us, event | category | flops | bytes accessed | tf_op | source)
XLA Modules:
  0.0 381.9 jit_solution(654535008873299456)
XLA Ops:
  13.7 8.0 %collective-permute-done.1 = bf16[1,3,8,128,128]{4,3,2,1,0:T(8,128)(2,1)S(1)} collective-permute-done((bf16[1,3,8,128,128]{4,3,2,1,0:T(8,128)(2,1)S(1)}, bf16[1,3,8,128,128]{4,3,2,1,0:T(8,128)(2,1)S(1)}, u32[]{:S(2)}, u32[]{:S(2)}) %collective-permute-start.1) | collective-permute-done | bytes 786464 | tf_op jit(solution)/shard_map/ppermute | solution.py:20
  25.2 5.6 %collective-permute-start.3 = (bf16[5,1,8,128,128]{4,3,2,1,0:T(8,128)(2,1)}, bf16[5,1,8,128,128]{4,3,2,1,0:T(8,128)(2,1)}, u32[]{:S(2)}, u32[]{:S(2)}) collective-permute-start(bf16[5,1,8,128,128]{4,3,2,1,0:T(8,128)(2,1)} %get-tuple-element.16), channel_id=1, source_target_pairs={{1,0},{2,1},{3,2},{4,3},{5,4},{6,5},{7,6},{8,7},{9,8},{10,9},{11,1... | collective-permute-start | bytes 3932168 | tf_op jit(solution)/shard_map/ppermute | solution.py:20
  32.8 4.7 %collective-permute-start.5 = (f32[1,12,256]{2,1,0:T(8,128)S(1)}, f32[1,12,256]{2,1,0:T(8,128)S(1)}, u32[]{:S(2)}, u32[]{:S(2)}) collective-permute-start(f32[1,12,256]{2,1,0:T(8,128)S(1)} %get-tuple-element.30), channel_id=1, source_target_pairs={{0,16},{16,32},{32,48},{48,64},{64,80},{80,96},{96,112},{1,17},{17... | collective-permute-start | bytes 36872 | tf_op jit(solution)/shard_map/ppermute | solution.py:19
  39.5 3.5 collective-permute-done.4
  43.0 5.8 %collective-permute-start.6 = (f32[6,1,256]{2,1,0:T(1,128)S(1)}, f32[6,1,256]{2,1,0:T(1,128)S(1)}, u32[]{:S(2)}, u32[]{:S(2)}) collective-permute-start(f32[6,1,256]{2,1,0:T(1,128)S(1)} %get-tuple-element.24), channel_id=1, source_target_pairs={{1,0},{2,1},{3,2},{4,3},{5,4},{6,5},{7,6},{8,7},{9,8},{10,9},{11,1... | collective-permute-start | bytes 18440 | tf_op jit(solution)/shard_map/ppermute | solution.py:20
  50.7 16.6 %copy.13 = bf16[4,12,4,256,128]{3,4,2,1,0:T(8,128)(2,1)} copy(bf16[4,12,4,256,128]{4,3,2,1,0:T(8,128)(2,1)} %param.9) | data formatting | bytes 25165824 | tf_op args[3]
  67.8 3.2 pad_maximum_fusion.1
  71.2 18.7 %gather_fusion.1 = bf16[768,128,128]{2,1,0:T(8,128)(2,1)} fusion(bf16[72,128,128]{2,1,0:T(8,128)(2,1)S(1)} %bitcast.57, s32[1024]{0:T(1024)S(1)} %get-tuple-element.31), kind=kCustom, calls=%fused_computation.1 | custom fusion | bytes 50334720 | tf_op jit(solution)/shard_map/gather | solution.py:68
  90.0 18.1 %fusion.3 = f32[48,256]{1,0:T(8,128)S(1)} fusion(bf16[4,12,4,256,128]{3,4,2,1,0:T(8,128)(2,1)} %copy.13, bf16[48,4,256,128,1]{3,2,1,4,0:T(8,128)(2,1)} %bitcast.61, bf16[48,4,4,128,128]{4,3,2,1,0:T(8,128)(2,1)} %bitcast.64, pred[48,4,4]{2,1,0:T(4,128)(4,1)S(1)} %bitcast.67), kind=kOutput, calls=%fused_computation.8 | convolution fusion | flops 6473895936 | bytes 50381568 | tf_op jit(solution)/shard_map/nbzv,nabuv->nazu/dot_general | solution.py:71
  110.2 3.6 collective-permute-start.9
  114.7 5.5 %collective-permute-start.10 = (f32[6,1,256]{2,1,0:T(1,128)S(1)}, f32[6,1,256]{2,1,0:T(1,128)S(1)}, u32[]{:S(2)}, u32[]{:S(2)}) collective-permute-start(f32[6,1,256]{2,1,0:T(1,128)S(1)} %get-tuple-element.22), channel_id=1, source_target_pairs={{1,0},{2,1},{3,2},{4,3},{5,4},{6,5},{7,6},{8,7},{9,8},{10,9},{11,1... | collective-permute-start | bytes 18440 | tf_op jit(solution)/shard_map/ppermute | solution.py:20
  122.1 4.5 %collective-permute-done.11 = f32[6,1,256]{2,1,0:T(1,128)S(1)} collective-permute-done((f32[6,1,256]{2,1,0:T(1,128)S(1)}, f32[6,1,256]{2,1,0:T(1,128)S(1)}, u32[]{:S(2)}, u32[]{:S(2)}) %collective-permute-start.11) | collective-permute-done | bytes 6176 | tf_op jit(solution)/shard_map/ppermute | solution.py:19
  126.9 5.0 %collective-permute-start.12 = (f32[1,12,256]{2,1,0:T(8,128)S(1)}, f32[1,12,256]{2,1,0:T(8,128)S(1)}, u32[]{:S(2)}, u32[]{:S(2)}) collective-permute-start(f32[1,12,256]{2,1,0:T(8,128)S(1)} %get-tuple-element.26), channel_id=1, source_target_pairs={{16,0},{32,16},{48,32},{64,48},{80,64},{96,80},{112,96},{17,1},{33... | collective-permute-start | bytes 36872 | tf_op jit(solution)/shard_map/ppermute | solution.py:20
  137.3 3.5 collective-permute-start.15
  144.1 25.6 %multiply_bitcast_fusion = f32[48,4,4,128,128]{3,4,1,2,0:T(8,128)} fusion(bf16[48,4,256,128,1]{3,2,1,4,0:T(8,128)(2,1)} %bitcast.62, bf16[48,4,256,128]{2,3,1,0:T(8,128)(2,1)} %bitcast.63, f32[48,256]{1,0:T(8,128)S(1)} %mul.23), kind=kOutput, calls=%fused_computation.5 | convolution fusion | flops 6473908224 | bytes 75546624 | tf_op jit(solution)/shard_map/nazu,nbzv->nabuv/dot_general | solution.py:83
  169.7 49.0 %copy.27 = f32[48,4,4,128,128]{4,3,2,1,0:T(8,128)} copy(f32[48,4,4,128,128]{3,4,1,2,0:T(8,128)} %multiply_bitcast_fusion) | data formatting | bytes 100663296 | tf_op jit(solution)/shard_map/mul | solution.py:83
  218.6 58.2 %fusion = f32[72,16384]{1,0:T(8,128)} fusion(f32[96,8,128,128]{3,2,1,0:T(8,128)} %bitcast.58, s32[768]{0:T(1024)S(1)} %compare_select_fusion.2), kind=kOutput, calls=%fused_computation.2 | convolution fusion | flops 10871691264 | bytes 55053312 | tf_op jit(solution)/shard_map/dot_general | solution.py:89
  279.1 4.8 %collective-permute-start.17 = (f32[1,3,8,128,128]{4,2,3,1,0:T(8,128)S(1)}, f32[1,3,8,128,128]{4,2,3,1,0:T(8,128)S(1)}, u32[]{:S(2)}, u32[]{:S(2)}) collective-permute-start(f32[1,3,8,128,128]{4,2,3,1,0:T(8,128)S(1)} %get-tuple-element.14), channel_id=1, source_target_pairs={{16,0},{32,16},{48,32},{64,48},{80,64},{96,80},{112,96},{17,1},{33... | collective-permute-start | bytes 4718600 | tf_op jit(solution)/shard_map/ppermute | solution.py:20
  286.5 16.5 %collective-permute-done.17 = f32[1,3,8,128,128]{4,2,3,1,0:T(8,128)S(1)} collective-permute-done((f32[1,3,8,128,128]{4,2,3,1,0:T(8,128)S(1)}, f32[1,3,8,128,128]{4,2,3,1,0:T(8,128)S(1)}, u32[]{:S(2)}, u32[]{:S(2)}) %collective-permute-start.17) | collective-permute-done | bytes 1572896 | tf_op jit(solution)/shard_map/ppermute | solution.py:20
  308.5 3.6 collective-permute-start.18
  313.6 51.8 %collective-permute-done.19 = f32[5,1,8,128,128]{4,2,3,1,0:T(8,128)} collective-permute-done((f32[5,1,8,128,128]{4,2,3,1,0:T(8,128)}, f32[5,1,8,128,128]{4,2,3,1,0:T(8,128)}, u32[]{:S(2)}, u32[]{:S(2)}) %collective-permute-start.19) | collective-permute-done | bytes 2621472 | tf_op jit(solution)/shard_map/ppermute | solution.py:20
  365.3 4.0 %collective-permute-done.18 = f32[5,1,8,128,128]{4,2,3,1,0:T(8,128)} collective-permute-done((f32[5,1,8,128,128]{4,2,3,1,0:T(8,128)}, f32[5,1,8,128,128]{4,2,3,1,0:T(8,128)}, u32[]{:S(2)}, u32[]{:S(2)}) %collective-permute-start.18) | collective-permute-done | bytes 2621472 | tf_op jit(solution)/shard_map/ppermute | solution.py:19
  369.4 5.0 %pad_maximum_fusion = f32[5,5,8,128,128]{4,2,3,1,0:T(8,128)S(1)} fusion(f32[5,1,8,128,128]{4,2,3,1,0:T(8,128)} %collective-permute-done.19, f32[1,3,8,128,128]{4,2,3,1,0:T(8,128)S(1)} %collective-permute-done.17, f32[3,3,8,128,128]{4,2,3,1,0:T(8,128)} %bitcast.59, f32[1,3,8,128,128]{4,2,3,1,0:T(8,128)S(1)} %collective-permute-done.16, ...), kind=kLoop, calls=%fused_computation.13 | loop fusion | flops 13107200 | bytes 26214400 | tf_op jit(solution)/shard_map/concatenate | solution.py:21
  377.4 4.4 %copy.31 = f32[64,128,128]{2,1,0:T(8,128)} copy(f32[64,128,128]{2,0,1:T(8,128)S(1)} %fusion.14) | data formatting | bytes 8388608
  (105 shorter events, 51.4 us)
Async XLA Ops:
  7.8 42.9 %copy-start.4 = (s32[4,12,4,4]{1,3,2,0:T(4,128)S(1)}, s32[4,12,4,4]{1,3,2,0:T(4,128)}, u32[]{:S(2)}) copy-start(s32[4,12,4,4]{1,3,2,0:T(4,128)} %param.8) | copy-start | bytes 9220
  8.0 13.7 %collective-permute-start.1 = (bf16[1,3,8,128,128]{4,3,2,1,0:T(8,128)(2,1)S(1)}, bf16[1,3,8,128,128]{4,3,2,1,0:T(8,128)(2,1)S(1)}, u32[]{:S(2)}, u32[]{:S(2)}) collective-permute-start(bf16[1,3,8,128,128]{4,3,2,1,0:T(8,128)(2,1)S(1)} %get-tuple-element.18), channel_id=1, source_target_pairs={{16,0},{32,16},{48,32},{64,48},{80,64},{96,80},{112,96},{17,1},{33... | collective-permute-start | bytes 2359304 | tf_op jit(solution)/shard_map/ppermute | solution.py:20
  10.5 12.0 %collective-permute-start = (bf16[1,3,8,128,128]{4,3,2,1,0:T(8,128)(2,1)S(1)}, bf16[1,3,8,128,128]{4,3,2,1,0:T(8,128)(2,1)S(1)}, u32[]{:S(2)}, u32[]{:S(2)}) collective-permute-start(bf16[1,3,8,128,128]{4,3,2,1,0:T(8,128)(2,1)S(1)} %get-tuple-element.17), channel_id=1, source_target_pairs={{0,16},{16,32},{32,48},{48,64},{64,80},{80,96},{96,112},{1,17},{17... | collective-permute-start | bytes 2359304 | tf_op jit(solution)/shard_map/ppermute | solution.py:19
  25.2 42.5 %collective-permute-start.3 = (bf16[5,1,8,128,128]{4,3,2,1,0:T(8,128)(2,1)}, bf16[5,1,8,128,128]{4,3,2,1,0:T(8,128)(2,1)}, u32[]{:S(2)}, u32[]{:S(2)}) collective-permute-start(bf16[5,1,8,128,128]{4,3,2,1,0:T(8,128)(2,1)} %get-tuple-element.16), channel_id=1, source_target_pairs={{1,0},{2,1},{3,2},{4,3},{5,4},{6,5},{7,6},{8,7},{9,8},{10,9},{11,1... | collective-permute-start | bytes 3932168 | tf_op jit(solution)/shard_map/ppermute | solution.py:20
  30.9 36.9 %collective-permute-start.2 = (bf16[5,1,8,128,128]{4,3,2,1,0:T(8,128)(2,1)}, bf16[5,1,8,128,128]{4,3,2,1,0:T(8,128)(2,1)}, u32[]{:S(2)}, u32[]{:S(2)}) collective-permute-start(bf16[5,1,8,128,128]{4,3,2,1,0:T(8,128)(2,1)} %get-tuple-element.15), channel_id=1, source_target_pairs={{0,1},{1,2},{2,3},{3,4},{4,5},{5,6},{6,7},{7,8},{8,9},{9,10},{10,1... | collective-permute-start | bytes 3932168 | tf_op jit(solution)/shard_map/ppermute | solution.py:19
  32.8 6.6 %collective-permute-start.5 = (f32[1,12,256]{2,1,0:T(8,128)S(1)}, f32[1,12,256]{2,1,0:T(8,128)S(1)}, u32[]{:S(2)}, u32[]{:S(2)}) collective-permute-start(f32[1,12,256]{2,1,0:T(8,128)S(1)} %get-tuple-element.30), channel_id=1, source_target_pairs={{0,16},{16,32},{32,48},{48,64},{64,80},{80,96},{96,112},{1,17},{17... | collective-permute-start | bytes 36872 | tf_op jit(solution)/shard_map/ppermute | solution.py:19
  37.5 5.5 %collective-permute-start.4 = (f32[1,12,256]{2,1,0:T(8,128)S(1)}, f32[1,12,256]{2,1,0:T(8,128)S(1)}, u32[]{:S(2)}, u32[]{:S(2)}) collective-permute-start(f32[1,12,256]{2,1,0:T(8,128)S(1)} %get-tuple-element.29), channel_id=1, source_target_pairs={{16,0},{32,16},{48,32},{64,48},{80,64},{96,80},{112,96},{17,1},{33... | collective-permute-start | bytes 36872 | tf_op jit(solution)/shard_map/ppermute | solution.py:20
  39.5 27.9 %copy-start.6 = (f32[1,12,256]{2,1,0:T(8,128)}, f32[1,12,256]{2,1,0:T(8,128)S(1)}, u32[]{:S(2)}) copy-start(f32[1,12,256]{2,1,0:T(8,128)S(1)} %collective-permute-done.5) | copy-start | bytes 36868
  43.0 24.6 %collective-permute-start.6 = (f32[6,1,256]{2,1,0:T(1,128)S(1)}, f32[6,1,256]{2,1,0:T(1,128)S(1)}, u32[]{:S(2)}, u32[]{:S(2)}) collective-permute-start(f32[6,1,256]{2,1,0:T(1,128)S(1)} %get-tuple-element.24), channel_id=1, source_target_pairs={{1,0},{2,1},{3,2},{4,3},{5,4},{6,5},{7,6},{8,7},{9,8},{10,9},{11,1... | collective-permute-start | bytes 18440 | tf_op jit(solution)/shard_map/ppermute | solution.py:20
  48.8 18.8 %collective-permute-start.7 = (f32[6,1,256]{2,1,0:T(1,128)S(1)}, f32[6,1,256]{2,1,0:T(1,128)S(1)}, u32[]{:S(2)}, u32[]{:S(2)}) collective-permute-start(f32[6,1,256]{2,1,0:T(1,128)S(1)} %get-tuple-element.23), channel_id=1, source_target_pairs={{0,1},{1,2},{2,3},{3,4},{4,5},{5,6},{6,7},{7,8},{8,9},{9,10},{10,1... | collective-permute-start | bytes 18440 | tf_op jit(solution)/shard_map/ppermute | solution.py:19
  90.0 54.0 %copy-start.10 = (f32[4,12,256]{2,0,1:T(4,128)S(1)}, f32[4,12,256]{2,0,1:T(4,128)}, u32[]{:S(2)}) copy-start(f32[4,12,256]{2,0,1:T(4,128)} %param.11) | copy-start | bytes 147460
  108.3 5.6 %collective-permute-start.8 = (f32[1,12,256]{2,1,0:T(8,128)S(1)}, f32[1,12,256]{2,1,0:T(8,128)S(1)}, u32[]{:S(2)}, u32[]{:S(2)}) collective-permute-start(f32[1,12,256]{2,1,0:T(8,128)S(1)} %get-tuple-element.28), channel_id=1, source_target_pairs={{16,0},{32,16},{48,32},{64,48},{80,64},{96,80},{112,96},{17,1},{33... | collective-permute-start | bytes 36872 | tf_op jit(solution)/shard_map/ppermute | solution.py:20
  110.2 4.5 %collective-permute-start.9 = (f32[1,12,256]{2,1,0:T(8,128)S(1)}, f32[1,12,256]{2,1,0:T(8,128)S(1)}, u32[]{:S(2)}, u32[]{:S(2)}) collective-permute-start(f32[1,12,256]{2,1,0:T(8,128)S(1)} %get-tuple-element.27), channel_id=1, source_target_pairs={{0,16},{16,32},{32,48},{48,64},{64,80},{80,96},{96,112},{1,17},{17... | collective-permute-start | bytes 36872 | tf_op jit(solution)/shard_map/ppermute | solution.py:19
  114.7 7.4 %collective-permute-start.10 = (f32[6,1,256]{2,1,0:T(1,128)S(1)}, f32[6,1,256]{2,1,0:T(1,128)S(1)}, u32[]{:S(2)}, u32[]{:S(2)}) collective-permute-start(f32[6,1,256]{2,1,0:T(1,128)S(1)} %get-tuple-element.22), channel_id=1, source_target_pairs={{1,0},{2,1},{3,2},{4,3},{5,4},{6,5},{7,6},{8,7},{9,8},{10,9},{11,1... | collective-permute-start | bytes 18440 | tf_op jit(solution)/shard_map/ppermute | solution.py:20
  120.2 6.5 %collective-permute-start.11 = (f32[6,1,256]{2,1,0:T(1,128)S(1)}, f32[6,1,256]{2,1,0:T(1,128)S(1)}, u32[]{:S(2)}, u32[]{:S(2)}) collective-permute-start(f32[6,1,256]{2,1,0:T(1,128)S(1)} %get-tuple-element.21), channel_id=1, source_target_pairs={{0,1},{1,2},{2,3},{3,4},{4,5},{5,6},{6,7},{7,8},{8,9},{9,10},{10,1... | collective-permute-start | bytes 18440 | tf_op jit(solution)/shard_map/ppermute | solution.py:19
  126.9 7.9 %collective-permute-start.12 = (f32[1,12,256]{2,1,0:T(8,128)S(1)}, f32[1,12,256]{2,1,0:T(8,128)S(1)}, u32[]{:S(2)}, u32[]{:S(2)}) collective-permute-start(f32[1,12,256]{2,1,0:T(8,128)S(1)} %get-tuple-element.26), channel_id=1, source_target_pairs={{16,0},{32,16},{48,32},{64,48},{80,64},{96,80},{112,96},{17,1},{33... | collective-permute-start | bytes 36872 | tf_op jit(solution)/shard_map/ppermute | solution.py:20
  131.9 3.4 collective-permute-start.13
  135.4 5.5 %collective-permute-start.14 = (f32[6,1,256]{2,1,0:T(1,128)S(1)}, f32[6,1,256]{2,1,0:T(1,128)S(1)}, u32[]{:S(2)}, u32[]{:S(2)}) collective-permute-start(f32[6,1,256]{2,1,0:T(1,128)S(1)} %get-tuple-element.20), channel_id=1, source_target_pairs={{1,0},{2,1},{3,2},{4,3},{5,4},{6,5},{7,6},{8,7},{9,8},{10,9},{11,1... | collective-permute-start | bytes 18440 | tf_op jit(solution)/shard_map/ppermute | solution.py:20
  137.3 6.5 %collective-permute-start.15 = (f32[6,1,256]{2,1,0:T(1,128)S(1)}, f32[6,1,256]{2,1,0:T(1,128)S(1)}, u32[]{:S(2)}, u32[]{:S(2)}) collective-permute-start(f32[6,1,256]{2,1,0:T(1,128)S(1)} %get-tuple-element.19), channel_id=1, source_target_pairs={{0,1},{1,2},{2,3},{3,4},{4,5},{5,6},{6,7},{7,8},{8,9},{9,10},{10,1... | collective-permute-start | bytes 18440 | tf_op jit(solution)/shard_map/ppermute | solution.py:19
  276.8 27.0 %copy-start.2 = (f32[72,16384]{1,0:T(8,128)S(1)}, f32[72,16384]{1,0:T(8,128)}, u32[]{:S(2)}) copy-start(f32[72,16384]{1,0:T(8,128)} %fusion) | copy-start | bytes 14155780
  279.1 23.9 %collective-permute-start.17 = (f32[1,3,8,128,128]{4,2,3,1,0:T(8,128)S(1)}, f32[1,3,8,128,128]{4,2,3,1,0:T(8,128)S(1)}, u32[]{:S(2)}, u32[]{:S(2)}) collective-permute-start(f32[1,3,8,128,128]{4,2,3,1,0:T(8,128)S(1)} %get-tuple-element.14), channel_id=1, source_target_pairs={{16,0},{32,16},{48,32},{64,48},{80,64},{96,80},{112,96},{17,1},{33... | collective-permute-start | bytes 4718600 | tf_op jit(solution)/shard_map/ppermute | solution.py:20
  283.9 19.9 %collective-permute-start.16 = (f32[1,3,8,128,128]{4,2,3,1,0:T(8,128)S(1)}, f32[1,3,8,128,128]{4,2,3,1,0:T(8,128)S(1)}, u32[]{:S(2)}, u32[]{:S(2)}) collective-permute-start(f32[1,3,8,128,128]{4,2,3,1,0:T(8,128)S(1)} %get-tuple-element.13), channel_id=1, source_target_pairs={{0,16},{16,32},{32,48},{48,64},{64,80},{80,96},{96,112},{1,17},{17... | collective-permute-start | bytes 4718600 | tf_op jit(solution)/shard_map/ppermute | solution.py:19
  306.6 58.7 %collective-permute-start.19 = (f32[5,1,8,128,128]{4,2,3,1,0:T(8,128)}, f32[5,1,8,128,128]{4,2,3,1,0:T(8,128)}, u32[]{:S(2)}, u32[]{:S(2)}) collective-permute-start(f32[5,1,8,128,128]{4,2,3,1,0:T(8,128)} %get-tuple-element.12), channel_id=1, source_target_pairs={{1,0},{2,1},{3,2},{4,3},{5,4},{6,5},{7,6},{8,7},{9,8},{10,9},{11,1... | collective-permute-start | bytes 7864328 | tf_op jit(solution)/shard_map/ppermute | solution.py:20
  308.5 60.8 %collective-permute-start.18 = (f32[5,1,8,128,128]{4,2,3,1,0:T(8,128)}, f32[5,1,8,128,128]{4,2,3,1,0:T(8,128)}, u32[]{:S(2)}, u32[]{:S(2)}) collective-permute-start(f32[5,1,8,128,128]{4,2,3,1,0:T(8,128)} %get-tuple-element.11), channel_id=1, source_target_pairs={{0,1},{1,2},{2,3},{3,4},{4,5},{5,6},{6,7},{7,8},{8,9},{9,10},{10,1... | collective-permute-start | bytes 7864328 | tf_op jit(solution)/shard_map/ppermute | solution.py:19
  (12 other events, 148.0 us)
where the time goes:
time: 386 us; the launch traced here: 382 us
  matrix products  105 us (27%)
  local copies, waits for them, and re-layouts  97.6 us (25%)
  waiting for transfers between devices  94.3 us (24%)
  starting transfers between devices  66.4 us (17%)
  other arithmetic  17.7 us (5%)
    ppermute x10, waiting for transfers between devices, padded(): after = lax.ppermute(initial, axis, down)  79.7 us
    dot_general x1, matrix products, per_device(): jnp.dot(slot_onehot, flat_integrals, precision=lax.Precision.HIGHEST, pre...  58.2 us
    mul x1, local copies, waits for them, and re-layouts, per_device(): cell_volume * jnp.einsum('nazu,nbzv->nabuv', basis_cols, weighted, prefer...  49 us
    ppermute x10, starting transfers between devices, padded(): after = lax.ppermute(initial, axis, down)  36.9 us
    ppermute x10, starting transfers between devices, padded(): before = lax.ppermute(last, axis, up)  29.5 us
    dot_general x1, matrix products, per_device(): jnp.einsum('nazu,nbzv->nabuv', basis_cols, weighted, preferred_element_ty...  25.6 us
    unnamed x41, local copies, waits for them, and re-layouts  23.6 us
    gather x1, local copies, waits for them, and re-layouts, per_device(): arrived[jnp.clip(pair_slots, 0, slot_count - 1)]  18.7 us
  transfers between devices with their start and end apart: 20, of which 11 were waited for; matrix products, arithmetic and copies ran while one was open for 5% of the time, Pallas kernels for 0%

commit v1 on v0

v1 whole, which is shorter than its diff:
```python
import functools

import jax
import jax.numpy as jnp
from jax import lax
from jax.experimental import pallas as pl
from jax.experimental.pallas import tpu as pltpu
from jax.sharding import PartitionSpec as P

SWEEPS = 3
CELL_VOLUME = 0.0625
VMEM_LIMIT = 56 * 1024 * 1024

KINDS = ((0, 0), (0, 1), (0, 2), (1, 1), (1, 2), (2, 1), (2, 2), (2, 0), (1, 0))


def partner(index, kind):
    if kind == 0:
        return index
    return index + 1 if index % 2 == kind - 1 else index - 1


def swap(value, kind, sizes):
    count_x, count_y = sizes
    pairs = []
    for p in range(count_x):
        for q in range(count_y):
            to_p, to_q = partner(p, kind[0]), partner(q, kind[1])
            if 0 <= to_p < count_x and 0 <= to_q < count_y:
                pairs.append((p * count_y + q, to_p * count_y + to_q))
    return lax.ppermute(value, ("gx", "gy"), pairs)


def group_ids():
    p, q = lax.axis_index("gx"), lax.axis_index("gy")

    def side(index, kind):
        if kind == 0:
            return jnp.int32(1)
        ahead = index % 2 == kind - 1
        return jnp.where(ahead, 2, 0).astype(jnp.int32)

    return jnp.stack([side(p, a) * 3 + side(q, b) for a, b in KINDS])


def call(body, name, **options):
    return pl.pallas_call(
        body,
        name=name,
        compiler_params=pltpu.CompilerParams(vmem_limit_bytes=VMEM_LIMIT),
        **options,
    )


SMEM = pl.BlockSpec(memory_space=pltpu.SMEM)
VMEM = pl.BlockSpec(memory_space=pltpu.VMEM)
ANY = pl.BlockSpec(memory_space=pl.ANY)


def gather_body(groups, table, blocks, *rest):
    outs, sems = rest[:-1], rest[-1]
    depth = table.shape[2]
    for t, out in enumerate(outs):
        k, l = groups[t] // 3, groups[t] % 3
        for c in range(depth):
            row = jnp.maximum(table[k, l, c], 0)
            pltpu.make_async_copy(blocks.at[row], out.at[c], sems.at[t]).start()
    for t, out in enumerate(outs):
        pltpu.make_async_copy(blocks.at[pl.ds(0, depth)], out, sems.at[t]).wait()


def gather(groups, table, blocks):
    depth, width = table.shape[2], blocks.shape[1]
    kinds = len(KINDS)
    return call(
        gather_body,
        "gather",
        in_specs=[SMEM, SMEM, ANY],
        out_specs=[ANY] * kinds,
        out_shape=[jax.ShapeDtypeStruct((depth, width, width), blocks.dtype)] * kinds,
        scratch_shapes=[pltpu.SemaphoreType.DMA((kinds,))],
    )(groups, table, blocks)


def transpose_body(chunk, source, out, held, turned, sems_in, sems_out):
    count, blocks, _, width = source.shape
    steps = count // chunk

    def part(c):
        return pl.ds(c * chunk, chunk)

    def coming(c):
        return pltpu.make_async_copy(source.at[part(c)], held.at[part(c)], sems_in.at[c])

    def going(c):
        return pltpu.make_async_copy(turned.at[part(c)], out.at[part(c)], sems_out.at[c])

    for c in range(steps):
        coming(c).start()
    for c in range(steps):
        coming(c).wait()
        for n in range(c * chunk, (c + 1) * chunk):
            for b in range(blocks):
                turned[n, b * width : (b + 1) * width, :] = held[n, b].T
        going(c).start()
    for c in range(steps):
        going(c).wait()


def transposed(basis, chunk=4):
    count, blocks, points, width = basis.shape
    shape = (count, blocks * width, points)
    return call(
        functools.partial(transpose_body, chunk),
        "transpose",
        in_specs=[ANY],
        out_specs=ANY,
        out_shape=jax.ShapeDtypeStruct(shape, basis.dtype),
        scratch_shapes=[
            pltpu.VMEM(basis.shape, basis.dtype),
            pltpu.VMEM(shape, basis.dtype),
            pltpu.SemaphoreType.DMA((count // chunk,)),
            pltpu.SemaphoreType.DMA((count // chunk,)),
        ],
        cost_estimate=pl.CostEstimate(flops=0, bytes_accessed=4 * basis.size, transcendentals=0),
    )(basis)


def density_body(chunk, ahead, groups, slots, basis, *rest):
    kinds = len(KINDS)
    messages, (out, held, blocks, sems, block_sems) = rest[:kinds], rest[kinds:]
    count, rows, _ = basis.shape
    depth, width, _ = messages[0].shape
    per = rows // width
    steps = count // chunk

    def coming(c):
        part = pl.ds(c * chunk, chunk)
        return pltpu.make_async_copy(basis.at[part], held.at[part], sems.at[c])

    arrivals = [
        pltpu.make_async_copy(message, blocks.at[pl.ds(groups[t] * depth, depth)], block_sems.at[t])
        for t, message in enumerate(messages)
    ]
    for copy in arrivals:
        copy.start()
    for c in range(ahead):
        coming(c).start()
    blocks[kinds * depth] = jnp.zeros((width, width), blocks.dtype)
    for copy in arrivals:
        copy.wait()

    def one(n):
        rows_of = [
            jnp.concatenate([blocks[slots[n * per * per + a * per + b]] for b in range(per)], axis=1)
            for a in range(per)
        ]
        mixed = jnp.dot(
            jnp.concatenate(rows_of, axis=0), held[n], preferred_element_type=jnp.float32
        )
        product = mixed * held[n].astype(jnp.float32)
        out[pl.ds(n, 1), :] = jnp.sum(product, axis=0, keepdims=True)

    def step(c, carry):
        @pl.when(c + ahead < steps)
        def _():
            coming(c + ahead).start()

        coming(c).wait()
        for u in range(chunk):
            one(c * chunk + u)
        return carry

    lax.fori_loop(0, steps, step, 0)


def density_of(groups, slots, basis, messages, chunk=8, ahead=2):
    count, rows, points = basis.shape
    depth, width, _ = messages[0].shape
    kinds = len(KINDS)
    return call(
        functools.partial(density_body, chunk, ahead),
        "density",
        in_specs=[SMEM, SMEM] + [ANY] * (1 + kinds),
        out_specs=VMEM,
        out_shape=jax.ShapeDtypeStruct((count, points), jnp.float32),
        scratch_shapes=[
            pltpu.VMEM(basis.shape, basis.dtype),
            pltpu.VMEM((kinds * depth + 1, width, width), basis.dtype),
            pltpu.SemaphoreType.DMA((count // chunk,)),
            pltpu.SemaphoreType.DMA((kinds,)),
        ],
    )(groups, slots, basis, *messages)


def stencil(field, charge):
    z_padded = jnp.pad(field, ((0, 0), (0, 0), (1, 1)))
    beside = z_padded[2:, 1:-1, 1:-1] + z_padded[:-2, 1:-1, 1:-1]
    beside = beside + z_padded[1:-1, 2:, 1:-1] + z_padded[1:-1, :-2, 1:-1]
    beside = beside + z_padded[1:-1, 1:-1, 2:] + z_padded[1:-1, 1:-1, :-2]
    return (beside + charge) / 6.0


def halo(field, charge, dim, axis, sizes):
    length = field.shape[dim]
    wide, thin = SWEEPS, SWEEPS - 1
    even = lax.axis_index(axis) % 2 == 0
    field_shape = list(field.shape)
    charge_shape = list(charge.shape)
    field_shape[dim], charge_shape[dim] = wide, thin
    points = field.shape[-1]

    def pack(field_start, charge_start):
        a = lax.slice_in_dim(field, field_start, field_start + wide, axis=dim)
        b = lax.slice_in_dim(charge, charge_start, charge_start + thin, axis=dim)
        return jnp.concatenate([a.reshape(-1, points), b.reshape(-1, points)], axis=0)

    low, high = pack(0, 0), pack(length - wide, length - thin)
    kinds = ((1, 0), (2, 0)) if axis == "gx" else ((0, 1), (0, 2))
    first = swap(jnp.where(even, high, low), kinds[0], sizes)
    second = swap(jnp.where(even, low, high), kinds[1], sizes)
    before, after = jnp.where(even, second, first), jnp.where(even, first, second)

    def unpack(rows):
        cut = 1
        for size in field_shape[:-1]:
            cut *= size
        return rows[:cut].reshape(field_shape), rows[cut:].reshape(charge_shape)

    (field_before, charge_before), (field_after, charge_after) = unpack(before), unpack(after)
    return (
        jnp.concatenate([field_before, field, field_after], axis=dim),
        jnp.concatenate([charge_before, charge, charge_after], axis=dim),
    )


def inside(width, brick_x, brick_y, sizes):
    p, q = lax.axis_index("gx"), lax.axis_index("gy")
    x = lax.broadcasted_iota(jnp.int32, (brick_x + 2 * width, brick_y + 2 * width, 1), 0)
    y = lax.broadcasted_iota(jnp.int32, (brick_x + 2 * width, brick_y + 2 * width, 1), 1)
    x, y = x - width + p * brick_x, y - width + q * brick_y
    return (x >= 0) & (x < sizes[0] * brick_x) & (y >= 0) & (y < sizes[1] * brick_y)


def sweeps(previous, density, sizes):
    brick_x, brick_y, _ = density.shape
    field, charge = halo(previous, density, 0, "gx", sizes)
    field, charge = halo(field, charge, 1, "gy", sizes)
    for done in range(1, SWEEPS + 1):
        width = SWEEPS - done
        field = stencil(field, charge)
        if width:
            field = jnp.where(inside(width, brick_x, brick_y, sizes), field, 0.0)
            charge = charge[1:-1, 1:-1]
    return field


def integrals_body(chunk, ahead, groups, slots, basis, potential, *rest):
    kinds = len(KINDS)
    outs, (held, sums, sems) = rest[:kinds], rest[kinds:]
    count, rows, _ = basis.shape
    depth, width, _ = outs[0].shape
    per = rows // width
    steps = count // chunk

    def coming(c):
        part = pl.ds(c * chunk, chunk)
        return pltpu.make_async_copy(basis.at[part], held.at[part], sems.at[c])

    for c in range(ahead):
        coming(c).start()
    sums[...] = jnp.zeros_like(sums)

    def one(n):
        wide = held[n].astype(jnp.float32)
        weighted = (wide * potential[pl.ds(n, 1), :]).astype(basis.dtype)
        product = lax.dot_general(
            held[n], weighted, (((1,), (1,)), ((), ())), preferred_element_type=jnp.float32
        )
        for a in range(per):
            for b in range(per):
                slot = slots[n * per * per + a * per + b]
                sums[slot] += product[a * width : (a + 1) * width, b * width : (b + 1) * width]

    def step(c, carry):
        @pl.when(c + ahead < steps)
        def _():
            coming(c + ahead).start()

        coming(c).wait()
        for u in range(chunk):
            one(c * chunk + u)
        return carry

    lax.fori_loop(0, steps, step, 0)
    for t, out in enumerate(outs):
        part = sums[pl.ds(groups[t] * depth, depth)]
        out[...] = (CELL_VOLUME * part).astype(out.dtype)


def integrals_of(groups, slots, basis, potential, depth, width, chunk=8, ahead=2):
    count, rows, _ = basis.shape
    kinds = len(KINDS)
    shape = (depth, width, width)
    return call(
        functools.partial(integrals_body, chunk, ahead),
        "integrals",
        in_specs=[SMEM, SMEM, ANY, VMEM],
        out_specs=[VMEM] * kinds,
        out_shape=[jax.ShapeDtypeStruct(shape, jnp.float32)]
        + [jax.ShapeDtypeStruct(shape, jnp.bfloat16)] * (kinds - 1),
        scratch_shapes=[
            pltpu.VMEM(basis.shape, basis.dtype),
            pltpu.VMEM((kinds * depth + 1, width, width), jnp.float32),
            pltpu.SemaphoreType.DMA((count // chunk,)),
        ],
    )(groups, slots, basis, potential)


def collect_body(groups, table, *rest):
    messages, out = rest[:-1], rest[-1]
    depth = table.shape[2]
    out[...] = jnp.zeros_like(out)
    for t, message in enumerate(messages):
        k, l = groups[t] // 3, groups[t] % 3
        for c in range(depth):
            row = table[k, l, c]

            @pl.when(row >= 0)
            def _():
                out[row] += message[c].astype(jnp.float32)


def collect(groups, table, messages, owned):
    width = messages[0].shape[1]
    return call(
        collect_body,
        "collect",
        in_specs=[SMEM, SMEM] + [VMEM] * len(messages),
        out_specs=VMEM,
        out_shape=jax.ShapeDtypeStruct((owned, width, width), jnp.float32),
    )(groups, table, *messages)


def per_device(
    sizes, density_blocks, send_table, batch_pairs, basis_values, previous_hartree, external_potential
):
    owned, width, _ = density_blocks.shape
    table = send_table[0]
    depth = table.shape[2]
    brick_x, brick_y, per, points, _ = basis_values.shape
    count = brick_x * brick_y
    groups = group_ids()
    outgoing = gather(groups, table, density_blocks)
    arrived = [outgoing[0]] + [swap(m, kind, sizes) for m, kind in zip(outgoing[1:], KINDS[1:])]
    slots = jnp.where(batch_pairs >= 0, batch_pairs, len(KINDS) * depth).reshape(-1)
    basis = transposed(basis_values.reshape(count, per, points, width))
    density = density_of(groups, slots, basis, arrived).reshape(brick_x, brick_y, points)
    hartree = sweeps(previous_hartree, density, sizes)
    field = (hartree + external_potential).reshape(count, points)
    partial = integrals_of(groups, slots, basis, field, depth, width)
    returned = [partial[0]] + [swap(m, kind, sizes) for m, kind in zip(partial[1:], KINDS[1:])]
    return density, hartree, collect(groups, table, returned, owned)


def solution(mesh):
    sizes = (mesh.shape["gx"], mesh.shape["gy"])
    in_specs = (
        P(("gx", "gy"), None, None),
        P(("gx", "gy"), None, None, None),
        P("gx", "gy", None, None),
        P("gx", "gy", None, None, None),
        P("gx", "gy", None),
        P("gx", "gy", None),
    )
    out_specs = (P("gx", "gy", None), P("gx", "gy", None), P(("gx", "gy"), None, None))
    return jax.shard_map(
        functools.partial(per_device, sizes),
        mesh=mesh,
        in_specs=in_specs,
        out_specs=out_specs,
        check_vma=False,
    )
```

time: 386 us -> 184 us (0.48)
  Pallas kernels: 0 us -> 113 us
  matrix products: 105 us -> 0 us
  local copies, waits for them, and re-layouts: 97.6 us -> 9.35 us
  waiting for transfers between devices: 94.3 us -> 10.5 us
  starting transfers between devices: 66.4 us -> 47.7 us
  other arithmetic: 17.7 us -> 1.46 us
    pallas_call x0 -> x5, Pallas kernels: none -> 113 us  [the longest x1 73.4 us: gather(): call(gather_body, 'gather', in_specs=[SMEM, SMEM, ANY], out_specs=[ANY] *...]
    dot_general x4 -> x0, matrix products: 105 us -> none  [the longest x1 58.2 us: per_device(): jnp.dot(slot_onehot, flat_integrals, precision=lax.Precision.HIGHEST, pre...]
    ppermute x20, waiting for transfers between devices: 94.3 us -> 10.5 us  [swap(): return lax.ppermute(value, ('gx', 'gy'), pairs)]
    mul x2 -> x0, local copies, waits for them, and re-layouts: 49 us -> none  [the longest x1 49 us: per_device(): cell_volume * jnp.einsum('nazu,nbzv->nabuv', basis_cols, weighted, prefer...]
    gather x2 -> x0, local copies, waits for them, and re-layouts: 21.2 us -> none  [the longest x1 18.7 us: per_device(): arrived[jnp.clip(pair_slots, 0, slot_count - 1)]]
    unnamed x41 -> x43, local copies, waits for them, and re-layouts: 23.6 us -> 4.39 us
    ppermute x20, starting transfers between devices: 66.4 us -> 47.7 us  [swap(): return lax.ppermute(value, ('gx', 'gy'), pairs)]
    concatenate x7 -> x1, other arithmetic: 8.58 us -> 0.05 us  [halo(): jnp.concatenate([field_before, field, field_after], axis=dim)]
  transfers between devices with their start and end apart: 20 -> 20, of which waited for: 11 -> 4; matrix products, arithmetic and copies ran while one was open for 5% -> 3% of each run, Pallas kernels for 0% -> 5%
where the time goes in v1:
time: 184 us; the launch traced here: 183 us
  Pallas kernels  113 us (61%)
  starting transfers between devices  47.7 us (26%)
  waiting for transfers between devices  10.5 us (6%)
  local copies, waits for them, and re-layouts  9.35 us (5%)
    pallas_call x1, Pallas kernels, gather(): call(gather_body, 'gather', in_specs=[SMEM, SMEM, ANY], out_specs=[ANY] *...  73.4 us
    ppermute x20, starting transfers between devices, swap(): return lax.ppermute(value, ('gx', 'gy'), pairs)  47.7 us
    pallas_call x1, Pallas kernels, integrals_of(): call(functools.partial(integrals_body, chunk, ahead), 'integrals', in_spe...  12.9 us
    pallas_call x1, Pallas kernels, density_of(): call(functools.partial(density_body, chunk, ahead), 'density', in_specs=[...  11.9 us
    ppermute x20, waiting for transfers between devices, swap(): return lax.ppermute(value, ('gx', 'gy'), pairs)  10.5 us
    pallas_call x1, Pallas kernels, transposed(): call(functools.partial(transpose_body, chunk), 'transpose', in_specs=[ANY...  9.52 us
    pallas_call x1, Pallas kernels, collect(): call(collect_body, 'collect', in_specs=[SMEM, SMEM] + [VMEM] * len(messag...  4.94 us
    unnamed x43, local copies, waits for them, and re-layouts  4.39 us
  transfers between devices with their start and end apart: 20, of which 4 were waited for; matrix products, arithmetic and copies ran while one was open for 3% of the time, Pallas kernels for 5%

profile of v1, /device:TPU:13, one launch (start us, length us, event | category | flops | bytes accessed | tf_op | source)
XLA Modules:
  0.0 183.1 jit_solution(10116099584485689079)
XLA Ops:
  0.7 1.3 copy.24
  2.6 73.4 %gather.1 = (bf16[8,128,128]{2,1,0:T(8,128)(2,1)}, bf16[8,128,128]{2,1,0:T(8,128)(2,1)}, bf16[8,128,128]{2,1,0:T(8,128)(2,1)}, bf16[8,128,128]{2,1,0:T(8,128)(2,...) custom-call(s32[9]{0:T(128)} %stack.35.groups, ...), custom_call_target="tpu_custom_call" | custom-call | tf_op jit(solution)/shard_map/gather/pallas_call | solution.py:75
  76.1 1.7 collective-permute-start
  77.8 4.1 %collective-permute-start.1 = (bf16[8,128,128]{2,1,0:T(8,128)(2,1)}, bf16[8,128,128]{2,1,0:T(8,128)(2,1)S(1)}, u32[]{:S(2)}, u32[]{:S(2)}) collective-permute-start(bf16[8,128,128]{2,1,0:T(8,128)(2,1)} %get-tuple-element.23), channel_id=1, source_target_pairs={{1,2},{2,1},{3,4},{4,3},{5,6},{6,5},{7,8},{8,7},{9,10},{10,9},{11,... | collective-permute-start | bytes 786440 | tf_op jit(solution)/shard_map/ppermute | solution.py:31
  81.9 2.0 %collective-permute-start.2 = (bf16[8,128,128]{2,1,0:T(8,128)(2,1)}, bf16[8,128,128]{2,1,0:T(8,128)(2,1)S(1)}, u32[]{:S(2)}, u32[]{:S(2)}) collective-permute-start(bf16[8,128,128]{2,1,0:T(8,128)(2,1)} %get-tuple-element.24), channel_id=1, source_target_pairs={{0,17},{1,16},{2,19},{3,18},{4,21},{5,20},{6,23},{7,22},{8,25},{9,... | collective-permute-start | bytes 786440 | tf_op jit(solution)/shard_map/ppermute | solution.py:31
  83.9 2.5 %collective-permute-start.3 = (bf16[8,128,128]{2,1,0:T(8,128)(2,1)}, bf16[8,128,128]{2,1,0:T(8,128)(2,1)S(1)}, u32[]{:S(2)}, u32[]{:S(2)}) collective-permute-start(bf16[8,128,128]{2,1,0:T(8,128)(2,1)} %get-tuple-element.25), channel_id=1, source_target_pairs={{1,18},{2,17},{3,20},{4,19},{5,22},{6,21},{7,24},{8,23},{9,26},{10... | collective-permute-start | bytes 786440 | tf_op jit(solution)/shard_map/ppermute | solution.py:31
  86.4 3.8 %collective-permute-start.4 = (bf16[8,128,128]{2,1,0:T(8,128)(2,1)}, bf16[8,128,128]{2,1,0:T(8,128)(2,1)S(1)}, u32[]{:S(2)}, u32[]{:S(2)}) collective-permute-start(bf16[8,128,128]{2,1,0:T(8,128)(2,1)} %get-tuple-element.26), channel_id=1, source_target_pairs={{16,33},{17,32},{18,35},{19,34},{20,37},{21,36},{22,39},{23,38},{2... | collective-permute-start | bytes 786440 | tf_op jit(solution)/shard_map/ppermute | solution.py:31
  91.9 4.3 %collective-permute-start.5 = (bf16[8,128,128]{2,1,0:T(8,128)(2,1)}, bf16[8,128,128]{2,1,0:T(8,128)(2,1)S(1)}, u32[]{:S(2)}, u32[]{:S(2)}) collective-permute-start(bf16[8,128,128]{2,1,0:T(8,128)(2,1)} %get-tuple-element.27), channel_id=1, source_target_pairs={{17,34},{18,33},{19,36},{20,35},{21,38},{22,37},{23,40},{24,39},{2... | collective-permute-start | bytes 786440 | tf_op jit(solution)/shard_map/ppermute | solution.py:31
  96.2 2.5 %collective-permute-start.6 = (bf16[8,128,128]{2,1,0:T(8,128)(2,1)}, bf16[8,128,128]{2,1,0:T(8,128)(2,1)S(1)}, u32[]{:S(2)}, u32[]{:S(2)}) collective-permute-start(bf16[8,128,128]{2,1,0:T(8,128)(2,1)} %get-tuple-element.28), channel_id=1, source_target_pairs={{16,32},{17,33},{18,34},{19,35},{20,36},{21,37},{22,38},{23,39},{2... | collective-permute-start | bytes 786440 | tf_op jit(solution)/shard_map/ppermute | solution.py:31
  99.8 9.5 %transpose.5.basis = bf16[48,512,256]{2,1,0:T(8,128)(2,1)} custom-call(bf16[48,4,256,128]{3,2,1,0:T(8,128)(2,1)} %bitcast.12), custom_call_target="tpu_custom_call" | custom-call | bytes 25165824 | tf_op jit(solution)/shard_map/transpose/pallas_call | solution.py:113
  110.6 11.9 %density.1 = f32[48,256]{1,0:T(8,128)} custom-call(s32[9]{0:T(128)} %stack.35.groups, s32[768]{0:T(1024)} %reshape.142.slots, bf16[48,512,256]{2,1,0:T(8,128)(2,1)} %transpose.5.basis, bf16[8,128,128]{2,1,0:T(8,128)(2,1)} %get-tuple-element.21.rest_0_, bf16[8,128,128]{2,1,0:T(8,128)(2,1)} %copy-done.1, bf16[8,128,128]{2,1,0:T(8,128)(2,1)} %copy-done.2, ...), custom_call_target="tpu_custom_call" | custom-call | tf_op jit(solution)/shard_map/density/pallas_call | solution.py:181
  123.9 3.0 %collective-permute-start.8 = (f32[60,256]{1,0:T(8,128)S(1)}, f32[60,256]{1,0:T(8,128)S(1)}, u32[]{:S(2)}, u32[]{:S(2)}) collective-permute-start(f32[60,256]{1,0:T(8,128)S(1)} %get-tuple-element.56), channel_id=1, source_target_pairs={{16,32},{17,33},{18,34},{19,35},{20,36},{21,37},{22,38},{23,39},{2... | collective-permute-start | bytes 184328 | tf_op jit(solution)/shard_map/ppermute | solution.py:31
  127.7 1.7 collective-permute-done.8
  129.8 3.9 %collective-permute-start.10 = (f32[46,256]{1,0:T(8,128)S(1)}, f32[46,256]{1,0:T(8,128)S(1)}, u32[]{:S(2)}, u32[]{:S(2)}) collective-permute-start(f32[46,256]{1,0:T(8,128)S(1)} %get-tuple-element.59), channel_id=1, source_target_pairs={{1,2},{2,1},{3,4},{4,3},{5,6},{6,5},{7,8},{8,7},{9,10},{10,9},{11,... | collective-permute-start | bytes 141320 | tf_op jit(solution)/shard_map/ppermute | solution.py:31
  133.9 3.2 %collective-permute-done.10 = f32[46,256]{1,0:T(8,128)S(1)} collective-permute-done((f32[46,256]{1,0:T(8,128)S(1)}, f32[46,256]{1,0:T(8,128)S(1)}, u32[]{:S(2)}, u32[]{:S(2)}) %collective-permute-start.10) | collective-permute-done | bytes 47136 | tf_op jit(solution)/shard_map/ppermute | solution.py:31
  138.5 12.9 %integrals.1 = (f32[8,128,128]{2,1,0:T(8,128)}, bf16[8,128,128]{2,1,0:T(8,128)(2,1)}, bf16[8,128,128]{2,1,0:T(8,128)(2,1)}, bf16[8,128,128]{2,1,0:T(8,128)(2,1)}...) custom-call(s32[9]{0:T(128)} %stack.35.groups, ...), custom_call_target="tpu_custom_call" | custom-call | tf_op jit(solution)/shard_map/integrals/pallas_call | solution.py:305
  151.4 3.9 %collective-permute-start.13 = (bf16[8,128,128]{2,1,0:T(8,128)(2,1)}, bf16[8,128,128]{2,1,0:T(8,128)(2,1)S(1)}, u32[]{:S(2)}, u32[]{:S(2)}) collective-permute-start(bf16[8,128,128]{2,1,0:T(8,128)(2,1)} %get-tuple-element.32), channel_id=1, source_target_pairs={{1,2},{2,1},{3,4},{4,3},{5,6},{6,5},{7,8},{8,7},{9,10},{10,9},{11,... | collective-permute-start | bytes 786440 | tf_op jit(solution)/shard_map/ppermute | solution.py:31
  155.3 2.0 %collective-permute-start.14 = (bf16[8,128,128]{2,1,0:T(8,128)(2,1)}, bf16[8,128,128]{2,1,0:T(8,128)(2,1)S(1)}, u32[]{:S(2)}, u32[]{:S(2)}) collective-permute-start(bf16[8,128,128]{2,1,0:T(8,128)(2,1)} %get-tuple-element.33), channel_id=1, source_target_pairs={{0,17},{1,16},{2,19},{3,18},{4,21},{5,20},{6,23},{7,22},{8,25},{9,... | collective-permute-start | bytes 786440 | tf_op jit(solution)/shard_map/ppermute | solution.py:31
  157.3 2.9 %collective-permute-start.15 = (bf16[8,128,128]{2,1,0:T(8,128)(2,1)}, bf16[8,128,128]{2,1,0:T(8,128)(2,1)S(1)}, u32[]{:S(2)}, u32[]{:S(2)}) collective-permute-start(bf16[8,128,128]{2,1,0:T(8,128)(2,1)} %get-tuple-element.34), channel_id=1, source_target_pairs={{1,18},{2,17},{3,20},{4,19},{5,22},{6,21},{7,24},{8,23},{9,26},{10... | collective-permute-start | bytes 786440 | tf_op jit(solution)/shard_map/ppermute | solution.py:31
  160.1 3.5 %collective-permute-start.16 = (bf16[8,128,128]{2,1,0:T(8,128)(2,1)}, bf16[8,128,128]{2,1,0:T(8,128)(2,1)S(1)}, u32[]{:S(2)}, u32[]{:S(2)}) collective-permute-start(bf16[8,128,128]{2,1,0:T(8,128)(2,1)} %get-tuple-element.35), channel_id=1, source_target_pairs={{16,33},{17,32},{18,35},{19,34},{20,37},{21,36},{22,39},{23,38},{2... | collective-permute-start | bytes 786440 | tf_op jit(solution)/shard_map/ppermute | solution.py:31
  163.6 4.0 %collective-permute-start.17 = (bf16[8,128,128]{2,1,0:T(8,128)(2,1)}, bf16[8,128,128]{2,1,0:T(8,128)(2,1)S(1)}, u32[]{:S(2)}, u32[]{:S(2)}) collective-permute-start(bf16[8,128,128]{2,1,0:T(8,128)(2,1)} %get-tuple-element.36), channel_id=1, source_target_pairs={{17,34},{18,33},{19,36},{20,35},{21,38},{22,37},{23,40},{24,39},{2... | collective-permute-start | bytes 786440 | tf_op jit(solution)/shard_map/ppermute | solution.py:31
  167.6 2.7 %collective-permute-start.18 = (bf16[8,128,128]{2,1,0:T(8,128)(2,1)}, bf16[8,128,128]{2,1,0:T(8,128)(2,1)S(1)}, u32[]{:S(2)}, u32[]{:S(2)}) collective-permute-start(bf16[8,128,128]{2,1,0:T(8,128)(2,1)} %get-tuple-element.37), channel_id=1, source_target_pairs={{16,32},{17,33},{18,34},{19,35},{20,36},{21,37},{22,38},{23,39},{2... | collective-permute-start | bytes 786440 | tf_op jit(solution)/shard_map/ppermute | solution.py:31
  171.8 4.4 %collective-permute-done.17.rest_6_ = bf16[8,128,128]{2,1,0:T(8,128)(2,1)S(1)} collective-permute-done((bf16[8,128,128]{2,1,0:T(8,128)(2,1)}, bf16[8,128,128]{2,1,0:T(8,128)(2,1)S(1)}, u32[]{:S(2)}, u32[]{:S(2)}) %collective-permute-start.17) | collective-permute-done | bytes 262176 | tf_op jit(solution)/shard_map/ppermute | solution.py:31
  178.1 4.9 %collect.1 = f32[64,128,128]{2,1,0:T(8,128)} custom-call(s32[9]{0:T(128)} %stack.35.groups, s32[3,3,8]{2,1,0:T(4,128)} %bitcast.14, f32[8,128,128]{2,1,0:T(8,128)} %get-tuple-element.30.rest_0_, bf16[8,128,128]{2,1,0:T(8,128)(2,1)} %copy-done.9, bf16[8,128,128]{2,1,0:T(8,128)(2,1)} %copy-done.10, bf16[8,128,128]{2,1,0:T(8,128)(2,1)} %copy-done.11, ...), custom_call_target="tpu_custom_call" | custom-call | tf_op jit(solution)/shard_map/collect/pallas_call | solution.py:336
  (114 shorter events, 11.7 us)
Async XLA Ops:
  76.1 15.8 %collective-permute-start = (bf16[8,128,128]{2,1,0:T(8,128)(2,1)}, bf16[8,128,128]{2,1,0:T(8,128)(2,1)S(1)}, u32[]{:S(2)}, u32[]{:S(2)}) collective-permute-start(bf16[8,128,128]{2,1,0:T(8,128)(2,1)} %get-tuple-element.22), channel_id=1, source_target_pairs={{0,1},{1,0},{2,3},{3,2},{4,5},{5,4},{6,7},{7,6},{8,9},{9,8},{10,11... | collective-permute-start | bytes 786440 | tf_op jit(solution)/shard_map/ppermute | solution.py:31
  77.8 18.4 %collective-permute-start.1 = (bf16[8,128,128]{2,1,0:T(8,128)(2,1)}, bf16[8,128,128]{2,1,0:T(8,128)(2,1)S(1)}, u32[]{:S(2)}, u32[]{:S(2)}) collective-permute-start(bf16[8,128,128]{2,1,0:T(8,128)(2,1)} %get-tuple-element.23), channel_id=1, source_target_pairs={{1,2},{2,1},{3,4},{4,3},{5,6},{6,5},{7,8},{8,7},{9,10},{10,9},{11,... | collective-permute-start | bytes 786440 | tf_op jit(solution)/shard_map/ppermute | solution.py:31
  81.9 16.9 %collective-permute-start.2 = (bf16[8,128,128]{2,1,0:T(8,128)(2,1)}, bf16[8,128,128]{2,1,0:T(8,128)(2,1)S(1)}, u32[]{:S(2)}, u32[]{:S(2)}) collective-permute-start(bf16[8,128,128]{2,1,0:T(8,128)(2,1)} %get-tuple-element.24), channel_id=1, source_target_pairs={{0,17},{1,16},{2,19},{3,18},{4,21},{5,20},{6,23},{7,22},{8,25},{9,... | collective-permute-start | bytes 786440 | tf_op jit(solution)/shard_map/ppermute | solution.py:31
  83.9 25.7 %collective-permute-start.3 = (bf16[8,128,128]{2,1,0:T(8,128)(2,1)}, bf16[8,128,128]{2,1,0:T(8,128)(2,1)S(1)}, u32[]{:S(2)}, u32[]{:S(2)}) collective-permute-start(bf16[8,128,128]{2,1,0:T(8,128)(2,1)} %get-tuple-element.25), channel_id=1, source_target_pairs={{1,18},{2,17},{3,20},{4,19},{5,22},{6,21},{7,24},{8,23},{9,26},{10... | collective-permute-start | bytes 786440 | tf_op jit(solution)/shard_map/ppermute | solution.py:31
  86.4 23.2 %collective-permute-start.4 = (bf16[8,128,128]{2,1,0:T(8,128)(2,1)}, bf16[8,128,128]{2,1,0:T(8,128)(2,1)S(1)}, u32[]{:S(2)}, u32[]{:S(2)}) collective-permute-start(bf16[8,128,128]{2,1,0:T(8,128)(2,1)} %get-tuple-element.26), channel_id=1, source_target_pairs={{16,33},{17,32},{18,35},{19,34},{20,37},{21,36},{22,39},{23,38},{2... | collective-permute-start | bytes 786440 | tf_op jit(solution)/shard_map/ppermute | solution.py:31
  91.9 17.5 %copy-start.1 = (bf16[8,128,128]{2,1,0:T(8,128)(2,1)}, bf16[8,128,128]{2,1,0:T(8,128)(2,1)S(1)}, u32[]{:S(2)}) copy-start(bf16[8,128,128]{2,1,0:T(8,128)(2,1)S(1)} %collective-permute-done.rest_1_) | copy-start | bytes 786436
  91.9 17.7 %collective-permute-start.5 = (bf16[8,128,128]{2,1,0:T(8,128)(2,1)}, bf16[8,128,128]{2,1,0:T(8,128)(2,1)S(1)}, u32[]{:S(2)}, u32[]{:S(2)}) collective-permute-start(bf16[8,128,128]{2,1,0:T(8,128)(2,1)} %get-tuple-element.27), channel_id=1, source_target_pairs={{17,34},{18,33},{19,36},{20,35},{21,38},{22,37},{23,40},{24,39},{2... | collective-permute-start | bytes 786440 | tf_op jit(solution)/shard_map/ppermute | solution.py:31
  96.2 13.4 %collective-permute-start.6 = (bf16[8,128,128]{2,1,0:T(8,128)(2,1)}, bf16[8,128,128]{2,1,0:T(8,128)(2,1)S(1)}, u32[]{:S(2)}, u32[]{:S(2)}) collective-permute-start(bf16[8,128,128]{2,1,0:T(8,128)(2,1)} %get-tuple-element.28), channel_id=1, source_target_pairs={{16,32},{17,33},{18,34},{19,35},{20,36},{21,37},{22,38},{23,39},{2... | collective-permute-start | bytes 786440 | tf_op jit(solution)/shard_map/ppermute | solution.py:31
  98.8 10.8 %collective-permute-start.7 = (bf16[8,128,128]{2,1,0:T(8,128)(2,1)}, bf16[8,128,128]{2,1,0:T(8,128)(2,1)S(1)}, u32[]{:S(2)}, u32[]{:S(2)}) collective-permute-start(bf16[8,128,128]{2,1,0:T(8,128)(2,1)} %get-tuple-element.29), channel_id=1, source_target_pairs={{0,16},{1,17},{2,18},{3,19},{4,20},{5,21},{6,22},{7,23},{8,24},{9,... | collective-permute-start | bytes 786440 | tf_op jit(solution)/shard_map/ppermute | solution.py:31
  109.4 20.3 %copy-start = (f32[4,12,256]{2,0,1:T(4,128)S(1)}, f32[4,12,256]{2,0,1:T(4,128)}, u32[]{:S(2)}) copy-start(f32[4,12,256]{2,0,1:T(4,128)} %param.10) | copy-start | bytes 147460
  109.4 28.3 %copy-start.17 = (f32[4,12,256]{2,0,1:T(4,128)S(1)}, f32[4,12,256]{2,0,1:T(4,128)}, u32[]{:S(2)}) copy-start(f32[4,12,256]{2,0,1:T(4,128)} %param.11) | copy-start | bytes 147460
  123.3 4.4 %collective-permute-start.9 = (f32[60,256]{1,0:T(8,128)S(1)}, f32[60,256]{1,0:T(8,128)S(1)}, u32[]{:S(2)}, u32[]{:S(2)}) collective-permute-start(f32[60,256]{1,0:T(8,128)S(1)} %get-tuple-element.55), channel_id=1, source_target_pairs={{0,16},{1,17},{2,18},{3,19},{4,20},{5,21},{6,22},{7,23},{8,24},{9,... | collective-permute-start | bytes 184328 | tf_op jit(solution)/shard_map/ppermute | solution.py:31
  123.9 5.6 %collective-permute-start.8 = (f32[60,256]{1,0:T(8,128)S(1)}, f32[60,256]{1,0:T(8,128)S(1)}, u32[]{:S(2)}, u32[]{:S(2)}) collective-permute-start(f32[60,256]{1,0:T(8,128)S(1)} %get-tuple-element.56), channel_id=1, source_target_pairs={{16,32},{17,33},{18,34},{19,35},{20,36},{21,37},{22,38},{23,39},{2... | collective-permute-start | bytes 184328 | tf_op jit(solution)/shard_map/ppermute | solution.py:31
  129.8 7.4 %collective-permute-start.10 = (f32[46,256]{1,0:T(8,128)S(1)}, f32[46,256]{1,0:T(8,128)S(1)}, u32[]{:S(2)}, u32[]{:S(2)}) collective-permute-start(f32[46,256]{1,0:T(8,128)S(1)} %get-tuple-element.59), channel_id=1, source_target_pairs={{1,2},{2,1},{3,4},{4,3},{5,6},{6,5},{7,8},{8,7},{9,10},{10,9},{11,... | collective-permute-start | bytes 141320 | tf_op jit(solution)/shard_map/ppermute | solution.py:31
  133.8 3.4 %collective-permute-start.11 = (f32[46,256]{1,0:T(8,128)S(1)}, f32[46,256]{1,0:T(8,128)S(1)}, u32[]{:S(2)}, u32[]{:S(2)}) collective-permute-start(f32[46,256]{1,0:T(8,128)S(1)} %get-tuple-element.60), channel_id=1, source_target_pairs={{0,1},{1,0},{2,3},{3,2},{4,5},{5,4},{6,7},{7,6},{8,9},{9,8},{10,11... | collective-permute-start | bytes 141320 | tf_op jit(solution)/shard_map/ppermute | solution.py:31
  151.3 12.3 %collective-permute-start.12 = (bf16[8,128,128]{2,1,0:T(8,128)(2,1)}, bf16[8,128,128]{2,1,0:T(8,128)(2,1)S(1)}, u32[]{:S(2)}, u32[]{:S(2)}) collective-permute-start(bf16[8,128,128]{2,1,0:T(8,128)(2,1)} %get-tuple-element.31), channel_id=1, source_target_pairs={{0,1},{1,0},{2,3},{3,2},{4,5},{5,4},{6,7},{7,6},{8,9},{9,8},{10,11... | collective-permute-start | bytes 786440 | tf_op jit(solution)/shard_map/ppermute | solution.py:31
  151.4 16.2 %collective-permute-start.13 = (bf16[8,128,128]{2,1,0:T(8,128)(2,1)}, bf16[8,128,128]{2,1,0:T(8,128)(2,1)S(1)}, u32[]{:S(2)}, u32[]{:S(2)}) collective-permute-start(bf16[8,128,128]{2,1,0:T(8,128)(2,1)} %get-tuple-element.32), channel_id=1, source_target_pairs={{1,2},{2,1},{3,4},{4,3},{5,6},{6,5},{7,8},{8,7},{9,10},{10,9},{11,... | collective-permute-start | bytes 786440 | tf_op jit(solution)/shard_map/ppermute | solution.py:31
  155.3 15.0 %collective-permute-start.14 = (bf16[8,128,128]{2,1,0:T(8,128)(2,1)}, bf16[8,128,128]{2,1,0:T(8,128)(2,1)S(1)}, u32[]{:S(2)}, u32[]{:S(2)}) collective-permute-start(bf16[8,128,128]{2,1,0:T(8,128)(2,1)} %get-tuple-element.33), channel_id=1, source_target_pairs={{0,17},{1,16},{2,19},{3,18},{4,21},{5,20},{6,23},{7,22},{8,25},{9,... | collective-permute-start | bytes 786440 | tf_op jit(solution)/shard_map/ppermute | solution.py:31
  157.3 14.5 %collective-permute-start.15 = (bf16[8,128,128]{2,1,0:T(8,128)(2,1)}, bf16[8,128,128]{2,1,0:T(8,128)(2,1)S(1)}, u32[]{:S(2)}, u32[]{:S(2)}) collective-permute-start(bf16[8,128,128]{2,1,0:T(8,128)(2,1)} %get-tuple-element.34), channel_id=1, source_target_pairs={{1,18},{2,17},{3,20},{4,19},{5,22},{6,21},{7,24},{8,23},{9,26},{10... | collective-permute-start | bytes 786440 | tf_op jit(solution)/shard_map/ppermute | solution.py:31
  160.1 11.7 %collective-permute-start.16 = (bf16[8,128,128]{2,1,0:T(8,128)(2,1)}, bf16[8,128,128]{2,1,0:T(8,128)(2,1)S(1)}, u32[]{:S(2)}, u32[]{:S(2)}) collective-permute-start(bf16[8,128,128]{2,1,0:T(8,128)(2,1)} %get-tuple-element.35), channel_id=1, source_target_pairs={{16,33},{17,32},{18,35},{19,34},{20,37},{21,36},{22,39},{23,38},{2... | collective-permute-start | bytes 786440 | tf_op jit(solution)/shard_map/ppermute | solution.py:31
  163.6 13.7 %copy-start.9 = (bf16[8,128,128]{2,1,0:T(8,128)(2,1)}, bf16[8,128,128]{2,1,0:T(8,128)(2,1)S(1)}, u32[]{:S(2)}) copy-start(bf16[8,128,128]{2,1,0:T(8,128)(2,1)S(1)} %collective-permute-done.12.rest_1_) | copy-start | bytes 786436
  163.6 12.6 %collective-permute-start.17 = (bf16[8,128,128]{2,1,0:T(8,128)(2,1)}, bf16[8,128,128]{2,1,0:T(8,128)(2,1)S(1)}, u32[]{:S(2)}, u32[]{:S(2)}) collective-permute-start(bf16[8,128,128]{2,1,0:T(8,128)(2,1)} %get-tuple-element.36), channel_id=1, source_target_pairs={{17,34},{18,33},{19,36},{20,35},{21,38},{22,37},{23,40},{24,39},{2... | collective-permute-start | bytes 786440 | tf_op jit(solution)/shard_map/ppermute | solution.py:31
  167.6 9.7 %collective-permute-start.18 = (bf16[8,128,128]{2,1,0:T(8,128)(2,1)}, bf16[8,128,128]{2,1,0:T(8,128)(2,1)S(1)}, u32[]{:S(2)}, u32[]{:S(2)}) collective-permute-start(bf16[8,128,128]{2,1,0:T(8,128)(2,1)} %get-tuple-element.37), channel_id=1, source_target_pairs={{16,32},{17,33},{18,34},{19,35},{20,36},{21,37},{22,38},{23,39},{2... | collective-permute-start | bytes 786440 | tf_op jit(solution)/shard_map/ppermute | solution.py:31
  170.3 7.0 %collective-permute-start.19 = (bf16[8,128,128]{2,1,0:T(8,128)(2,1)}, bf16[8,128,128]{2,1,0:T(8,128)(2,1)S(1)}, u32[]{:S(2)}, u32[]{:S(2)}) collective-permute-start(bf16[8,128,128]{2,1,0:T(8,128)(2,1)} %get-tuple-element.38), channel_id=1, source_target_pairs={{0,16},{1,17},{2,18},{3,19},{4,20},{5,21},{6,22},{7,23},{8,24},{9,... | collective-permute-start | bytes 786440 | tf_op jit(solution)/shard_map/ppermute | solution.py:31
  (14 other events, 58.6 us)

commit v2 on v1

v2 whole, which is shorter than its diff:
```python
import functools

import jax
import jax.numpy as jnp
from jax import lax
from jax.experimental import pallas as pl
from jax.experimental.pallas import tpu as pltpu
from jax.sharding import PartitionSpec as P

SWEEPS = 3
CELL_VOLUME = 0.0625

KINDS = ((0, 0), (0, 1), (0, 2), (1, 1), (1, 2), (2, 1), (2, 2), (2, 0), (1, 0))


def partner(index, kind):
    if kind == 0:
        return index
    return index + 1 if index % 2 == kind - 1 else index - 1


def swap(value, kind, sizes):
    count_x, count_y = sizes
    pairs = []
    for p in range(count_x):
        for q in range(count_y):
            to_p, to_q = partner(p, kind[0]), partner(q, kind[1])
            if 0 <= to_p < count_x and 0 <= to_q < count_y:
                pairs.append((p * count_y + q, to_p * count_y + to_q))
    return lax.ppermute(value, ("gx", "gy"), pairs)


def group_ids():
    p, q = lax.axis_index("gx"), lax.axis_index("gy")

    def side(index, kind):
        if kind == 0:
            return 1
        return jnp.where((index & 1) == kind - 1, 2, 0)

    return [side(p, a) * 3 + side(q, b) for a, b in KINDS]


def call(body, name, megabytes, **options):
    return pl.pallas_call(
        body,
        name=name,
        compiler_params=pltpu.CompilerParams(vmem_limit_bytes=megabytes * 1024 * 1024),
        **options,
    )


SMEM = pl.BlockSpec(memory_space=pltpu.SMEM)
VMEM = pl.BlockSpec(memory_space=pltpu.VMEM)
ANY = pl.BlockSpec(memory_space=pl.ANY)


def gather_body(table, blocks, *outs):
    depth = table.shape[2]
    for group, out in zip(group_ids(), outs):
        for c in range(depth):
            out[c] = blocks[jnp.maximum(table[group, 0, c], 0)]


def gather(table, blocks):
    depth, width = table.shape[2], blocks.shape[1]
    kinds = len(KINDS)
    return call(
        gather_body,
        "gather",
        12,
        in_specs=[SMEM, VMEM],
        out_specs=[VMEM] * kinds,
        out_shape=[jax.ShapeDtypeStruct((depth, width, width), blocks.dtype)] * kinds,
    )(table, blocks)


def slot_of(slots, x, y, a, b, empty):
    slot = slots[x, a, b, y]
    return jnp.where(slot < 0, empty, slot)


def density_body(slots, basis, *rest):
    kinds = len(KINDS)
    messages, rest = rest[:kinds], rest[kinds:]
    out, turned_out, held, turned, blocks, sems_in, sems_out, block_sems = rest
    brick_x, brick_y, per, points, width = basis.shape
    depth = messages[0].shape[0]
    empty = kinds * depth

    def coming(x):
        return pltpu.make_async_copy(basis.at[x], held.at[x % 2], sems_in.at[x])

    def going(x):
        return pltpu.make_async_copy(turned.at[x % 2], turned_out.at[x], sems_out.at[x])

    arrivals = [
        pltpu.make_async_copy(message, blocks.at[pl.ds(group * depth, depth)], block_sems.at[t])
        for t, (group, message) in enumerate(zip(group_ids(), messages))
    ]
    coming(0).start()
    for copy in arrivals:
        copy.start()
    coming(1).start()
    blocks[empty] = jnp.zeros((width, width), blocks.dtype)
    for copy in arrivals:
        copy.wait()

    def one(x, y):
        side = x % 2
        for b in range(per):
            turned[side, y, b * width : (b + 1) * width, :] = held[side, y, b].T
        rows = [
            jnp.concatenate(
                [blocks[slot_of(slots, x, y, a, b, empty)] for b in range(per)], axis=1
            )
            for a in range(per)
        ]
        right = turned[side, y]
        mixed = jnp.dot(
            jnp.concatenate(rows, axis=0), right, preferred_element_type=jnp.float32
        )
        product = mixed * right.astype(jnp.float32)
        out[y, pl.ds(x, 1), :] = jnp.sum(product, axis=0, keepdims=True)

    def step(x, carry):
        coming(x).wait()

        @pl.when(x >= 2)
        def _():
            going(x - 2).wait()

        for y in range(brick_y):
            one(x, y)
        going(x).start()

        @pl.when(x + 2 < brick_x)
        def _():
            coming(x + 2).start()

        return carry

    lax.fori_loop(0, brick_x, step, 0)
    going(brick_x - 2).wait()
    going(brick_x - 1).wait()


def density_of(slots, basis, messages):
    brick_x, brick_y, per, points, width = basis.shape
    depth = messages[0].shape[0]
    kinds = len(KINDS)
    turned = (brick_x, brick_y, per * width, points)
    return call(
        density_body,
        "density",
        20,
        in_specs=[SMEM] + [ANY] * (1 + kinds),
        out_specs=[VMEM, ANY],
        out_shape=[
            jax.ShapeDtypeStruct((brick_y, brick_x, points), jnp.float32),
            jax.ShapeDtypeStruct(turned, basis.dtype),
        ],
        scratch_shapes=[
            pltpu.VMEM((2,) + basis.shape[1:], basis.dtype),
            pltpu.VMEM((2,) + turned[1:], basis.dtype),
            pltpu.VMEM((kinds * depth + 1, width, width), basis.dtype),
            pltpu.SemaphoreType.DMA((brick_x,)),
            pltpu.SemaphoreType.DMA((brick_x,)),
            pltpu.SemaphoreType.DMA((kinds,)),
        ],
    )(slots, basis, *messages)


def stencil(field, charge):
    z_padded = jnp.pad(field, ((0, 0), (0, 0), (1, 1)))
    beside = z_padded[2:, 1:-1, 1:-1] + z_padded[:-2, 1:-1, 1:-1]
    beside = beside + z_padded[1:-1, 2:, 1:-1] + z_padded[1:-1, :-2, 1:-1]
    beside = beside + z_padded[1:-1, 1:-1, 2:] + z_padded[1:-1, 1:-1, :-2]
    return (beside + charge) / 6.0


def halo(field, charge, dim, axis, sizes):
    length = field.shape[dim]
    wide, thin = SWEEPS, SWEEPS - 1
    even = lax.axis_index(axis) % 2 == 0
    field_shape = list(field.shape)
    charge_shape = list(charge.shape)
    field_shape[dim], charge_shape[dim] = wide, thin
    points = field.shape[-1]

    def pack(field_start, charge_start):
        a = lax.slice_in_dim(field, field_start, field_start + wide, axis=dim)
        b = lax.slice_in_dim(charge, charge_start, charge_start + thin, axis=dim)
        return jnp.concatenate([a.reshape(-1, points), b.reshape(-1, points)], axis=0)

    low, high = pack(0, 0), pack(length - wide, length - thin)
    kinds = ((1, 0), (2, 0)) if axis == "gx" else ((0, 1), (0, 2))
    first = swap(jnp.where(even, high, low), kinds[0], sizes)
    second = swap(jnp.where(even, low, high), kinds[1], sizes)
    before, after = jnp.where(even, second, first), jnp.where(even, first, second)

    def unpack(rows):
        cut = 1
        for size in field_shape[:-1]:
            cut *= size
        return rows[:cut].reshape(field_shape), rows[cut:].reshape(charge_shape)

    (field_before, charge_before), (field_after, charge_after) = unpack(before), unpack(after)
    return (
        jnp.concatenate([field_before, field, field_after], axis=dim),
        jnp.concatenate([charge_before, charge, charge_after], axis=dim),
    )


def inside(width, brick_x, brick_y, sizes):
    p, q = lax.axis_index("gx"), lax.axis_index("gy")
    shape = (brick_y + 2 * width, brick_x + 2 * width, 1)
    y = lax.broadcasted_iota(jnp.int32, shape, 0) - width + q * brick_y
    x = lax.broadcasted_iota(jnp.int32, shape, 1) - width + p * brick_x
    return (x >= 0) & (x < sizes[0] * brick_x) & (y >= 0) & (y < sizes[1] * brick_y)


def sweeps(previous, density, sizes):
    brick_y, brick_x, _ = density.shape
    field, charge = halo(previous, density, 1, "gx", sizes)
    field, charge = halo(field, charge, 0, "gy", sizes)
    for done in range(1, SWEEPS + 1):
        width = SWEEPS - done
        field = stencil(field, charge)
        if width:
            field = jnp.where(inside(width, brick_x, brick_y, sizes), field, 0.0)
            charge = charge[1:-1, 1:-1]
    return field


def integrals_body(unroll, slots, basis, potential, *rest):
    kinds = len(KINDS)
    outs, (held, sums, sems) = rest[:kinds], rest[kinds:]
    brick_x, brick_y, rows, _ = basis.shape
    depth, width, _ = outs[0].shape
    per = rows // width
    empty = kinds * depth

    def coming(x):
        return pltpu.make_async_copy(basis.at[x], held.at[x % 2], sems.at[x])

    coming(0).start()
    coming(1).start()
    sums[...] = jnp.zeros_like(sums)

    def one(x, y):
        left = held[x % 2, y]
        weighted = (left.astype(jnp.float32) * potential[y, pl.ds(x, 1), :]).astype(basis.dtype)
        product = lax.dot_general(
            left, weighted, (((1,), (1,)), ((), ())), preferred_element_type=jnp.float32
        )
        for a in range(per):
            for b in range(per):
                slot = slot_of(slots, x, y, a, b, empty)
                sums[slot] += product[a * width : (a + 1) * width, b * width : (b + 1) * width]

    def step(x, carry):
        coming(x).wait()

        def some(j, carry):
            for u in range(unroll):
                one(x, j * unroll + u)
            return carry

        lax.fori_loop(0, brick_y // unroll, some, 0)

        @pl.when(x + 2 < brick_x)
        def _():
            coming(x + 2).start()

        return carry

    lax.fori_loop(0, brick_x, step, 0)
    for group, out in zip(group_ids(), outs):
        part = sums[pl.ds(group * depth, depth)]
        out[...] = (CELL_VOLUME * part).astype(out.dtype)


def integrals_of(slots, basis, potential, depth, width, unroll=6):
    brick_x = basis.shape[0]
    kinds = len(KINDS)
    shape = (depth, width, width)
    return call(
        functools.partial(integrals_body, unroll),
        "integrals",
        20,
        in_specs=[SMEM, ANY, VMEM],
        out_specs=[VMEM] * kinds,
        out_shape=[jax.ShapeDtypeStruct(shape, jnp.float32)]
        + [jax.ShapeDtypeStruct(shape, jnp.bfloat16)] * (kinds - 1),
        scratch_shapes=[
            pltpu.VMEM((2,) + basis.shape[1:], basis.dtype),
            pltpu.VMEM((kinds * depth + 1, width, width), jnp.float32),
            pltpu.SemaphoreType.DMA((brick_x,)),
        ],
    )(slots, basis, potential)


def collect_body(table, *rest):
    messages, out = rest[:-1], rest[-1]
    depth = table.shape[2]
    out[...] = jnp.zeros_like(out)
    for group, message in zip(group_ids(), messages):
        for c in range(depth):
            row = table[group, 0, c]

            @pl.when(row >= 0)
            def _():
                out[row] += message[c].astype(jnp.float32)


def collect(table, messages, owned):
    width = messages[0].shape[1]
    return call(
        collect_body,
        "collect",
        12,
        in_specs=[SMEM] + [VMEM] * len(messages),
        out_specs=VMEM,
        out_shape=jax.ShapeDtypeStruct((owned, width, width), jnp.float32),
    )(table, *messages)


def per_device(
    sizes, density_blocks, send_table, batch_pairs, basis_values, previous_hartree, external_potential
):
    owned, width, _ = density_blocks.shape
    depth = send_table.shape[3]
    table = send_table.reshape(9, 1, depth)
    slots = batch_pairs.transpose(0, 2, 3, 1)
    outgoing = gather(table, density_blocks)
    arrived = [outgoing[0]] + [swap(m, kind, sizes) for m, kind in zip(outgoing[1:], KINDS[1:])]
    density, basis = density_of(slots, basis_values, arrived)
    hartree = sweeps(previous_hartree.transpose(1, 0, 2), density, sizes)
    field = hartree + external_potential.transpose(1, 0, 2)
    partial = integrals_of(slots, basis, field, depth, width)
    returned = [partial[0]] + [swap(m, kind, sizes) for m, kind in zip(partial[1:], KINDS[1:])]
    potential = collect(table, returned, owned)
    return density.transpose(1, 0, 2), hartree.transpose(1, 0, 2), potential


def solution(mesh):
    sizes = (mesh.shape["gx"], mesh.shape["gy"])
    in_specs = (
        P(("gx", "gy"), None, None),
        P(("gx", "gy"), None, None, None),
        P("gx", "gy", None, None),
        P("gx", "gy", None, None, None),
        P("gx", "gy", None),
        P("gx", "gy", None),
    )
    out_specs = (P("gx", "gy", None), P("gx", "gy", None), P(("gx", "gy"), None, None))
    return jax.shard_map(
        functools.partial(per_device, sizes),
        mesh=mesh,
        in_specs=in_specs,
        out_specs=out_specs,
        check_vma=False,
    )
```

time: 184 us -> 119 us (0.65)
  Pallas kernels: 113 us -> 28.4 us
  local copies, waits for them, and re-layouts: 9.35 us -> 21.4 us
  waiting for transfers between devices: 10.5 us -> 17.1 us
  other arithmetic: 1.46 us -> 4.87 us
  starting transfers between devices: 47.7 us -> 45.4 us
    pallas_call x5 -> x4, Pallas kernels: 113 us -> 28.3 us  [the longest x1 11.7 us: integrals_of(): call(functools.partial(integrals_body, unroll), 'integrals', 20, in_specs...]
    unnamed x43 -> x24, local copies, waits for them, and re-layouts: 4.39 us -> 16.7 us
    ppermute x20, waiting for transfers between devices: 10.5 us -> 17.1 us  [swap(): return lax.ppermute(value, ('gx', 'gy'), pairs)]
    ppermute x20, starting transfers between devices: 47.7 us -> 45.4 us  [swap(): return lax.ppermute(value, ('gx', 'gy'), pairs)]
    reshape x3 -> x0, local copies, waits for them, and re-layouts: 2.17 us -> none  [the longest x1 0.81 us: per_device(): density_of(groups, slots, basis, arrived).reshape(brick_x, brick_y, points)]
    reshape x4, local copies, waits for them, and re-layouts: 0.05 us -> 2.07 us  [pack(): a.reshape(-1, points)]
  transfers between devices with their start and end apart: 20 -> 20, of which waited for: 4 -> 7; matrix products, arithmetic and copies ran while one was open for 3% -> 4% of each run, Pallas kernels for 5% -> 0%
where the time goes in v2:
time: 119 us; the launch traced here: 118 us
  starting transfers between devices  45.4 us (38%)
  Pallas kernels  28.4 us (24%)
  local copies, waits for them, and re-layouts  21.4 us (18%)
  waiting for transfers between devices  17.1 us (14%)
  other arithmetic  4.87 us (4%)
    ppermute x20, starting transfers between devices, swap(): return lax.ppermute(value, ('gx', 'gy'), pairs)  45.4 us
    ppermute x20, waiting for transfers between devices, swap(): return lax.ppermute(value, ('gx', 'gy'), pairs)  17.1 us
    unnamed x24, local copies, waits for them, and re-layouts  16.7 us
    pallas_call x1, Pallas kernels, integrals_of(): call(functools.partial(integrals_body, unroll), 'integrals', 20, in_specs...  11.7 us
    pallas_call x1, Pallas kernels, density_of(): call(density_body, 'density', 20, in_specs=[SMEM] + [ANY] * (1 + kinds),...  11.4 us
    pallas_call x1, Pallas kernels, collect(): call(collect_body, 'collect', 12, in_specs=[SMEM] + [VMEM] * len(messages...  3.77 us
  transfers between devices with their start and end apart: 20, of which 7 were waited for; matrix products, arithmetic and copies ran while one was open for 4% of the time, Pallas kernels for 0%

profile of v2, /device:TPU:13, one launch (start us, length us, event | category | flops | bytes accessed | tf_op | source)
XLA Modules:
  0.0 118.2 jit_solution(17464394176881041565)
XLA Ops:
  4.4 1.6 %collective-permute-start = (bf16[8,128,128]{2,1,0:T(8,128)(2,1)S(1)}, bf16[8,128,128]{2,1,0:T(8,128)(2,1)S(1)}, u32[]{:S(2)}, u32[]{:S(2)}) collective-permute-start(bf16[8,128,128]{2,1,0:T(8,128)(2,1)S(1)} %get-tuple-element.24), channel_id=1, source_target_pairs={{0,1},{1,0},{2,3},{3,2},{4,5},{5,4},{6,7},{7,6},{8,9},{9,8},{10,11... | collective-permute-start | bytes 786440 | tf_op jit(solution)/shard_map/ppermute | solution.py:30
  6.0 4.1 %collective-permute-start.1 = (bf16[8,128,128]{2,1,0:T(8,128)(2,1)S(1)}, bf16[8,128,128]{2,1,0:T(8,128)(2,1)S(1)}, u32[]{:S(2)}, u32[]{:S(2)}) collective-permute-start(bf16[8,128,128]{2,1,0:T(8,128)(2,1)S(1)} %get-tuple-element.25), channel_id=1, source_target_pairs={{1,2},{2,1},{3,4},{4,3},{5,6},{6,5},{7,8},{8,7},{9,10},{10,9},{11,... | collective-permute-start | bytes 786440 | tf_op jit(solution)/shard_map/ppermute | solution.py:30
  10.2 2.0 %collective-permute-start.2 = (bf16[8,128,128]{2,1,0:T(8,128)(2,1)S(1)}, bf16[8,128,128]{2,1,0:T(8,128)(2,1)S(1)}, u32[]{:S(2)}, u32[]{:S(2)}) collective-permute-start(bf16[8,128,128]{2,1,0:T(8,128)(2,1)S(1)} %get-tuple-element.26), channel_id=1, source_target_pairs={{0,17},{1,16},{2,19},{3,18},{4,21},{5,20},{6,23},{7,22},{8,25},{9,... | collective-permute-start | bytes 786440 | tf_op jit(solution)/shard_map/ppermute | solution.py:30
  12.1 2.5 %collective-permute-start.3 = (bf16[8,128,128]{2,1,0:T(8,128)(2,1)}, bf16[8,128,128]{2,1,0:T(8,128)(2,1)S(1)}, u32[]{:S(2)}, u32[]{:S(2)}) collective-permute-start(bf16[8,128,128]{2,1,0:T(8,128)(2,1)} %get-tuple-element.27), channel_id=1, source_target_pairs={{1,18},{2,17},{3,20},{4,19},{5,22},{6,21},{7,24},{8,23},{9,26},{10... | collective-permute-start | bytes 786440 | tf_op jit(solution)/shard_map/ppermute | solution.py:30
  14.6 3.8 %collective-permute-start.4 = (bf16[8,128,128]{2,1,0:T(8,128)(2,1)S(1)}, bf16[8,128,128]{2,1,0:T(8,128)(2,1)S(1)}, u32[]{:S(2)}, u32[]{:S(2)}) collective-permute-start(bf16[8,128,128]{2,1,0:T(8,128)(2,1)S(1)} %get-tuple-element.28), channel_id=1, source_target_pairs={{16,33},{17,32},{18,35},{19,34},{20,37},{21,36},{22,39},{23,38},{2... | collective-permute-start | bytes 786440 | tf_op jit(solution)/shard_map/ppermute | solution.py:30
  20.0 4.3 %collective-permute-start.5 = (bf16[8,128,128]{2,1,0:T(8,128)(2,1)S(1)}, bf16[8,128,128]{2,1,0:T(8,128)(2,1)S(1)}, u32[]{:S(2)}, u32[]{:S(2)}) collective-permute-start(bf16[8,128,128]{2,1,0:T(8,128)(2,1)S(1)} %get-tuple-element.29), channel_id=1, source_target_pairs={{17,34},{18,33},{19,36},{20,35},{21,38},{22,37},{23,40},{24,39},{2... | collective-permute-start | bytes 786440 | tf_op jit(solution)/shard_map/ppermute | solution.py:30
  24.3 2.5 %collective-permute-start.6 = (bf16[8,128,128]{2,1,0:T(8,128)(2,1)S(1)}, bf16[8,128,128]{2,1,0:T(8,128)(2,1)S(1)}, u32[]{:S(2)}, u32[]{:S(2)}) collective-permute-start(bf16[8,128,128]{2,1,0:T(8,128)(2,1)S(1)} %get-tuple-element.30), channel_id=1, source_target_pairs={{16,32},{17,33},{18,34},{19,35},{20,36},{21,37},{22,38},{23,39},{2... | collective-permute-start | bytes 786440 | tf_op jit(solution)/shard_map/ppermute | solution.py:30
  30.2 2.3 %collective-permute-done.5.rest_6_ = bf16[8,128,128]{2,1,0:T(8,128)(2,1)S(1)} collective-permute-done((bf16[8,128,128]{2,1,0:T(8,128)(2,1)S(1)}, bf16[8,128,128]{2,1,0:T(8,128)(2,1)S(1)}, u32[]{:S(2)}, u32[]{:S(2)}) %collective-permute-start.5) | collective-permute-done | bytes 262176 | tf_op jit(solution)/shard_map/ppermute | solution.py:30
  33.7 4.6 %copy-done = bf16[4,12,4,256,128]{4,3,2,1,0:T(8,128)(2,1)S(1)} copy-done((bf16[4,12,4,256,128]{4,3,2,1,0:T(8,128)(2,1)S(1)}, bf16[4,12,4,256,128]{4,3,2,1,0:T(8,128)(2,1)}, u32[]{:S(2)}) %copy-start) | copy-done | bytes 12582936
  39.1 11.4 %density.1 = (f32[12,4,256]{2,1,0:T(4,128)}, bf16[4,12,512,256]{3,2,1,0:T(8,128)(2,1)S(1)}) custom-call(s32[4,4,4,12]{3,2,1,0:T(4,128)S(1)} %bitcast.15, bf16[4,12,4,256,128]{4,3,2,1,0:T(8,128)(2,1)S(1)} %copy-done, bf16[8,128,128]{2,1,0:T(8,128)(2,1)S(1)} %get-tuple-element.23.rest_0_, bf16[8,128,128]{2,1,0:T(8,128)(2,1)S(1)} %collective-permute-done.rest_1_, ...), custom_call_target="tpu_custom_call" | custom-call | tf_op jit(solution)/shard_map/density/pallas_call | solution.py:153
  50.5 4.5 %copy-done.1 = bf16[4,12,512,256]{3,2,1,0:T(8,128)(2,1)} copy-done((bf16[4,12,512,256]{3,2,1,0:T(8,128)(2,1)}, bf16[4,12,512,256]{3,2,1,0:T(8,128)(2,1)S(1)}, u32[]{:S(2)}) %copy-start.1) | copy-done | bytes 12582936
  56.0 2.6 %collective-permute-start.8 = (f32[60,256]{1,0:T(8,128)S(1)}, f32[60,256]{1,0:T(8,128)S(1)}, u32[]{:S(2)}, u32[]{:S(2)}) collective-permute-start(f32[60,256]{1,0:T(8,128)S(1)} %get-tuple-element.51), channel_id=1, source_target_pairs={{16,32},{17,33},{18,34},{19,35},{20,36},{21,37},{22,38},{23,39},{2... | collective-permute-start | bytes 184328 | tf_op jit(solution)/shard_map/ppermute | solution.py:30
  58.8 2.8 %collective-permute-done.8 = f32[60,256]{1,0:T(8,128)S(1)} collective-permute-done((f32[60,256]{1,0:T(8,128)S(1)}, f32[60,256]{1,0:T(8,128)S(1)}, u32[]{:S(2)}, u32[]{:S(2)}) %collective-permute-start.8) | collective-permute-done | bytes 61472 | tf_op jit(solution)/shard_map/ppermute | solution.py:30
  62.6 3.1 %collective-permute-start.10 = (f32[46,256]{1,0:T(8,128)S(1)}, f32[46,256]{1,0:T(8,128)S(1)}, u32[]{:S(2)}, u32[]{:S(2)}) collective-permute-start(f32[46,256]{1,0:T(8,128)S(1)} %get-tuple-element.55), channel_id=1, source_target_pairs={{1,2},{2,1},{3,4},{4,3},{5,6},{6,5},{7,8},{8,7},{9,10},{10,9},{11,... | collective-permute-start | bytes 141320 | tf_op jit(solution)/shard_map/ppermute | solution.py:30
  65.9 3.6 %collective-permute-done.10 = f32[46,256]{1,0:T(8,128)S(1)} collective-permute-done((f32[46,256]{1,0:T(8,128)S(1)}, f32[46,256]{1,0:T(8,128)S(1)}, u32[]{:S(2)}, u32[]{:S(2)}) %collective-permute-start.10) | collective-permute-done | bytes 47136 | tf_op jit(solution)/shard_map/ppermute | solution.py:30
  72.4 4.6 %copy-done.2 = bf16[4,12,512,256]{3,2,1,0:T(8,128)(2,1)S(1)} copy-done((bf16[4,12,512,256]{3,2,1,0:T(8,128)(2,1)S(1)}, bf16[4,12,512,256]{3,2,1,0:T(8,128)(2,1)}, u32[]{:S(2)}) %copy-start.2) | copy-done | bytes 12582936
  77.0 11.7 %integrals.1 = (f32[8,128,128]{2,1,0:T(8,128)S(1)}, bf16[8,128,128]{2,1,0:T(8,128)(2,1)S(1)}, bf16[8,128,128]{2,1,0:T(8,128)(2,1)S(1)}, bf16[8,128,128]{2,1,0:T(...) custom-call(s32[4,4,4,12]{3,2,1,0:T(4,128)S(1)} %bitcast.16, ...), custom_call_target="tpu_custom_call" | custom-call | tf_op jit(solution)/shard_map/integrals/pallas_call | solution.py:288
  88.8 3.5 %collective-permute-start.13 = (bf16[8,128,128]{2,1,0:T(8,128)(2,1)S(1)}, bf16[8,128,128]{2,1,0:T(8,128)(2,1)S(1)}, u32[]{:S(2)}, u32[]{:S(2)}) collective-permute-start(bf16[8,128,128]{2,1,0:T(8,128)(2,1)S(1)} %get-tuple-element.36), channel_id=1, source_target_pairs={{1,2},{2,1},{3,4},{4,3},{5,6},{6,5},{7,8},{8,7},{9,10},{10,9},{11,... | collective-permute-start | bytes 786440 | tf_op jit(solution)/shard_map/ppermute | solution.py:30
  93.7 3.8 %collective-permute-start.15 = (bf16[8,128,128]{2,1,0:T(8,128)(2,1)S(1)}, bf16[8,128,128]{2,1,0:T(8,128)(2,1)S(1)}, u32[]{:S(2)}, u32[]{:S(2)}) collective-permute-start(bf16[8,128,128]{2,1,0:T(8,128)(2,1)S(1)} %get-tuple-element.38), channel_id=1, source_target_pairs={{1,18},{2,17},{3,20},{4,19},{5,22},{6,21},{7,24},{8,23},{9,26},{10... | collective-permute-start | bytes 786440 | tf_op jit(solution)/shard_map/ppermute | solution.py:30
  97.6 3.7 %collective-permute-start.16 = (bf16[8,128,128]{2,1,0:T(8,128)(2,1)S(1)}, bf16[8,128,128]{2,1,0:T(8,128)(2,1)S(1)}, u32[]{:S(2)}, u32[]{:S(2)}) collective-permute-start(bf16[8,128,128]{2,1,0:T(8,128)(2,1)S(1)} %get-tuple-element.39), channel_id=1, source_target_pairs={{16,33},{17,32},{18,35},{19,34},{20,37},{21,36},{22,39},{23,38},{2... | collective-permute-start | bytes 786440 | tf_op jit(solution)/shard_map/ppermute | solution.py:30
  101.3 3.9 %collective-permute-start.17 = (bf16[8,128,128]{2,1,0:T(8,128)(2,1)S(1)}, bf16[8,128,128]{2,1,0:T(8,128)(2,1)S(1)}, u32[]{:S(2)}, u32[]{:S(2)}) collective-permute-start(bf16[8,128,128]{2,1,0:T(8,128)(2,1)S(1)} %get-tuple-element.40), channel_id=1, source_target_pairs={{17,34},{18,33},{19,36},{20,35},{21,38},{22,37},{23,40},{24,39},{2... | collective-permute-start | bytes 786440 | tf_op jit(solution)/shard_map/ppermute | solution.py:30
  105.2 2.0 %collective-permute-start.18 = (bf16[8,128,128]{2,1,0:T(8,128)(2,1)S(1)}, bf16[8,128,128]{2,1,0:T(8,128)(2,1)S(1)}, u32[]{:S(2)}, u32[]{:S(2)}) collective-permute-start(bf16[8,128,128]{2,1,0:T(8,128)(2,1)S(1)} %get-tuple-element.41), channel_id=1, source_target_pairs={{16,32},{17,33},{18,34},{19,35},{20,36},{21,37},{22,38},{23,39},{2... | collective-permute-start | bytes 786440 | tf_op jit(solution)/shard_map/ppermute | solution.py:30
  108.3 5.0 %collective-permute-done.17.rest_6_ = bf16[8,128,128]{2,1,0:T(8,128)(2,1)S(1)} collective-permute-done((bf16[8,128,128]{2,1,0:T(8,128)(2,1)S(1)}, bf16[8,128,128]{2,1,0:T(8,128)(2,1)S(1)}, u32[]{:S(2)}, u32[]{:S(2)}) %collective-permute-start.17) | collective-permute-done | bytes 262176 | tf_op jit(solution)/shard_map/ppermute | solution.py:30
  114.5 3.8 %collect.1 = f32[64,128,128]{2,1,0:T(8,128)} custom-call(s32[9,1,8]{2,1,0:T(1,128)S(1)} %bitcast.18, f32[8,128,128]{2,1,0:T(8,128)S(1)} %get-tuple-element.34.rest_0_, bf16[8,128,128]{2,1,0:T(8,128)(2,1)S(1)} %collective-permute-done.12.rest_1_, bf16[8,128,128]{2,1,0:T(8,128)(2,1)S(1)} %collective-permute-done.13.rest_2_, ...), custom_call_target="tpu_custom_call" | custom-call | tf_op jit(solution)/shard_map/collect/pallas_call | solution.py:319
  (81 shorter events, 19.3 us)
Async XLA Ops:
  2.9 58.9 %copy-start.8 = (f32[4,12,256]{2,0,1:T(4,128)S(1)}, f32[4,12,256]{2,0,1:T(4,128)}, u32[]{:S(2)}) copy-start(f32[4,12,256]{2,0,1:T(4,128)} %param.10) | copy-start | bytes 147460
  2.9 69.5 %copy-start.5 = (s32[4,12,4,4]{1,3,2,0:T(4,128)S(1)}, s32[4,12,4,4]{1,3,2,0:T(4,128)}, u32[]{:S(2)}) copy-start(s32[4,12,4,4]{1,3,2,0:T(4,128)} %param.8) | copy-start | bytes 9220
  4.4 15.6 %collective-permute-start = (bf16[8,128,128]{2,1,0:T(8,128)(2,1)S(1)}, bf16[8,128,128]{2,1,0:T(8,128)(2,1)S(1)}, u32[]{:S(2)}, u32[]{:S(2)}) collective-permute-start(bf16[8,128,128]{2,1,0:T(8,128)(2,1)S(1)} %get-tuple-element.24), channel_id=1, source_target_pairs={{0,1},{1,0},{2,3},{3,2},{4,5},{5,4},{6,7},{7,6},{8,9},{9,8},{10,11... | collective-permute-start | bytes 786440 | tf_op jit(solution)/shard_map/ppermute | solution.py:30
  6.0 18.2 %collective-permute-start.1 = (bf16[8,128,128]{2,1,0:T(8,128)(2,1)S(1)}, bf16[8,128,128]{2,1,0:T(8,128)(2,1)S(1)}, u32[]{:S(2)}, u32[]{:S(2)}) collective-permute-start(bf16[8,128,128]{2,1,0:T(8,128)(2,1)S(1)} %get-tuple-element.25), channel_id=1, source_target_pairs={{1,2},{2,1},{3,4},{4,3},{5,6},{6,5},{7,8},{8,7},{9,10},{10,9},{11,... | collective-permute-start | bytes 786440 | tf_op jit(solution)/shard_map/ppermute | solution.py:30
  10.2 16.7 %collective-permute-start.2 = (bf16[8,128,128]{2,1,0:T(8,128)(2,1)S(1)}, bf16[8,128,128]{2,1,0:T(8,128)(2,1)S(1)}, u32[]{:S(2)}, u32[]{:S(2)}) collective-permute-start(bf16[8,128,128]{2,1,0:T(8,128)(2,1)S(1)} %get-tuple-element.26), channel_id=1, source_target_pairs={{0,17},{1,16},{2,19},{3,18},{4,21},{5,20},{6,23},{7,22},{8,25},{9,... | collective-permute-start | bytes 786440 | tf_op jit(solution)/shard_map/ppermute | solution.py:30
  12.1 18.1 %collective-permute-start.3 = (bf16[8,128,128]{2,1,0:T(8,128)(2,1)}, bf16[8,128,128]{2,1,0:T(8,128)(2,1)S(1)}, u32[]{:S(2)}, u32[]{:S(2)}) collective-permute-start(bf16[8,128,128]{2,1,0:T(8,128)(2,1)} %get-tuple-element.27), channel_id=1, source_target_pairs={{1,18},{2,17},{3,20},{4,19},{5,22},{6,21},{7,24},{8,23},{9,26},{10... | collective-permute-start | bytes 786440 | tf_op jit(solution)/shard_map/ppermute | solution.py:30
  14.6 15.6 %collective-permute-start.4 = (bf16[8,128,128]{2,1,0:T(8,128)(2,1)S(1)}, bf16[8,128,128]{2,1,0:T(8,128)(2,1)S(1)}, u32[]{:S(2)}, u32[]{:S(2)}) collective-permute-start(bf16[8,128,128]{2,1,0:T(8,128)(2,1)S(1)} %get-tuple-element.28), channel_id=1, source_target_pairs={{16,33},{17,32},{18,35},{19,34},{20,37},{21,36},{22,39},{23,38},{2... | collective-permute-start | bytes 786440 | tf_op jit(solution)/shard_map/ppermute | solution.py:30
  20.0 12.5 %collective-permute-start.5 = (bf16[8,128,128]{2,1,0:T(8,128)(2,1)S(1)}, bf16[8,128,128]{2,1,0:T(8,128)(2,1)S(1)}, u32[]{:S(2)}, u32[]{:S(2)}) collective-permute-start(bf16[8,128,128]{2,1,0:T(8,128)(2,1)S(1)} %get-tuple-element.29), channel_id=1, source_target_pairs={{17,34},{18,33},{19,36},{20,35},{21,38},{22,37},{23,40},{24,39},{2... | collective-permute-start | bytes 786440 | tf_op jit(solution)/shard_map/ppermute | solution.py:30
  24.3 9.4 %collective-permute-start.6 = (bf16[8,128,128]{2,1,0:T(8,128)(2,1)S(1)}, bf16[8,128,128]{2,1,0:T(8,128)(2,1)S(1)}, u32[]{:S(2)}, u32[]{:S(2)}) collective-permute-start(bf16[8,128,128]{2,1,0:T(8,128)(2,1)S(1)} %get-tuple-element.30), channel_id=1, source_target_pairs={{16,32},{17,33},{18,34},{19,35},{20,36},{21,37},{22,38},{23,39},{2... | collective-permute-start | bytes 786440 | tf_op jit(solution)/shard_map/ppermute | solution.py:30
  26.8 6.9 %collective-permute-start.7 = (bf16[8,128,128]{2,1,0:T(8,128)(2,1)S(1)}, bf16[8,128,128]{2,1,0:T(8,128)(2,1)S(1)}, u32[]{:S(2)}, u32[]{:S(2)}) collective-permute-start(bf16[8,128,128]{2,1,0:T(8,128)(2,1)S(1)} %get-tuple-element.31), channel_id=1, source_target_pairs={{0,16},{1,17},{2,18},{3,19},{4,20},{5,21},{6,22},{7,23},{8,24},{9,... | collective-permute-start | bytes 786440 | tf_op jit(solution)/shard_map/ppermute | solution.py:30
  39.1 31.8 %copy-start.11 = (f32[4,12,256]{2,0,1:T(4,128)S(1)}, f32[4,12,256]{2,0,1:T(4,128)}, u32[]{:S(2)}) copy-start(f32[4,12,256]{2,0,1:T(4,128)} %param.11) | copy-start | bytes 147460
  55.0 59.4 %copy-start.7 = (s32[1,3,3,8]{3,0,2,1:T(1,128)S(1)}, s32[1,3,3,8]{3,0,2,1:T(1,128)}, u32[]{:S(2)}) copy-start(s32[1,3,3,8]{3,0,2,1:T(1,128)} %param.7) | copy-start | bytes 868
  56.0 5.6 %collective-permute-start.8 = (f32[60,256]{1,0:T(8,128)S(1)}, f32[60,256]{1,0:T(8,128)S(1)}, u32[]{:S(2)}, u32[]{:S(2)}) collective-permute-start(f32[60,256]{1,0:T(8,128)S(1)} %get-tuple-element.51), channel_id=1, source_target_pairs={{16,32},{17,33},{18,34},{19,35},{20,36},{21,37},{22,38},{23,39},{2... | collective-permute-start | bytes 184328 | tf_op jit(solution)/shard_map/ppermute | solution.py:30
  58.7 2.9 %collective-permute-start.9 = (f32[60,256]{1,0:T(8,128)S(1)}, f32[60,256]{1,0:T(8,128)S(1)}, u32[]{:S(2)}, u32[]{:S(2)}) collective-permute-start(f32[60,256]{1,0:T(8,128)S(1)} %get-tuple-element.52), channel_id=1, source_target_pairs={{0,16},{1,17},{2,18},{3,19},{4,20},{5,21},{6,22},{7,23},{8,24},{9,... | collective-permute-start | bytes 184328 | tf_op jit(solution)/shard_map/ppermute | solution.py:30
  62.6 6.9 %collective-permute-start.10 = (f32[46,256]{1,0:T(8,128)S(1)}, f32[46,256]{1,0:T(8,128)S(1)}, u32[]{:S(2)}, u32[]{:S(2)}) collective-permute-start(f32[46,256]{1,0:T(8,128)S(1)} %get-tuple-element.55), channel_id=1, source_target_pairs={{1,2},{2,1},{3,4},{4,3},{5,6},{6,5},{7,8},{8,7},{9,10},{10,9},{11,... | collective-permute-start | bytes 141320 | tf_op jit(solution)/shard_map/ppermute | solution.py:30
  65.8 3.8 %collective-permute-start.11 = (f32[46,256]{1,0:T(8,128)S(1)}, f32[46,256]{1,0:T(8,128)S(1)}, u32[]{:S(2)}, u32[]{:S(2)}) collective-permute-start(f32[46,256]{1,0:T(8,128)S(1)} %get-tuple-element.56), channel_id=1, source_target_pairs={{0,1},{1,0},{2,3},{3,2},{4,5},{5,4},{6,7},{7,6},{8,9},{9,8},{10,11... | collective-permute-start | bytes 141320 | tf_op jit(solution)/shard_map/ppermute | solution.py:30
  88.7 12.6 %collective-permute-start.12 = (bf16[8,128,128]{2,1,0:T(8,128)(2,1)S(1)}, bf16[8,128,128]{2,1,0:T(8,128)(2,1)S(1)}, u32[]{:S(2)}, u32[]{:S(2)}) collective-permute-start(bf16[8,128,128]{2,1,0:T(8,128)(2,1)S(1)} %get-tuple-element.35), channel_id=1, source_target_pairs={{0,1},{1,0},{2,3},{3,2},{4,5},{5,4},{6,7},{7,6},{8,9},{9,8},{10,11... | collective-permute-start | bytes 786440 | tf_op jit(solution)/shard_map/ppermute | solution.py:30
  88.8 16.4 %collective-permute-start.13 = (bf16[8,128,128]{2,1,0:T(8,128)(2,1)S(1)}, bf16[8,128,128]{2,1,0:T(8,128)(2,1)S(1)}, u32[]{:S(2)}, u32[]{:S(2)}) collective-permute-start(bf16[8,128,128]{2,1,0:T(8,128)(2,1)S(1)} %get-tuple-element.36), channel_id=1, source_target_pairs={{1,2},{2,1},{3,4},{4,3},{5,6},{6,5},{7,8},{8,7},{9,10},{10,9},{11,... | collective-permute-start | bytes 786440 | tf_op jit(solution)/shard_map/ppermute | solution.py:30
  92.3 14.9 %collective-permute-start.14 = (bf16[8,128,128]{2,1,0:T(8,128)(2,1)S(1)}, bf16[8,128,128]{2,1,0:T(8,128)(2,1)S(1)}, u32[]{:S(2)}, u32[]{:S(2)}) collective-permute-start(bf16[8,128,128]{2,1,0:T(8,128)(2,1)S(1)} %get-tuple-element.37), channel_id=1, source_target_pairs={{0,17},{1,16},{2,19},{3,18},{4,21},{5,20},{6,23},{7,22},{8,25},{9,... | collective-permute-start | bytes 786440 | tf_op jit(solution)/shard_map/ppermute | solution.py:30
  93.7 13.6 %collective-permute-start.15 = (bf16[8,128,128]{2,1,0:T(8,128)(2,1)S(1)}, bf16[8,128,128]{2,1,0:T(8,128)(2,1)S(1)}, u32[]{:S(2)}, u32[]{:S(2)}) collective-permute-start(bf16[8,128,128]{2,1,0:T(8,128)(2,1)S(1)} %get-tuple-element.38), channel_id=1, source_target_pairs={{1,18},{2,17},{3,20},{4,19},{5,22},{6,21},{7,24},{8,23},{9,26},{10... | collective-permute-start | bytes 786440 | tf_op jit(solution)/shard_map/ppermute | solution.py:30
  97.6 10.7 %collective-permute-start.16 = (bf16[8,128,128]{2,1,0:T(8,128)(2,1)S(1)}, bf16[8,128,128]{2,1,0:T(8,128)(2,1)S(1)}, u32[]{:S(2)}, u32[]{:S(2)}) collective-permute-start(bf16[8,128,128]{2,1,0:T(8,128)(2,1)S(1)} %get-tuple-element.39), channel_id=1, source_target_pairs={{16,33},{17,32},{18,35},{19,34},{20,37},{21,36},{22,39},{23,38},{2... | collective-permute-start | bytes 786440 | tf_op jit(solution)/shard_map/ppermute | solution.py:30
  101.3 12.0 %collective-permute-start.17 = (bf16[8,128,128]{2,1,0:T(8,128)(2,1)S(1)}, bf16[8,128,128]{2,1,0:T(8,128)(2,1)S(1)}, u32[]{:S(2)}, u32[]{:S(2)}) collective-permute-start(bf16[8,128,128]{2,1,0:T(8,128)(2,1)S(1)} %get-tuple-element.40), channel_id=1, source_target_pairs={{17,34},{18,33},{19,36},{20,35},{21,38},{22,37},{23,40},{24,39},{2... | collective-permute-start | bytes 786440 | tf_op jit(solution)/shard_map/ppermute | solution.py:30
  105.2 9.3 %collective-permute-start.18 = (bf16[8,128,128]{2,1,0:T(8,128)(2,1)S(1)}, bf16[8,128,128]{2,1,0:T(8,128)(2,1)S(1)}, u32[]{:S(2)}, u32[]{:S(2)}) collective-permute-start(bf16[8,128,128]{2,1,0:T(8,128)(2,1)S(1)} %get-tuple-element.41), channel_id=1, source_target_pairs={{16,32},{17,33},{18,34},{19,35},{20,36},{21,37},{22,38},{23,39},{2... | collective-permute-start | bytes 786440 | tf_op jit(solution)/shard_map/ppermute | solution.py:30
  107.2 7.3 %collective-permute-start.19 = (bf16[8,128,128]{2,1,0:T(8,128)(2,1)S(1)}, bf16[8,128,128]{2,1,0:T(8,128)(2,1)S(1)}, u32[]{:S(2)}, u32[]{:S(2)}) collective-permute-start(bf16[8,128,128]{2,1,0:T(8,128)(2,1)S(1)} %get-tuple-element.42), channel_id=1, source_target_pairs={{0,16},{1,17},{2,18},{3,19},{4,20},{5,21},{6,22},{7,23},{8,24},{9,... | collective-permute-start | bytes 786440 | tf_op jit(solution)/shard_map/ppermute | solution.py:30
  (8 other events, 50.6 us)

commit v3 on v2

v3 whole, which is shorter than its diff:
```python
import functools

import jax
import jax.numpy as jnp
from jax import lax
from jax.experimental import pallas as pl
from jax.experimental.pallas import tpu as pltpu
from jax.sharding import PartitionSpec as P

SWEEPS = 3
CELL_VOLUME = 0.0625

KINDS = ((0, 0), (0, 1), (0, 2), (1, 1), (1, 2), (2, 1), (2, 2), (2, 0), (1, 0))
SENT = (((0, 0),), ((1, 0), (1, 1), (1, 2)), ((2, 0), (2, 1), (2, 2)), ((0, 1),), ((0, 2),))
ARRIVED = (((0, 0),), ((1, 0),), ((2, 0),), ((0, 1), (1, 1)), ((0, 2), (1, 2)), ((2, 1),), ((2, 2),))


def partner(index, kind):
    if kind == 0:
        return index
    return index + 1 if index % 2 == kind - 1 else index - 1


def swap(value, kind, sizes):
    count_x, count_y = sizes
    pairs = []
    for p in range(count_x):
        for q in range(count_y):
            to_p, to_q = partner(p, kind[0]), partner(q, kind[1])
            if 0 <= to_p < count_x and 0 <= to_q < count_y:
                pairs.append((p * count_y + q, to_p * count_y + to_q))
    return lax.ppermute(value, ("gx", "gy"), pairs)


def group_ids():
    p, q = lax.axis_index("gx"), lax.axis_index("gy")

    def side(index, kind):
        if kind == 0:
            return 1
        return jnp.where((index & 1) == kind - 1, 2, 0)

    return [side(p, a) * 3 + side(q, b) for a, b in KINDS]


def call(body, name, megabytes, **options):
    return pl.pallas_call(
        body,
        name=name,
        compiler_params=pltpu.CompilerParams(vmem_limit_bytes=megabytes * 1024 * 1024),
        **options,
    )


SMEM = pl.BlockSpec(memory_space=pltpu.SMEM)
VMEM = pl.BlockSpec(memory_space=pltpu.VMEM)
ANY = pl.BlockSpec(memory_space=pl.ANY)


def gather_body(table, blocks, *outs):
    depth = table.shape[2]
    groups = dict(zip(KINDS, group_ids()))
    for out, kinds in zip(outs, SENT):
        for part, kind in enumerate(kinds):
            for c in range(depth):
                row = jnp.maximum(table[groups[kind], 0, c], 0)
                out[part * depth + c] = blocks[row]


def gather(table, blocks):
    depth, width = table.shape[2], blocks.shape[1]
    return call(
        gather_body,
        "gather",
        12,
        in_specs=[SMEM, VMEM],
        out_specs=[VMEM] * len(SENT),
        out_shape=[
            jax.ShapeDtypeStruct((len(kinds) * depth, width, width), blocks.dtype)
            for kinds in SENT
        ],
    )(table, blocks)


def spread(outgoing, depth, sizes):
    own, to_first, to_second, along_first, along_second = outgoing
    first = swap(to_first, (1, 0), sizes)
    second = swap(to_second, (2, 0), sizes)
    one = swap(jnp.concatenate([along_first, first[depth : 2 * depth]]), (0, 1), sizes)
    two = swap(jnp.concatenate([along_second, first[2 * depth :]]), (0, 2), sizes)
    three = swap(second[depth : 2 * depth], (0, 1), sizes)
    four = swap(second[2 * depth :], (0, 2), sizes)
    return [own, first, second, one, two, three, four]


def transpose_body(basis, after, turned, held, sems):
    brick_x, brick_y, per, _, width = basis.shape
    half = brick_y // 2
    parts = [(x, j) for x in range(brick_x) for j in range(2)]

    def coming(i):
        x, j = parts[i]
        here = pl.ds(j * half, half)
        return pltpu.make_async_copy(basis.at[x, here], held.at[x, here], sems.at[i])

    for i in range(len(parts)):
        coming(i).start()
    for i, (x, j) in enumerate(parts):
        coming(i).wait()
        for y in range(j * half, (j + 1) * half):
            for b in range(per):
                turned[x, y, b * width : (b + 1) * width, :] = held[x, y, b].T


def transposed(basis, after):
    brick_x, brick_y, per, points, width = basis.shape
    return call(
        transpose_body,
        "transpose",
        32,
        in_specs=[ANY, ANY],
        out_specs=VMEM,
        out_shape=pltpu.VMEM((brick_x, brick_y, per * width, points), basis.dtype),
        scratch_shapes=[
            pltpu.VMEM(basis.shape, basis.dtype),
            pltpu.SemaphoreType.DMA((2 * brick_x,)),
        ],
        cost_estimate=pl.CostEstimate(flops=0, bytes_accessed=4 * basis.size, transcendentals=0),
    )(basis, after)


def slot_of(slots, x, y, a, b, empty):
    slot = slots[x, a, b, y]
    return jnp.where(slot < 0, empty, slot)


def density_body(unroll, depth, slots, turned, previous, *rest):
    arrived, (density, to_first, to_second, kept, blocks, sems) = rest[: len(ARRIVED)], rest[len(ARRIVED) :]
    brick_x, brick_y, rows, points = turned.shape
    width = arrived[0].shape[1]
    per = rows // width
    empty = len(KINDS) * depth
    groups = dict(zip(KINDS, group_ids()))
    copies = []
    for message, kinds in zip(arrived, ARRIVED):
        for part, kind in enumerate(kinds):
            copies.append(
                pltpu.make_async_copy(
                    message.at[pl.ds(part * depth, depth)],
                    blocks.at[pl.ds(groups[kind] * depth, depth)],
                    sems.at[len(copies)],
                )
            )
    for copy in copies:
        copy.start()
    blocks[empty] = jnp.zeros((width, width), blocks.dtype)
    for copy in copies:
        copy.wait()

    def one(x, y):
        lefts = [
            jnp.concatenate(
                [blocks[slot_of(slots, x, y, a, b, empty)] for b in range(per)], axis=1
            )
            for a in range(per)
        ]
        right = turned[x, y]
        mixed = jnp.dot(jnp.concatenate(lefts, axis=0), right, preferred_element_type=jnp.float32)
        product = mixed * right.astype(jnp.float32)
        kept[y, pl.ds(x, 1), :] = jnp.sum(product, axis=0, keepdims=True)

    def step(x, carry):
        def some(j, carry):
            for u in range(unroll):
                one(x, j * unroll + u)
            return carry

        return lax.fori_loop(0, brick_y // unroll, some, carry)

    lax.fori_loop(0, brick_x, step, 0)
    density[...] = kept[...]
    even = (lax.axis_index("gx") & 1) == 0
    wide, thin = SWEEPS, SWEEPS - 1
    low = [previous[:, :wide, :], kept[:, :thin, :]]
    high = [previous[:, brick_x - wide :, :], kept[:, brick_x - thin :, :]]
    for out, where_even, where_odd in ((to_first, high, low), (to_second, low, high)):
        out[...] = jnp.zeros_like(out)
        out[:, :wide, :] = jnp.where(even, where_even[0], where_odd[0])
        out[:, wide : wide + thin, :] = jnp.where(even, where_even[1], where_odd[1])


def density_of(slots, turned, previous, arrived, depth, unroll=12):
    brick_x, brick_y, rows, points = turned.shape
    width = arrived[0].shape[1]
    kinds = len(KINDS)
    shape = (brick_y, brick_x, points)
    message = jax.ShapeDtypeStruct((brick_y, 8, points), jnp.float32)
    return call(
        functools.partial(density_body, unroll, depth),
        "density",
        12,
        in_specs=[SMEM, VMEM, VMEM] + [ANY] * len(arrived),
        out_specs=[VMEM] * 4,
        out_shape=[jax.ShapeDtypeStruct(shape, jnp.float32), message, message]
        + [jax.ShapeDtypeStruct(shape, jnp.float32)],
        scratch_shapes=[
            pltpu.VMEM((kinds * depth + 1, width, width), turned.dtype),
            pltpu.SemaphoreType.DMA((kinds,)),
        ],
    )(slots, turned, previous, *arrived)


def sides(axis, first, second):
    even = (lax.axis_index(axis) & 1) == 0
    return jnp.where(even, second, first), jnp.where(even, first, second)


def widen_body(previous, density, first, second, field, charge, to_first, to_second):
    wide, thin = SWEEPS, SWEEPS - 1
    brick_y, brick_x, points = density.shape
    before, after = sides("gx", first[...], second[...])
    field[...] = jnp.zeros_like(field)
    field[:, :wide, :] = before[:, :wide, :]
    field[:, wide : wide + brick_x, :] = previous[...]
    field[:, wide + brick_x : 2 * wide + brick_x, :] = after[:, :wide, :]
    charge[:, :thin, :] = before[:, wide : wide + thin, :]
    charge[:, thin : thin + brick_x, :] = density[...]
    charge[:, thin + brick_x :, :] = after[:, wide : wide + thin, :]
    width = brick_x + 2 * thin
    even = (lax.axis_index("gy") & 1) == 0
    low = [field[:wide, 1 : 1 + width, :], charge[:thin]]
    high = [field[brick_y - wide :, 1 : 1 + width, :], charge[brick_y - thin :]]
    for out, where_even, where_odd in ((to_first, high, low), (to_second, low, high)):
        out[:wide] = jnp.where(even, where_even[0], where_odd[0])
        out[wide:] = jnp.where(even, where_even[1], where_odd[1])


def widen(previous, density, first, second):
    brick_y, brick_x, points = density.shape
    wide, thin = SWEEPS, SWEEPS - 1
    width = brick_x + 2 * thin
    shapes = [(brick_y, 16, points), (brick_y, width, points)] + [(wide + thin, width, points)] * 2
    return call(
        widen_body,
        "widen",
        4,
        in_specs=[VMEM] * 4,
        out_specs=[VMEM] * 4,
        out_shape=[jax.ShapeDtypeStruct(shape, jnp.float32) for shape in shapes],
    )(previous, density, first, second)


def sweeps_in(field_x, charge_x, first, second, sizes, field, charge, steps):
    wide, thin = SWEEPS, SWEEPS - 1
    brick_y, width, points = charge_x.shape
    brick_x = width - 2 * thin
    before, after = sides("gy", first[...], second[...])
    field[...] = jnp.zeros_like(field)
    field[:wide, 1 : 1 + width, :] = before[:wide]
    field[wide : wide + brick_y] = field_x[...]
    field[wide + brick_y :, 1 : 1 + width, :] = after[:wide]
    charge[:thin] = before[wide:]
    charge[thin : thin + brick_y] = charge_x[...]
    charge[thin + brick_y :] = after[wide:]
    p, q = lax.axis_index("gx"), lax.axis_index("gy")
    source = field
    for done in range(1, SWEEPS + 1):
        margin = SWEEPS - done
        rows, columns = brick_y + 2 * margin, brick_x + 2 * margin
        here = source[1 : 1 + rows, 1 : 1 + columns, :]
        z = lax.broadcasted_iota(jnp.int32, here.shape, 2)
        total = source[:rows, 1 : 1 + columns, :] + source[2 : 2 + rows, 1 : 1 + columns, :]
        total += source[1 : 1 + rows, :columns, :] + source[1 : 1 + rows, 2 : 2 + columns, :]
        total += jnp.where(z == 0, 0.0, pltpu.roll(here, 1, 2))
        total += jnp.where(z == points - 1, 0.0, pltpu.roll(here, points - 1, 2))
        skip = thin - margin
        value = (total + charge[skip : skip + rows, skip : skip + columns, :]) / 6.0
        if margin == 0:
            return value
        y = lax.broadcasted_iota(jnp.int32, value.shape, 0) - margin + q * brick_y
        x = lax.broadcasted_iota(jnp.int32, value.shape, 1) - margin + p * brick_x
        known = (x >= 0) & (x < sizes[0] * brick_x) & (y >= 0) & (y < sizes[1] * brick_y)
        source = steps[done - 1]
        source[:, :columns, :] = jnp.where(known, value, 0.0)


def integrals_body(unroll, depth, sizes, slots, turned, external, *rest):
    kinds = len(KINDS)
    wide, rest = rest[:4], rest[4:]
    hartree, outs = rest[0], rest[1 : 1 + kinds]
    potential, sums, field, charge, *steps = rest[1 + kinds :]
    brick_x, brick_y, rows, _ = turned.shape
    width = outs[0].shape[1]
    per = rows // width
    empty = kinds * depth
    sums[...] = jnp.zeros_like(sums)
    swept = sweeps_in(*wide, sizes, field, charge, steps)
    hartree[...] = swept
    potential[...] = swept + external[...]

    def one(x, y):
        left = turned[x, y]
        weighted = (left.astype(jnp.float32) * potential[y, pl.ds(x, 1), :]).astype(turned.dtype)
        product = lax.dot_general(
            left, weighted, (((1,), (1,)), ((), ())), preferred_element_type=jnp.float32
        )
        for a in range(per):
            for b in range(per):
                slot = slot_of(slots, x, y, a, b, empty)
                sums[slot] += product[a * width : (a + 1) * width, b * width : (b + 1) * width]

    def step(x, carry):
        def some(j, carry):
            for u in range(unroll):
                one(x, j * unroll + u)
            return carry

        return lax.fori_loop(0, brick_y // unroll, some, carry)

    lax.fori_loop(0, brick_x, step, 0)
    for group, out in zip(group_ids(), outs):
        part = sums[pl.ds(group * depth, depth)]
        out[...] = (CELL_VOLUME * part).astype(out.dtype)


def integrals_of(slots, turned, external, wide, depth, width, sizes, unroll=6):
    brick_y, brick_x, points = external.shape
    kinds = len(KINDS)
    shape = (depth, width, width)
    return call(
        functools.partial(integrals_body, unroll, depth, sizes),
        "integrals",
        16,
        in_specs=[SMEM] + [VMEM] * 6,
        out_specs=[VMEM] * (1 + kinds),
        out_shape=[jax.ShapeDtypeStruct(external.shape, jnp.float32)]
        + [jax.ShapeDtypeStruct(shape, jnp.float32)]
        + [jax.ShapeDtypeStruct(shape, jnp.bfloat16)] * (kinds - 1),
        scratch_shapes=[
            pltpu.VMEM(external.shape, jnp.float32),
            pltpu.VMEM((kinds * depth + 1, width, width), jnp.float32),
            pltpu.VMEM((brick_y + 2 * SWEEPS, 16, points), jnp.float32),
            pltpu.VMEM((brick_y + 2 * SWEEPS - 2, brick_x + 2 * SWEEPS - 2, points), jnp.float32),
        ]
        + [
            pltpu.VMEM((brick_y + 2 * margin, 8, points), jnp.float32)
            for margin in range(SWEEPS - 1, 0, -1)
        ],
    )(slots, turned, external, *wide)


def collect_body(table, *rest):
    messages, out = rest[:-1], rest[-1]
    depth = table.shape[2]
    out[...] = jnp.zeros_like(out)
    for group, message in zip(group_ids(), messages):
        for c in range(depth):
            row = table[group, 0, c]

            @pl.when(row >= 0)
            def _():
                out[row] += message[c].astype(jnp.float32)


def collect(table, messages, owned):
    width = messages[0].shape[1]
    return call(
        collect_body,
        "collect",
        12,
        in_specs=[SMEM] + [VMEM] * len(messages),
        out_specs=VMEM,
        out_shape=jax.ShapeDtypeStruct((owned, width, width), jnp.float32),
    )(table, *messages)


def per_device(
    sizes, density_blocks, send_table, batch_pairs, basis_values, previous_hartree, external_potential
):
    owned, width, _ = density_blocks.shape
    depth = send_table.shape[3]
    table = send_table.reshape(9, 1, depth)
    slots = batch_pairs.transpose(0, 2, 3, 1)
    previous = previous_hartree.transpose(1, 0, 2)
    external = external_potential.transpose(1, 0, 2)
    arrived = spread(gather(table, density_blocks), depth, sizes)
    turned = transposed(basis_values, arrived[2])
    density, to_first, to_second, kept = density_of(slots, turned, previous, arrived, depth)
    first, second = swap(to_first, (1, 0), sizes), swap(to_second, (2, 0), sizes)
    field, charge, to_first, to_second = widen(previous, kept, first, second)
    first, second = swap(to_first, (0, 1), sizes), swap(to_second, (0, 2), sizes)
    wide = (field, charge, first, second)
    hartree, *partial = integrals_of(slots, turned, external, wide, depth, width, sizes)
    returned = [partial[0]] + [swap(m, kind, sizes) for m, kind in zip(partial[1:], KINDS[1:])]
    potential = collect(table, returned, owned)
    return density.transpose(1, 0, 2), hartree.transpose(1, 0, 2), potential


def solution(mesh):
    sizes = (mesh.shape["gx"], mesh.shape["gy"])
    in_specs = (
        P(("gx", "gy"), None, None),
        P(("gx", "gy"), None, None, None),
        P("gx", "gy", None, None),
        P("gx", "gy", None, None, None),
        P("gx", "gy", None),
        P("gx", "gy", None),
    )
    out_specs = (P("gx", "gy", None), P("gx", "gy", None), P(("gx", "gy"), None, None))
    return jax.shard_map(
        functools.partial(per_device, sizes),
        mesh=mesh,
        in_specs=in_specs,
        out_specs=out_specs,
        check_vma=False,
    )
```

time: 119 us -> 98.3 us (0.83)
  local copies, waits for them, and re-layouts: 21.4 us -> 2.37 us
  other arithmetic: 4.87 us -> 0.1 us
  waiting for transfers between devices: 17.1 us -> 20.5 us
  Pallas kernels: 28.4 us -> 30.9 us
  starting transfers between devices: 45.4 us -> 42.9 us
    unnamed x24 -> x12, local copies, waits for them, and re-layouts: 16.7 us -> 2.3 us
    ppermute x20 -> x18, waiting for transfers between devices: 17.1 us -> 20.5 us  [swap(): return lax.ppermute(value, ('gx', 'gy'), pairs)]
    pallas_call x2 -> x4, Pallas kernels: 23.1 us -> 26.3 us  [the longest x1 11.8 us: integrals_of(): call(functools.partial(integrals_body, unroll, depth, sizes), 'integrals'...]
    ppermute x20 -> x18, starting transfers between devices: 45.4 us -> 42.9 us  [swap(): return lax.ppermute(value, ('gx', 'gy'), pairs)]
    slice x8 -> x2, local copies, waits for them, and re-layouts: 2.43 us -> 0.08 us  [the longest x1 0.04 us: spread(): first[2 * depth:]]
    reshape x13 -> x0, local copies, waits for them, and re-layouts: 2.2 us -> none  [the longest x4 2.07 us: pack(): a.reshape(-1, points)]
    add x1 -> x0, other arithmetic: 1.54 us -> none  [per_device(): field = hartree + external_potential.transpose(1, 0, 2)]
    and x4 -> x0, other arithmetic: 1.34 us -> none  [inside(): (x >= 0) & (x < sizes[0] * brick_x) & (y >= 0) & (y < sizes[1] * brick_y)]
  transfers between devices with their start and end apart: 20 -> 18, of which waited for: 7 -> 7; matrix products, arithmetic and copies ran while one was open for 4% -> 0% of each run, Pallas kernels for 0% -> 5%
where the time goes in v3:
time: 98.3 us; the launch traced here: 97.6 us
  starting transfers between devices  42.9 us (44%)
  Pallas kernels  30.9 us (31%)
  waiting for transfers between devices  20.5 us (21%)
  local copies, waits for them, and re-layouts  2.37 us (2%)
    ppermute x18, starting transfers between devices, swap(): return lax.ppermute(value, ('gx', 'gy'), pairs)  42.9 us
    ppermute x18, waiting for transfers between devices, swap(): return lax.ppermute(value, ('gx', 'gy'), pairs)  20.5 us
    pallas_call x1, Pallas kernels, integrals_of(): call(functools.partial(integrals_body, unroll, depth, sizes), 'integrals'...  11.8 us
    pallas_call x1, Pallas kernels, density_of(): call(functools.partial(density_body, unroll, depth), 'density', 12, in_sp...  9.26 us
    pallas_call x1, Pallas kernels, transposed(): call(transpose_body, 'transpose', 32, in_specs=[ANY, ANY], out_specs=VMEM...  5.2 us
    pallas_call x1, Pallas kernels, collect(): call(collect_body, 'collect', 12, in_specs=[SMEM] + [VMEM] * len(messages...  3.76 us
    unnamed x12, local copies, waits for them, and re-layouts  2.3 us
  transfers between devices with their start and end apart: 18, of which 7 were waited for; matrix products, arithmetic and copies ran while one was open for 0% of the time, Pallas kernels for 5%

profile of v3, /device:TPU:13, one launch (start us, length us, event | category | flops | bytes accessed | tf_op | source)
XLA Modules:
  0.0 97.6 jit_solution(10659697490339480647)
XLA Ops:
  0.6 1.6 %copy-done = bf16[64,128,128]{2,1,0:T(8,128)(2,1)S(1)} copy-done((bf16[64,128,128]{2,1,0:T(8,128)(2,1)S(1)}, bf16[64,128,128]{2,1,0:T(8,128)(2,1)}, u32[]{:S(2)}) %copy-start) | copy-done | bytes 2097176
  2.9 0.8 gather.1
  4.4 3.1 %collective-permute-start = (bf16[24,128,128]{2,1,0:T(8,128)(2,1)S(1)}, bf16[24,128,128]{2,1,0:T(8,128)(2,1)S(1)}, u32[]{:S(2)}, u32[]{:S(2)}) collective-permute-start(bf16[24,128,128]{2,1,0:T(8,128)(2,1)S(1)} %get-tuple-element.26), channel_id=1, source_target_pairs={{16,32},{17,33},{18,34},{19,35},{20,36},{21,37},{22,38},{23,39},{2... | collective-permute-start | bytes 2359304 | tf_op jit(solution)/shard_map/ppermute | solution.py:32
  7.7 1.7 %collective-permute-start.2 = (bf16[16,128,128]{2,1,0:T(8,128)(2,1)S(1)}, bf16[16,128,128]{2,1,0:T(8,128)(2,1)S(1)}, u32[]{:S(2)}, u32[]{:S(2)}) collective-permute-start(bf16[16,128,128]{2,1,0:T(8,128)(2,1)S(1)} %pad_maximum_fusion), channel_id=1, source_target_pairs={{0,1},{1,0},{2,3},{3,2},{4,5},{5,4},{6,7},{7,6},{8,9},{9,8},{10,11... | collective-permute-start | bytes 1572872 | tf_op jit(solution)/shard_map/ppermute | solution.py:32
  9.4 4.1 %collective-permute-start.3 = (bf16[16,128,128]{2,1,0:T(8,128)(2,1)S(1)}, bf16[16,128,128]{2,1,0:T(8,128)(2,1)S(1)}, u32[]{:S(2)}, u32[]{:S(2)}) collective-permute-start(bf16[16,128,128]{2,1,0:T(8,128)(2,1)S(1)} %pad_maximum_fusion.1), channel_id=1, source_target_pairs={{1,2},{2,1},{3,4},{4,3},{5,6},{6,5},{7,8},{8,7},{9,10},{10,9},{11,... | collective-permute-start | bytes 1572872 | tf_op jit(solution)/shard_map/ppermute | solution.py:32
  13.6 4.5 %collective-permute-done.after.rest_2_ = bf16[24,128,128]{2,1,0:T(8,128)(2,1)S(1)} collective-permute-done((bf16[24,128,128]{2,1,0:T(8,128)(2,1)S(1)}, bf16[24,128,128]{2,1,0:T(8,128)(2,1)S(1)}, u32[]{:S(2)}, u32[]{:S(2)}) %collective-permute-start) | collective-permute-done | bytes 786464 | tf_op jit(solution)/shard_map/ppermute | solution.py:32
  18.1 5.6 %collective-permute-start.5 = (bf16[8,128,128]{2,1,0:T(8,128)(2,1)S(1)}, bf16[8,128,128]{2,1,0:T(8,128)(2,1)S(1)}, u32[]{:S(2)}, u32[]{:S(2)}) collective-permute-start(bf16[8,128,128]{2,1,0:T(8,128)(2,1)S(1)} %get-tuple-element.49), channel_id=1, source_target_pairs={{1,2},{2,1},{3,4},{4,3},{5,6},{6,5},{7,8},{8,7},{9,10},{10,9},{11,... | collective-permute-start | bytes 786440 | tf_op jit(solution)/shard_map/ppermute | solution.py:32
  23.8 5.2 %transpose.21.turned = bf16[4,12,512,256]{3,2,1,0:T(8,128)(2,1)S(1)} custom-call(bf16[4,12,4,256,128]{4,3,2,1,0:T(8,128)(2,1)} %basis.1, bf16[24,128,128]{2,1,0:T(8,128)(2,1)S(1)} %collective-permute-done.after.rest_2_), custom_call_target="tpu_custom_call" | custom-call | bytes 25165824 | tf_op jit(solution)/shard_map/transpose/pallas_call | solution.py:117
  29.1 3.8 %collective-permute-done.5.rest_6_ = bf16[8,128,128]{2,1,0:T(8,128)(2,1)S(1)} collective-permute-done((bf16[8,128,128]{2,1,0:T(8,128)(2,1)S(1)}, bf16[8,128,128]{2,1,0:T(8,128)(2,1)S(1)}, u32[]{:S(2)}, u32[]{:S(2)}) %collective-permute-start.5) | collective-permute-done | bytes 262176 | tf_op jit(solution)/shard_map/ppermute | solution.py:32
  33.0 9.3 %density.1 = (f32[12,4,256]{2,1,0:T(4,128)}, f32[12,8,256]{2,1,0:T(8,128)S(1)}, f32[12,8,256]{2,1,0:T(8,128)S(1)}, f32[12,4,256]{2,1,0:T(4,128)S(1)}) custom-call(s32[4,4,4,12]{3,2,1,0:T(4,128)S(1)} %bitcast.8, bf16[4,12,512,256]{3,2,1,0:T(8,128)(2,1)S(1)} %transpose.21.turned, f32[12,4,256]{2,1,0:T(4,128)S(1)} %bitcast.6, ...), custom_call_target="tpu_custom_call" | custom-call | tf_op jit(solution)/shard_map/density/pallas_call | solution.py:198
  42.8 2.8 %collective-permute-start.7 = (f32[12,8,256]{2,1,0:T(8,128)S(1)}, f32[12,8,256]{2,1,0:T(8,128)S(1)}, u32[]{:S(2)}, u32[]{:S(2)}) collective-permute-start(f32[12,8,256]{2,1,0:T(8,128)S(1)} %get-tuple-element.34), channel_id=1, source_target_pairs={{16,32},{17,33},{18,34},{19,35},{20,36},{21,37},{22,38},{23,39},{2... | collective-permute-start | bytes 294920 | tf_op jit(solution)/shard_map/ppermute | solution.py:32
  45.6 3.1 %collective-permute-done.7.second = f32[12,8,256]{2,1,0:T(8,128)S(1)} collective-permute-done((f32[12,8,256]{2,1,0:T(8,128)S(1)}, f32[12,8,256]{2,1,0:T(8,128)S(1)}, u32[]{:S(2)}, u32[]{:S(2)}) %collective-permute-start.7) | collective-permute-done | bytes 98336 | tf_op jit(solution)/shard_map/ppermute | solution.py:32
  48.9 4.1 %collective-permute-start.9 = (f32[5,8,256]{2,1,0:T(8,128)S(1)}, f32[5,8,256]{2,1,0:T(8,128)S(1)}, u32[]{:S(2)}, u32[]{:S(2)}) collective-permute-start(f32[5,8,256]{2,1,0:T(8,128)S(1)} %get-tuple-element.38), channel_id=1, source_target_pairs={{1,2},{2,1},{3,4},{4,3},{5,6},{6,5},{7,8},{8,7},{9,10},{10,9},{11,... | collective-permute-start | bytes 122888 | tf_op jit(solution)/shard_map/ppermute | solution.py:32
  53.0 2.7 %collective-permute-done.9.rest_3_ = f32[5,8,256]{2,1,0:T(8,128)S(1)} collective-permute-done((f32[5,8,256]{2,1,0:T(8,128)S(1)}, f32[5,8,256]{2,1,0:T(8,128)S(1)}, u32[]{:S(2)}, u32[]{:S(2)}) %collective-permute-start.9) | collective-permute-done | bytes 40992 | tf_op jit(solution)/shard_map/ppermute | solution.py:32
  55.7 11.8 %integrals.1 = (f32[12,4,256]{2,1,0:T(4,128)}, f32[8,128,128]{2,1,0:T(8,128)S(1)}, bf16[8,128,128]{2,1,0:T(8,128)(2,1)S(1)}, bf16[8,128,128]{2,1,0:T(8,128)(2,1)...) custom-call(s32[4,4,4,12]{3,2,1,0:T(4,128)S(1)} %bitcast.9, ...), custom_call_target="tpu_custom_call" | custom-call | tf_op jit(solution)/shard_map/integrals/pallas_call | solution.py:330
  67.5 4.1 %collective-permute-start.11 = (bf16[8,128,128]{2,1,0:T(8,128)(2,1)S(1)}, bf16[8,128,128]{2,1,0:T(8,128)(2,1)S(1)}, u32[]{:S(2)}, u32[]{:S(2)}) collective-permute-start(bf16[8,128,128]{2,1,0:T(8,128)(2,1)S(1)} %get-tuple-element.42), channel_id=1, source_target_pairs={{1,2},{2,1},{3,4},{4,3},{5,6},{6,5},{7,8},{8,7},{9,10},{10,9},{11,... | collective-permute-start | bytes 786440 | tf_op jit(solution)/shard_map/ppermute | solution.py:32
  71.7 2.6 %collective-permute-start.12 = (bf16[8,128,128]{2,1,0:T(8,128)(2,1)S(1)}, bf16[8,128,128]{2,1,0:T(8,128)(2,1)S(1)}, u32[]{:S(2)}, u32[]{:S(2)}) collective-permute-start(bf16[8,128,128]{2,1,0:T(8,128)(2,1)S(1)} %get-tuple-element.43), channel_id=1, source_target_pairs={{0,17},{1,16},{2,19},{3,18},{4,21},{5,20},{6,23},{7,22},{8,25},{9,... | collective-permute-start | bytes 786440 | tf_op jit(solution)/shard_map/ppermute | solution.py:32
  74.3 2.1 %collective-permute-start.13 = (bf16[8,128,128]{2,1,0:T(8,128)(2,1)S(1)}, bf16[8,128,128]{2,1,0:T(8,128)(2,1)S(1)}, u32[]{:S(2)}, u32[]{:S(2)}) collective-permute-start(bf16[8,128,128]{2,1,0:T(8,128)(2,1)S(1)} %get-tuple-element.44), channel_id=1, source_target_pairs={{1,18},{2,17},{3,20},{4,19},{5,22},{6,21},{7,24},{8,23},{9,26},{10... | collective-permute-start | bytes 786440 | tf_op jit(solution)/shard_map/ppermute | solution.py:32
  76.4 3.5 %collective-permute-start.14 = (bf16[8,128,128]{2,1,0:T(8,128)(2,1)S(1)}, bf16[8,128,128]{2,1,0:T(8,128)(2,1)S(1)}, u32[]{:S(2)}, u32[]{:S(2)}) collective-permute-start(bf16[8,128,128]{2,1,0:T(8,128)(2,1)S(1)} %get-tuple-element.45), channel_id=1, source_target_pairs={{16,33},{17,32},{18,35},{19,34},{20,37},{21,36},{22,39},{23,38},{2... | collective-permute-start | bytes 786440 | tf_op jit(solution)/shard_map/ppermute | solution.py:32
  79.9 4.7 %collective-permute-start.15 = (bf16[8,128,128]{2,1,0:T(8,128)(2,1)S(1)}, bf16[8,128,128]{2,1,0:T(8,128)(2,1)S(1)}, u32[]{:S(2)}, u32[]{:S(2)}) collective-permute-start(bf16[8,128,128]{2,1,0:T(8,128)(2,1)S(1)} %get-tuple-element.46), channel_id=1, source_target_pairs={{17,34},{18,33},{19,36},{20,35},{21,38},{22,37},{23,40},{24,39},{2... | collective-permute-start | bytes 786440 | tf_op jit(solution)/shard_map/ppermute | solution.py:32
  84.6 2.1 %collective-permute-start.16 = (bf16[8,128,128]{2,1,0:T(8,128)(2,1)S(1)}, bf16[8,128,128]{2,1,0:T(8,128)(2,1)S(1)}, u32[]{:S(2)}, u32[]{:S(2)}) collective-permute-start(bf16[8,128,128]{2,1,0:T(8,128)(2,1)S(1)} %get-tuple-element.47), channel_id=1, source_target_pairs={{16,32},{17,33},{18,34},{19,35},{20,36},{21,37},{22,38},{23,39},{2... | collective-permute-start | bytes 786440 | tf_op jit(solution)/shard_map/ppermute | solution.py:32
  87.7 4.8 %collective-permute-done.15.rest_6_ = bf16[8,128,128]{2,1,0:T(8,128)(2,1)S(1)} collective-permute-done((bf16[8,128,128]{2,1,0:T(8,128)(2,1)S(1)}, bf16[8,128,128]{2,1,0:T(8,128)(2,1)S(1)}, u32[]{:S(2)}, u32[]{:S(2)}) %collective-permute-start.15) | collective-permute-done | bytes 262176 | tf_op jit(solution)/shard_map/ppermute | solution.py:32
  92.4 1.4 %collective-permute-done.16.rest_7_ = bf16[8,128,128]{2,1,0:T(8,128)(2,1)S(1)} collective-permute-done((bf16[8,128,128]{2,1,0:T(8,128)(2,1)S(1)}, bf16[8,128,128]{2,1,0:T(8,128)(2,1)S(1)}, u32[]{:S(2)}, u32[]{:S(2)}) %collective-permute-start.16) | collective-permute-done | bytes 262176 | tf_op jit(solution)/shard_map/ppermute | solution.py:32
  93.8 3.8 %collect.1 = f32[64,128,128]{2,1,0:T(8,128)} custom-call(s32[9,1,8]{2,1,0:T(1,128)S(1)} %bitcast.12, f32[8,128,128]{2,1,0:T(8,128)S(1)} %get-tuple-element.40.rest_0_, bf16[8,128,128]{2,1,0:T(8,128)(2,1)S(1)} %collective-permute-done.10.rest_1_, bf16[8,128,128]{2,1,0:T(8,128)(2,1)S(1)} %collective-permute-done.11.rest_2_, ...), custom_call_target="tpu_custom_call" | custom-call | tf_op jit(solution)/shard_map/collect/pallas_call | solution.py:367
  (34 shorter events, 3.4 us)
Async XLA Ops:
  0.6 1.6 %copy-start = (bf16[64,128,128]{2,1,0:T(8,128)(2,1)S(1)}, bf16[64,128,128]{2,1,0:T(8,128)(2,1)}, u32[]{:S(2)}) copy-start(bf16[64,128,128]{2,1,0:T(8,128)(2,1)} %blocks.1) | copy-start | bytes 6291460
  2.2 0.7 copy-start.4
  3.7 3.9 %collective-permute-start.1 = (bf16[24,128,128]{2,1,0:T(8,128)(2,1)S(1)}, bf16[24,128,128]{2,1,0:T(8,128)(2,1)S(1)}, u32[]{:S(2)}, u32[]{:S(2)}) collective-permute-start(bf16[24,128,128]{2,1,0:T(8,128)(2,1)S(1)} %get-tuple-element.28), channel_id=1, source_target_pairs={{0,16},{1,17},{2,18},{3,19},{4,20},{5,21},{6,22},{7,23},{8,24},{9,... | collective-permute-start | bytes 2359304 | tf_op jit(solution)/shard_map/ppermute | solution.py:32
  4.4 13.6 %collective-permute-start = (bf16[24,128,128]{2,1,0:T(8,128)(2,1)S(1)}, bf16[24,128,128]{2,1,0:T(8,128)(2,1)S(1)}, u32[]{:S(2)}, u32[]{:S(2)}) collective-permute-start(bf16[24,128,128]{2,1,0:T(8,128)(2,1)S(1)} %get-tuple-element.26), channel_id=1, source_target_pairs={{16,32},{17,33},{18,34},{19,35},{20,36},{21,37},{22,38},{23,39},{2... | collective-permute-start | bytes 2359304 | tf_op jit(solution)/shard_map/ppermute | solution.py:32
  7.7 25.2 %collective-permute-start.2 = (bf16[16,128,128]{2,1,0:T(8,128)(2,1)S(1)}, bf16[16,128,128]{2,1,0:T(8,128)(2,1)S(1)}, u32[]{:S(2)}, u32[]{:S(2)}) collective-permute-start(bf16[16,128,128]{2,1,0:T(8,128)(2,1)S(1)} %pad_maximum_fusion), channel_id=1, source_target_pairs={{0,1},{1,0},{2,3},{3,2},{4,5},{5,4},{6,7},{7,6},{8,9},{9,8},{10,11... | collective-permute-start | bytes 1572872 | tf_op jit(solution)/shard_map/ppermute | solution.py:32
  9.4 23.5 %collective-permute-start.3 = (bf16[16,128,128]{2,1,0:T(8,128)(2,1)S(1)}, bf16[16,128,128]{2,1,0:T(8,128)(2,1)S(1)}, u32[]{:S(2)}, u32[]{:S(2)}) collective-permute-start(bf16[16,128,128]{2,1,0:T(8,128)(2,1)S(1)} %pad_maximum_fusion.1), channel_id=1, source_target_pairs={{1,2},{2,1},{3,4},{4,3},{5,6},{6,5},{7,8},{8,7},{9,10},{10,9},{11,... | collective-permute-start | bytes 1572872 | tf_op jit(solution)/shard_map/ppermute | solution.py:32
  18.1 14.8 %collective-permute-start.5 = (bf16[8,128,128]{2,1,0:T(8,128)(2,1)S(1)}, bf16[8,128,128]{2,1,0:T(8,128)(2,1)S(1)}, u32[]{:S(2)}, u32[]{:S(2)}) collective-permute-start(bf16[8,128,128]{2,1,0:T(8,128)(2,1)S(1)} %get-tuple-element.49), channel_id=1, source_target_pairs={{1,2},{2,1},{3,4},{4,3},{5,6},{6,5},{7,8},{8,7},{9,10},{10,9},{11,... | collective-permute-start | bytes 786440 | tf_op jit(solution)/shard_map/ppermute | solution.py:32
  23.7 9.2 %copy-start.1 = (f32[4,12,256]{2,0,1:T(4,128)S(1)}, f32[4,12,256]{2,0,1:T(4,128)}, u32[]{:S(2)}) copy-start(f32[4,12,256]{2,0,1:T(4,128)} %param.10) | copy-start | bytes 147460
  23.7 9.2 %copy-start.2 = (s32[4,12,4,4]{1,3,2,0:T(4,128)S(1)}, s32[4,12,4,4]{1,3,2,0:T(4,128)}, u32[]{:S(2)}) copy-start(s32[4,12,4,4]{1,3,2,0:T(4,128)} %param.8) | copy-start | bytes 9220
  23.7 9.2 %collective-permute-start.4 = (bf16[8,128,128]{2,1,0:T(8,128)(2,1)S(1)}, bf16[8,128,128]{2,1,0:T(8,128)(2,1)S(1)}, u32[]{:S(2)}, u32[]{:S(2)}) collective-permute-start(bf16[8,128,128]{2,1,0:T(8,128)(2,1)S(1)} %get-tuple-element.50), channel_id=1, source_target_pairs={{0,1},{1,0},{2,3},{3,2},{4,5},{5,4},{6,7},{7,6},{8,9},{9,8},{10,11... | collective-permute-start | bytes 786440 | tf_op jit(solution)/shard_map/ppermute | solution.py:32
  29.1 26.7 %copy-start.3 = (f32[4,12,256]{2,0,1:T(4,128)S(1)}, f32[4,12,256]{2,0,1:T(4,128)}, u32[]{:S(2)}) copy-start(f32[4,12,256]{2,0,1:T(4,128)} %param.11) | copy-start | bytes 147460
  32.9 60.9 %copy-start.5 = (s32[1,3,3,8]{3,0,2,1:T(1,128)S(1)}, s32[1,3,3,8]{3,0,2,1:T(1,128)}, u32[]{:S(2)}) copy-start(s32[1,3,3,8]{3,0,2,1:T(1,128)} %param.7) | copy-start | bytes 868
  42.2 3.4 %collective-permute-start.6 = (f32[12,8,256]{2,1,0:T(8,128)S(1)}, f32[12,8,256]{2,1,0:T(8,128)S(1)}, u32[]{:S(2)}, u32[]{:S(2)}) collective-permute-start(f32[12,8,256]{2,1,0:T(8,128)S(1)} %get-tuple-element.33), channel_id=1, source_target_pairs={{0,16},{1,17},{2,18},{3,19},{4,20},{5,21},{6,22},{7,23},{8,24},{9,... | collective-permute-start | bytes 294920 | tf_op jit(solution)/shard_map/ppermute | solution.py:32
  42.8 5.9 %collective-permute-start.7 = (f32[12,8,256]{2,1,0:T(8,128)S(1)}, f32[12,8,256]{2,1,0:T(8,128)S(1)}, u32[]{:S(2)}, u32[]{:S(2)}) collective-permute-start(f32[12,8,256]{2,1,0:T(8,128)S(1)} %get-tuple-element.34), channel_id=1, source_target_pairs={{16,32},{17,33},{18,34},{19,35},{20,36},{21,37},{22,38},{23,39},{2... | collective-permute-start | bytes 294920 | tf_op jit(solution)/shard_map/ppermute | solution.py:32
  48.8 4.2 %collective-permute-start.8 = (f32[5,8,256]{2,1,0:T(8,128)S(1)}, f32[5,8,256]{2,1,0:T(8,128)S(1)}, u32[]{:S(2)}, u32[]{:S(2)}) collective-permute-start(f32[5,8,256]{2,1,0:T(8,128)S(1)} %get-tuple-element.37), channel_id=1, source_target_pairs={{0,1},{1,0},{2,3},{3,2},{4,5},{5,4},{6,7},{7,6},{8,9},{9,8},{10,11... | collective-permute-start | bytes 122888 | tf_op jit(solution)/shard_map/ppermute | solution.py:32
  48.9 6.9 %collective-permute-start.9 = (f32[5,8,256]{2,1,0:T(8,128)S(1)}, f32[5,8,256]{2,1,0:T(8,128)S(1)}, u32[]{:S(2)}, u32[]{:S(2)}) collective-permute-start(f32[5,8,256]{2,1,0:T(8,128)S(1)} %get-tuple-element.38), channel_id=1, source_target_pairs={{1,2},{2,1},{3,4},{4,3},{5,6},{6,5},{7,8},{8,7},{9,10},{10,9},{11,... | collective-permute-start | bytes 122888 | tf_op jit(solution)/shard_map/ppermute | solution.py:32
  67.5 12.3 %collective-permute-start.10 = (bf16[8,128,128]{2,1,0:T(8,128)(2,1)S(1)}, bf16[8,128,128]{2,1,0:T(8,128)(2,1)S(1)}, u32[]{:S(2)}, u32[]{:S(2)}) collective-permute-start(bf16[8,128,128]{2,1,0:T(8,128)(2,1)S(1)} %get-tuple-element.41), channel_id=1, source_target_pairs={{0,1},{1,0},{2,3},{3,2},{4,5},{5,4},{6,7},{7,6},{8,9},{9,8},{10,11... | collective-permute-start | bytes 786440 | tf_op jit(solution)/shard_map/ppermute | solution.py:32
  67.5 17.0 %collective-permute-start.11 = (bf16[8,128,128]{2,1,0:T(8,128)(2,1)S(1)}, bf16[8,128,128]{2,1,0:T(8,128)(2,1)S(1)}, u32[]{:S(2)}, u32[]{:S(2)}) collective-permute-start(bf16[8,128,128]{2,1,0:T(8,128)(2,1)S(1)} %get-tuple-element.42), channel_id=1, source_target_pairs={{1,2},{2,1},{3,4},{4,3},{5,6},{6,5},{7,8},{8,7},{9,10},{10,9},{11,... | collective-permute-start | bytes 786440 | tf_op jit(solution)/shard_map/ppermute | solution.py:32
  71.7 15.1 %collective-permute-start.12 = (bf16[8,128,128]{2,1,0:T(8,128)(2,1)S(1)}, bf16[8,128,128]{2,1,0:T(8,128)(2,1)S(1)}, u32[]{:S(2)}, u32[]{:S(2)}) collective-permute-start(bf16[8,128,128]{2,1,0:T(8,128)(2,1)S(1)} %get-tuple-element.43), channel_id=1, source_target_pairs={{0,17},{1,16},{2,19},{3,18},{4,21},{5,20},{6,23},{7,22},{8,25},{9,... | collective-permute-start | bytes 786440 | tf_op jit(solution)/shard_map/ppermute | solution.py:32
  74.3 13.2 %collective-permute-start.13 = (bf16[8,128,128]{2,1,0:T(8,128)(2,1)S(1)}, bf16[8,128,128]{2,1,0:T(8,128)(2,1)S(1)}, u32[]{:S(2)}, u32[]{:S(2)}) collective-permute-start(bf16[8,128,128]{2,1,0:T(8,128)(2,1)S(1)} %get-tuple-element.44), channel_id=1, source_target_pairs={{1,18},{2,17},{3,20},{4,19},{5,22},{6,21},{7,24},{8,23},{9,26},{10... | collective-permute-start | bytes 786440 | tf_op jit(solution)/shard_map/ppermute | solution.py:32
  76.4 11.3 %collective-permute-start.14 = (bf16[8,128,128]{2,1,0:T(8,128)(2,1)S(1)}, bf16[8,128,128]{2,1,0:T(8,128)(2,1)S(1)}, u32[]{:S(2)}, u32[]{:S(2)}) collective-permute-start(bf16[8,128,128]{2,1,0:T(8,128)(2,1)S(1)} %get-tuple-element.45), channel_id=1, source_target_pairs={{16,33},{17,32},{18,35},{19,34},{20,37},{21,36},{22,39},{23,38},{2... | collective-permute-start | bytes 786440 | tf_op jit(solution)/shard_map/ppermute | solution.py:32
  79.9 12.6 %collective-permute-start.15 = (bf16[8,128,128]{2,1,0:T(8,128)(2,1)S(1)}, bf16[8,128,128]{2,1,0:T(8,128)(2,1)S(1)}, u32[]{:S(2)}, u32[]{:S(2)}) collective-permute-start(bf16[8,128,128]{2,1,0:T(8,128)(2,1)S(1)} %get-tuple-element.46), channel_id=1, source_target_pairs={{17,34},{18,33},{19,36},{20,35},{21,38},{22,37},{23,40},{24,39},{2... | collective-permute-start | bytes 786440 | tf_op jit(solution)/shard_map/ppermute | solution.py:32
  84.6 9.2 %collective-permute-start.16 = (bf16[8,128,128]{2,1,0:T(8,128)(2,1)S(1)}, bf16[8,128,128]{2,1,0:T(8,128)(2,1)S(1)}, u32[]{:S(2)}, u32[]{:S(2)}) collective-permute-start(bf16[8,128,128]{2,1,0:T(8,128)(2,1)S(1)} %get-tuple-element.47), channel_id=1, source_target_pairs={{16,32},{17,33},{18,34},{19,35},{20,36},{21,37},{22,38},{23,39},{2... | collective-permute-start | bytes 786440 | tf_op jit(solution)/shard_map/ppermute | solution.py:32
  86.7 7.1 %collective-permute-start.17 = (bf16[8,128,128]{2,1,0:T(8,128)(2,1)S(1)}, bf16[8,128,128]{2,1,0:T(8,128)(2,1)S(1)}, u32[]{:S(2)}, u32[]{:S(2)}) collective-permute-start(bf16[8,128,128]{2,1,0:T(8,128)(2,1)S(1)} %get-tuple-element.48), channel_id=1, source_target_pairs={{0,16},{1,17},{2,18},{3,19},{4,20},{5,21},{6,22},{7,23},{8,24},{9,... | collective-permute-start | bytes 786440 | tf_op jit(solution)/shard_map/ppermute | solution.py:32

commit v4 on v3

v4 whole, which is shorter than its diff:
```python
import functools

import jax
import jax.numpy as jnp
from jax import lax
from jax.experimental import pallas as pl
from jax.experimental.pallas import tpu as pltpu
from jax.sharding import PartitionSpec as P

SWEEPS = 3
CELL_VOLUME = 0.0625

KINDS = ((0, 0), (0, 1), (0, 2), (1, 1), (1, 2), (2, 1), (2, 2), (2, 0), (1, 0))
SENT = (((0, 0),), ((1, 0), (1, 1), (1, 2)), ((2, 0), (2, 1), (2, 2)), ((0, 1),), ((0, 2),))
ARRIVED = (((0, 0),), ((1, 0),), ((2, 0),), ((0, 1), (1, 1)), ((0, 2), (1, 2)), ((2, 1),), ((2, 2),))


def partner(index, kind):
    if kind == 0:
        return index
    return index + 1 if index % 2 == kind - 1 else index - 1


def swap(value, kind, sizes):
    count_x, count_y = sizes
    pairs = []
    for p in range(count_x):
        for q in range(count_y):
            to_p, to_q = partner(p, kind[0]), partner(q, kind[1])
            if 0 <= to_p < count_x and 0 <= to_q < count_y:
                pairs.append((p * count_y + q, to_p * count_y + to_q))
    return lax.ppermute(value, ("gx", "gy"), pairs)


def group_ids():
    p, q = lax.axis_index("gx"), lax.axis_index("gy")

    def side(index, kind):
        if kind == 0:
            return 1
        return jnp.where((index & 1) == kind - 1, 2, 0)

    return [side(p, a) * 3 + side(q, b) for a, b in KINDS]


def call(body, name, megabytes, **options):
    return pl.pallas_call(
        body,
        name=name,
        compiler_params=pltpu.CompilerParams(vmem_limit_bytes=megabytes * 1024 * 1024),
        **options,
    )


SMEM = pl.BlockSpec(memory_space=pltpu.SMEM)
VMEM = pl.BlockSpec(memory_space=pltpu.VMEM)
ANY = pl.BlockSpec(memory_space=pl.ANY)
HBM = pl.BlockSpec(memory_space=pltpu.HBM)


def gather_body(table_far, blocks_far, *rest):
    outs, (table, blocks, sems) = rest[: len(SENT)], rest[len(SENT) :]
    depth = table.shape[2]
    copies = [
        pltpu.make_async_copy(table_far, table, sems.at[0]),
        pltpu.make_async_copy(blocks_far, blocks, sems.at[1]),
    ]
    for copy in copies:
        copy.start()
    for copy in copies:
        copy.wait()
    groups = dict(zip(KINDS, group_ids()))
    for out, kinds in zip(outs, SENT):
        for part, kind in enumerate(kinds):
            for c in range(depth):
                row = jnp.maximum(table[groups[kind], 0, c], 0)
                out[part * depth + c] = blocks[row]


def gather(table, blocks):
    depth, width = table.shape[2], blocks.shape[1]
    return call(
        gather_body,
        "gather",
        12,
        in_specs=[HBM, HBM],
        out_specs=[VMEM] * len(SENT),
        out_shape=[
            jax.ShapeDtypeStruct((len(kinds) * depth, width, width), blocks.dtype)
            for kinds in SENT
        ],
        scratch_shapes=[
            pltpu.SMEM(table.shape, table.dtype),
            pltpu.VMEM(blocks.shape, blocks.dtype),
            pltpu.SemaphoreType.DMA((2,)),
        ],
    )(table, blocks)


def spread(outgoing, depth, sizes):
    own, to_first, to_second, along_first, along_second = outgoing
    first = swap(to_first, (1, 0), sizes)
    second = swap(to_second, (2, 0), sizes)
    one = swap(jnp.concatenate([along_first, first[depth : 2 * depth]]), (0, 1), sizes)
    two = swap(jnp.concatenate([along_second, first[2 * depth :]]), (0, 2), sizes)
    three = swap(second[depth : 2 * depth], (0, 1), sizes)
    four = swap(second[2 * depth :], (0, 2), sizes)
    return [own, first, second, one, two, three, four]


def transpose_body(basis, after, turned, held, sems):
    brick_x, brick_y, per, _, width = basis.shape
    half = brick_y // 2
    parts = [(x, j) for x in range(brick_x) for j in range(2)]

    def coming(i):
        x, j = parts[i]
        here = pl.ds(j * half, half)
        return pltpu.make_async_copy(basis.at[x, here], held.at[x, here], sems.at[i])

    for i in range(len(parts)):
        coming(i).start()
    for i, (x, j) in enumerate(parts):
        coming(i).wait()
        for y in range(j * half, (j + 1) * half):
            for b in range(per):
                turned[x, y, b * width : (b + 1) * width, :] = held[x, y, b].T


def transposed(basis, after):
    brick_x, brick_y, per, points, width = basis.shape
    return call(
        transpose_body,
        "transpose",
        32,
        in_specs=[ANY, ANY],
        out_specs=VMEM,
        out_shape=pltpu.VMEM((brick_x, brick_y, per * width, points), basis.dtype),
        scratch_shapes=[
            pltpu.VMEM(basis.shape, basis.dtype),
            pltpu.SemaphoreType.DMA((2 * brick_x,)),
        ],
        cost_estimate=pl.CostEstimate(flops=0, bytes_accessed=4 * basis.size, transcendentals=0),
    )(basis, after)


def slot_of(slots, x, y, a, b, empty):
    slot = slots[x, a, b, y]
    return jnp.where(slot < 0, empty, slot)


def message_of(out, previous, density, low):
    brick_y, brick_x, _ = previous.shape
    thin = SWEEPS - 1
    out[:brick_y] = previous[...]
    per = brick_x // thin
    for y in range(brick_y):
        layers = jnp.where(low, density[y, :thin, :], density[y, brick_x - thin :, :])
        out[brick_y + y // per, (y % per) * thin : (y % per + 1) * thin, :] = layers


def density_body(depth, slots, turned, previous, *rest):
    arrived, (to_first, to_second, kept, blocks) = rest[: len(ARRIVED)], rest[len(ARRIVED) :]
    brick_x, brick_y, rows, _ = turned.shape
    width = blocks.shape[1]
    per = rows // width
    empty = len(KINDS) * depth
    groups = dict(zip(KINDS, group_ids()))
    for message, kinds in zip(arrived, ARRIVED):
        for part, kind in enumerate(kinds):
            blocks[pl.ds(groups[kind] * depth, depth)] = message[part * depth : (part + 1) * depth]
    blocks[empty] = jnp.zeros((width, width), blocks.dtype)

    def step(x, carry):
        for y in range(brick_y):
            lefts = [
                jnp.concatenate(
                    [blocks[slot_of(slots, x, y, a, b, empty)] for b in range(per)], axis=1
                )
                for a in range(per)
            ]
            right = turned[x, y]
            mixed = jnp.dot(
                jnp.concatenate(lefts, axis=0), right, preferred_element_type=jnp.float32
            )
            product = mixed * right.astype(jnp.float32)
            kept[y, pl.ds(x, 1), :] = jnp.sum(product, axis=0, keepdims=True)
        return carry

    lax.fori_loop(0, brick_x, step, 0)
    odd = (lax.axis_index("gx") & 1) == 1
    message_of(to_first, previous, kept, odd)
    message_of(to_second, previous, kept, jnp.logical_not(odd))


def density_of(slots, turned, previous, arrived, depth):
    brick_x, brick_y, rows, points = turned.shape
    width = arrived[0].shape[1]
    thin = SWEEPS - 1
    shape = (brick_y, brick_x, points)
    message = jax.ShapeDtypeStruct((brick_y + brick_y * thin // brick_x, brick_x, points), jnp.float32)
    return call(
        functools.partial(density_body, depth),
        "density",
        12,
        in_specs=[SMEM] + [VMEM] * (2 + len(arrived)),
        out_specs=[VMEM] * 3,
        out_shape=[message, message, pltpu.VMEM(shape, jnp.float32)],
        scratch_shapes=[pltpu.VMEM((len(KINDS) * depth + 1, width, width), turned.dtype)],
    )(slots, turned, previous, *arrived)


def copied_body(kept, density, sums):
    density[...] = kept[...]
    sums[...] = jnp.zeros_like(sums)


def copied(kept, shape):
    return call(
        copied_body,
        "copied",
        4,
        in_specs=[VMEM],
        out_specs=[VMEM] * 2,
        out_shape=[jax.ShapeDtypeStruct(kept.shape, kept.dtype), pltpu.VMEM(shape, jnp.float32)],
    )(kept)


def cost(flops):
    return pl.CostEstimate(flops=flops, bytes_accessed=0, transcendentals=0)


def sides(axis, first, second):
    even = (lax.axis_index(axis) & 1) == 0
    return jnp.where(even, second, first), jnp.where(even, first, second)


def widen_body(previous, density, first, second, field, charge, to_first, to_second):
    wide, thin = SWEEPS, SWEEPS - 1
    brick_y, brick_x, points = density.shape
    per = brick_x // thin
    before, after = sides("gx", first[...], second[...])
    field[...] = jnp.zeros_like(field)
    field[:, :wide, :] = before[:brick_y, brick_x - wide :, :]
    field[:, wide : wide + brick_x, :] = previous[...]
    field[:, wide + brick_x : 2 * wide + brick_x, :] = after[:brick_y, :wide, :]
    charge[:, thin : thin + brick_x, :] = density[...]
    for y in range(brick_y):
        row, start = brick_y + y // per, (y % per) * thin
        charge[y, :thin, :] = before[row, start : start + thin, :]
        charge[y, thin + brick_x :, :] = after[row, start : start + thin, :]
    width = brick_x + 2 * thin
    even = (lax.axis_index("gy") & 1) == 0
    low = [field[:wide, 1 : 1 + width, :], charge[:thin]]
    high = [field[brick_y - wide :, 1 : 1 + width, :], charge[brick_y - thin :]]
    for out, where_even, where_odd in ((to_first, high, low), (to_second, low, high)):
        out[:wide] = jnp.where(even, where_even[0], where_odd[0])
        out[wide:] = jnp.where(even, where_even[1], where_odd[1])


def widen(previous, density, first, second):
    brick_y, brick_x, points = density.shape
    wide, thin = SWEEPS, SWEEPS - 1
    width = brick_x + 2 * thin
    shapes = [(brick_y, 16, points), (brick_y, width, points)] + [(wide + thin, width, points)] * 2
    return call(
        widen_body,
        "widen",
        4,
        in_specs=[VMEM] * 4,
        out_specs=[VMEM] * 4,
        out_shape=[jax.ShapeDtypeStruct(shape, jnp.float32) for shape in shapes],
    )(previous, density, first, second)


def sweeps_in(field, field_y, charge, charge_y, first, last, brick_y, sizes, steps):
    points = field.shape[2]
    brick_x = charge.shape[1] - 2 * (SWEEPS - 1)
    p, q = lax.axis_index("gx"), lax.axis_index("gy")
    source, source_y = field, field_y
    for done in range(1, SWEEPS + 1):
        margin = SWEEPS - done
        start, stop = first - margin, last + margin
        rows, columns = stop - start, brick_x + 2 * margin
        row, skip = start - source_y, SWEEPS - 1 - margin
        here = source[row : row + rows, 1 : 1 + columns, :]
        z = lax.broadcasted_iota(jnp.int32, here.shape, 2)
        total = source[row - 1 : row - 1 + rows, 1 : 1 + columns, :]
        total += source[row + 1 : row + 1 + rows, 1 : 1 + columns, :]
        total += source[row : row + rows, :columns, :]
        total += source[row : row + rows, 2 : 2 + columns, :]
        total += jnp.where(z == 0, 0.0, pltpu.roll(here, 1, 2))
        total += jnp.where(z == points - 1, 0.0, pltpu.roll(here, points - 1, 2))
        row = start - charge_y
        value = (total + charge[row : row + rows, skip : skip + columns, :]) * (1.0 / 6.0)
        if margin == 0:
            return value
        source, source_y = steps[done - 1], start
        source[:rows, :columns, :] = value

        def clear(condition, rows_out, columns_out):
            @pl.when(condition)
            def _():
                part = source[rows_out, columns_out, :]
                source[rows_out, columns_out, :] = jnp.zeros_like(part)

        clear(p == 0, slice(0, rows), slice(0, margin))
        clear(p == sizes[0] - 1, slice(0, rows), slice(margin + brick_x, columns))
        if start < 0:
            clear(q == 0, slice(0, -start), slice(0, columns))
        if stop > brick_y:
            clear(q == sizes[1] - 1, slice(brick_y - start, rows), slice(0, columns))


def lengthen(field_x, charge_x, first, second, field, charge):
    wide, thin = SWEEPS, SWEEPS - 1
    brick_y, width, _ = charge_x.shape
    before, after = sides("gy", first[...], second[...])
    field[:wide, 1 : 1 + width, :] = before[:wide]
    field[wide : wide + brick_y] = field_x[...]
    field[wide + brick_y :, 1 : 1 + width, :] = after[:wide]
    charge[:thin] = before[wide:]
    charge[thin : thin + brick_y] = charge_x[...]
    charge[thin + brick_y :] = after[wide:]


def add_integrals(slots, turned, potential, sums, columns):
    width = sums.shape[1]
    per = turned.shape[2] // width
    empty = sums.shape[0] - 1

    def step(i, carry):
        for x, y in [(2 * i + j, y) for j in range(2) for y in columns]:
            left = turned[x, y]
            weighted = left.astype(jnp.float32) * potential[y, pl.ds(x, 1), :]
            product = lax.dot_general(
                left,
                weighted.astype(turned.dtype),
                (((1,), (1,)), ((), ())),
                preferred_element_type=jnp.float32,
            )
            for a in range(per):
                for b in range(per):
                    slot = slot_of(slots, x, y, a, b, empty)
                    sums[slot] += product[a * width : (a + 1) * width, b * width : (b + 1) * width]
        return carry

    lax.fori_loop(0, turned.shape[0] // 2, step, 0)


def inner_body(sizes, slots, turned, external, field_x, charge_x, _, sums, potential, *steps):
    brick_y = external.shape[0]
    first, last = SWEEPS, brick_y - SWEEPS
    swept = sweeps_in(field_x, 0, charge_x, 0, first, last, brick_y, sizes, steps)
    potential[first:last] = swept + external[first:last]
    add_integrals(slots, turned, potential, sums, range(first, last))


def outer_body(depth, sizes, slots, turned, external, *rest):
    kinds = len(KINDS)
    wide, rest = rest[:4], rest[5:]
    hartree, sums, outs = rest[0], rest[1], rest[2 : 2 + kinds]
    potential, *steps = rest[2 + kinds : 2 + kinds + SWEEPS]
    field, charge, swept, sem = rest[2 + kinds + SWEEPS :]
    brick_y = external.shape[0]
    field[...] = jnp.zeros_like(field)
    lengthen(*wide, field, charge)
    swept[...] = sweeps_in(field, -SWEEPS, charge, 1 - SWEEPS, 0, brick_y, brick_y, sizes, steps)
    copy = pltpu.make_async_copy(swept, hartree, sem)
    copy.start()
    potential[...] = swept[...] + external[...]
    columns = [*range(SWEEPS), *range(brick_y - SWEEPS, brick_y)]
    add_integrals(slots, turned, potential, sums, columns)
    for group, out in zip(group_ids(), outs):
        part = sums[pl.ds(group * depth, depth)]
        out[...] = (CELL_VOLUME * part).astype(out.dtype)
    copy.wait()


def sweep_scratch(brick_y, brick_x, points):
    return [pltpu.VMEM((brick_y, brick_x, points), jnp.float32)] + [
        pltpu.VMEM((brick_y + 2 * margin, 8, points), jnp.float32)
        for margin in range(SWEEPS - 1, 0, -1)
    ]


def integrals_inner(slots, turned, external, field, charge, sums, sizes):
    return call(
        functools.partial(inner_body, sizes),
        "integrals_inner",
        8,
        in_specs=[SMEM] + [VMEM] * 5,
        out_specs=VMEM,
        out_shape=pltpu.VMEM(sums.shape, sums.dtype),
        input_output_aliases={5: 0},
        scratch_shapes=sweep_scratch(*external.shape),
        cost_estimate=cost(turned.size * turned.shape[2]),
    )(slots, turned, external, field, charge, sums)


def integrals_outer(slots, turned, external, wide, sums, depth, sizes):
    kinds = len(KINDS)
    shape = (depth,) + sums.shape[1:]
    brick_y, brick_x, points = external.shape
    return call(
        functools.partial(outer_body, depth, sizes),
        "integrals_outer",
        12,
        in_specs=[SMEM] + [VMEM] * 7,
        out_specs=[ANY] + [VMEM] * (1 + kinds),
        out_shape=[
            jax.ShapeDtypeStruct(external.shape, jnp.float32),
            pltpu.VMEM(sums.shape, sums.dtype),
            jax.ShapeDtypeStruct(shape, jnp.float32),
        ]
        + [jax.ShapeDtypeStruct(shape, jnp.bfloat16)] * (kinds - 1),
        input_output_aliases={7: 1},
        scratch_shapes=sweep_scratch(*external.shape)
        + [
            pltpu.VMEM((brick_y + 2 * SWEEPS, 16, points), jnp.float32),
            pltpu.VMEM((brick_y + 2 * SWEEPS - 2, brick_x + 2 * SWEEPS - 2, points), jnp.float32),
            pltpu.VMEM(external.shape, jnp.float32),
            pltpu.SemaphoreType.DMA,
        ],
        cost_estimate=cost(turned.size * turned.shape[2]),
    )(slots, turned, external, *wide, sums)


def add_blocks(table, messages, kinds, out):
    depth = table.shape[2]
    groups = dict(zip(KINDS, group_ids()))
    for message, kind in zip(messages, kinds):
        for c in range(depth):
            row = table[groups[kind], 0, c]

            @pl.when(row >= 0)
            def _():
                out[row] += message[c].astype(jnp.float32)


def early_body(kinds, table, *rest):
    messages, (total, out, sem) = rest[: len(kinds)], rest[len(kinds) :]
    total[...] = jnp.zeros_like(total)
    add_blocks(table, messages, kinds, total)
    copy = pltpu.make_async_copy(total, out, sem)
    copy.start()
    copy.wait()


def late_body(kinds, table, *rest):
    messages, (_, _, total, out, sems) = rest[: len(kinds)], rest[len(kinds) :]
    add_blocks(table, messages, kinds, total)
    depth = table.shape[2]
    groups = dict(zip(KINDS, group_ids()))
    rows = [table[groups[kind], 0, c] for kind in kinds for c in range(depth)]

    def renewed(i):
        return pltpu.make_async_copy(total.at[rows[i]], out.at[rows[i]], sems.at[i])

    for i, row in enumerate(rows):

        @pl.when(row >= 0)
        def _():
            renewed(i).start()

    for i, row in enumerate(rows):

        @pl.when(row >= 0)
        def _():
            renewed(i).wait()


def collect(table, messages, owned, late=4):
    depth, width, _ = messages[0].shape
    shape = (owned, width, width)
    outs = [pltpu.VMEM(shape, jnp.float32), jax.ShapeDtypeStruct(shape, jnp.float32)]
    early = len(messages) - late
    total, out = call(
        functools.partial(early_body, KINDS[:early]),
        "collect_early",
        4,
        in_specs=[SMEM] + [VMEM] * early,
        out_specs=[VMEM, ANY],
        out_shape=outs,
        scratch_shapes=[pltpu.SemaphoreType.DMA],
        cost_estimate=cost(10**9),
    )(table, *messages[:early])
    return call(
        functools.partial(late_body, KINDS[early:]),
        "collect_late",
        4,
        in_specs=[SMEM] + [VMEM] * (late + 1) + [ANY],
        out_specs=[VMEM, ANY],
        out_shape=outs,
        input_output_aliases={late + 1: 0, late + 2: 1},
        scratch_shapes=[pltpu.SemaphoreType.DMA((late * depth,))],
    )(table, *messages[early:], total, out)[1]


def per_device(
    sizes, density_blocks, send_table, batch_pairs, basis_values, previous_hartree, external_potential
):
    owned, width, _ = density_blocks.shape
    depth = send_table.shape[3]
    table = send_table.reshape(9, 1, depth)
    slots = batch_pairs.transpose(0, 2, 3, 1)
    previous = previous_hartree.transpose(1, 0, 2)
    external = external_potential.transpose(1, 0, 2)
    table_far = pltpu.with_memory_space_constraint(table, pltpu.HBM)
    blocks_far = pltpu.with_memory_space_constraint(density_blocks, pltpu.HBM)
    arrived = spread(gather(table_far, blocks_far), depth, sizes)
    turned = transposed(basis_values, arrived[2])
    to_first, to_second, kept = density_of(slots, turned, previous, arrived, depth)
    second, first = swap(to_second, (2, 0), sizes), swap(to_first, (1, 0), sizes)
    density, sums = copied(kept, (len(KINDS) * depth + 1, width, width))
    field, charge, to_first, to_second = widen(previous, kept, first, second)
    first, second = swap(to_first, (0, 1), sizes), swap(to_second, (0, 2), sizes)
    sums = integrals_inner(slots, turned, external, field, charge, sums, sizes)
    wide = (field, charge, first, second)
    hartree, _, *partial = integrals_outer(slots, turned, external, wide, sums, depth, sizes)
    returned = [partial[0]] + [swap(m, kind, sizes) for m, kind in zip(partial[1:], KINDS[1:])]
    potential = collect(table, returned, owned)
    return density.transpose(1, 0, 2), hartree.transpose(1, 0, 2), potential


def solution(mesh):
    sizes = (mesh.shape["gx"], mesh.shape["gy"])
    in_specs = (
        P(("gx", "gy"), None, None),
        P(("gx", "gy"), None, None, None),
        P("gx", "gy", None, None),
        P("gx", "gy", None, None, None),
        P("gx", "gy", None),
        P("gx", "gy", None),
    )
    out_specs = (P("gx", "gy", None), P("gx", "gy", None), P(("gx", "gy"), None, None))
    return jax.shard_map(
        functools.partial(per_device, sizes),
        mesh=mesh,
        in_specs=in_specs,
        out_specs=out_specs,
        check_vma=False,
    )
```

time: 98.3 us -> 91.4 us (0.930)
  waiting for transfers between devices: 20.5 us -> 13.8 us
  Pallas kernels: 30.9 us -> 34.1 us
  local copies, waits for them, and re-layouts: 2.37 us -> 0.1 us
  starting transfers between devices: 42.9 us -> 41.2 us
    ppermute x18, waiting for transfers between devices: 20.5 us -> 13.8 us  [swap(): return lax.ppermute(value, ('gx', 'gy'), pairs)]
    pallas_call x4 -> x7, Pallas kernels: 25.6 us -> 28.9 us  [the longest x1 8.52 us: density_of(): call(functools.partial(density_body, depth), 'density', 12, in_specs=[SME...]
    unnamed x12 -> x8, local copies, waits for them, and re-layouts: 2.3 us -> 0.03 us
    ppermute x18, starting transfers between devices: 42.9 us -> 41.2 us  [swap(): return lax.ppermute(value, ('gx', 'gy'), pairs)]
  transfers between devices with their start and end apart: 18 -> 18, of which waited for: 7 -> 6; matrix products, arithmetic and copies ran while one was open for 0% -> 0% of each run, Pallas kernels for 5% -> 17%
where the time goes in v4:
time: 91.4 us; the launch traced here: 90.4 us
  starting transfers between devices  41.2 us (45%)
  Pallas kernels  34.1 us (37%)
  waiting for transfers between devices  13.8 us (15%)
  between operations  1.09 us (1%)
    ppermute x18, starting transfers between devices, swap(): return lax.ppermute(value, ('gx', 'gy'), pairs)  41.2 us
    ppermute x18, waiting for transfers between devices, swap(): return lax.ppermute(value, ('gx', 'gy'), pairs)  13.8 us
    pallas_call x1, Pallas kernels, density_of(): call(functools.partial(density_body, depth), 'density', 12, in_specs=[SME...  8.52 us
    pallas_call x1, Pallas kernels, integrals_outer(): call(functools.partial(outer_body, depth, sizes), 'integrals_outer', 12,...  6.16 us
    pallas_call x1, Pallas kernels, integrals_inner(): call(functools.partial(inner_body, sizes), 'integrals_inner', 8, in_specs...  5.54 us
    pallas_call x1, Pallas kernels, transposed(): call(transpose_body, 'transpose', 32, in_specs=[ANY, ANY], out_specs=VMEM...  5.2 us
    pallas_call x1, Pallas kernels, collect(): call(functools.partial(early_body, KINDS[:early]), 'collect_early', 4, in...  3.38 us
    pallas_call x1, Pallas kernels, collect(): call(functools.partial(late_body, KINDS[early:]), 'collect_late', 4, in_s...  2.56 us
  transfers between devices with their start and end apart: 18, of which 6 were waited for; matrix products, arithmetic and copies ran while one was open for 0% of the time, Pallas kernels for 17%

profile of v4, /device:TPU:13, one launch (start us, length us, event | category | flops | bytes accessed | tf_op | source)
XLA Modules:
  0.0 90.4 jit_solution(5904644402169401234)
XLA Ops:
  0.6 1.8 %gather.1 = (bf16[8,128,128]{2,1,0:T(8,128)(2,1)S(1)}, bf16[24,128,128]{2,1,0:T(8,128)(2,1)S(1)}, bf16[24,128,128]{2,1,0:T(8,128)(2,1)S(1)}, bf16[8,128,128]{2,1,0:T(8,128)(2,1)S(1)}, bf16[8,128,128]{2,1,0:T(8,128)(2,1)S(1)}) custom-call(s32[9,1,8]{2,1,0:T(1,128)} %bitcast.13, bf16[64,128,128]{2,1,0:T(8,128)(2,1)} %blocks_far.1), custom_call_target="tpu_custom_call" | custom-call | tf_op jit(solution)/shard_map/gather/pallas_call | solution.py:82
  3.2 3.1 %collective-permute-start = (bf16[24,128,128]{2,1,0:T(8,128)(2,1)S(1)}, bf16[24,128,128]{2,1,0:T(8,128)(2,1)S(1)}, u32[]{:S(2)}, u32[]{:S(2)}) collective-permute-start(bf16[24,128,128]{2,1,0:T(8,128)(2,1)S(1)} %get-tuple-element.30), channel_id=1, source_target_pairs={{16,32},{17,33},{18,34},{19,35},{20,36},{21,37},{22,38},{23,39},{2... | collective-permute-start | bytes 2359304 | tf_op jit(solution)/shard_map/ppermute | solution.py:32
  6.4 1.7 %collective-permute-start.2 = (bf16[16,128,128]{2,1,0:T(8,128)(2,1)S(1)}, bf16[16,128,128]{2,1,0:T(8,128)(2,1)S(1)}, u32[]{:S(2)}, u32[]{:S(2)}) collective-permute-start(bf16[16,128,128]{2,1,0:T(8,128)(2,1)S(1)} %pad_maximum_fusion), channel_id=1, source_target_pairs={{0,1},{1,0},{2,3},{3,2},{4,5},{5,4},{6,7},{7,6},{8,9},{9,8},{10,11... | collective-permute-start | bytes 1572872 | tf_op jit(solution)/shard_map/ppermute | solution.py:32
  8.2 4.1 %collective-permute-start.3 = (bf16[16,128,128]{2,1,0:T(8,128)(2,1)S(1)}, bf16[16,128,128]{2,1,0:T(8,128)(2,1)S(1)}, u32[]{:S(2)}, u32[]{:S(2)}) collective-permute-start(bf16[16,128,128]{2,1,0:T(8,128)(2,1)S(1)} %pad_maximum_fusion.1), channel_id=1, source_target_pairs={{1,2},{2,1},{3,4},{4,3},{5,6},{6,5},{7,8},{8,7},{9,10},{10,9},{11,... | collective-permute-start | bytes 1572872 | tf_op jit(solution)/shard_map/ppermute | solution.py:32
  12.3 4.5 %collective-permute-done.after.rest_2_ = bf16[24,128,128]{2,1,0:T(8,128)(2,1)S(1)} collective-permute-done((bf16[24,128,128]{2,1,0:T(8,128)(2,1)S(1)}, bf16[24,128,128]{2,1,0:T(8,128)(2,1)S(1)}, u32[]{:S(2)}, u32[]{:S(2)}) %collective-permute-start) | collective-permute-done | bytes 786464 | tf_op jit(solution)/shard_map/ppermute | solution.py:32
  16.8 5.6 %collective-permute-start.5 = (bf16[8,128,128]{2,1,0:T(8,128)(2,1)S(1)}, bf16[8,128,128]{2,1,0:T(8,128)(2,1)S(1)}, u32[]{:S(2)}, u32[]{:S(2)}) collective-permute-start(bf16[8,128,128]{2,1,0:T(8,128)(2,1)S(1)} %get-tuple-element.57), channel_id=1, source_target_pairs={{1,2},{2,1},{3,4},{4,3},{5,6},{6,5},{7,8},{8,7},{9,10},{10,9},{11,... | collective-permute-start | bytes 786440 | tf_op jit(solution)/shard_map/ppermute | solution.py:32
  22.6 5.2 %transpose.21.turned = bf16[4,12,512,256]{3,2,1,0:T(8,128)(2,1)S(1)} custom-call(bf16[4,12,4,256,128]{4,3,2,1,0:T(8,128)(2,1)} %basis.1, bf16[24,128,128]{2,1,0:T(8,128)(2,1)S(1)} %collective-permute-done.after.rest_2_), custom_call_target="tpu_custom_call" | custom-call | bytes 25165824 | tf_op jit(solution)/shard_map/transpose/pallas_call | solution.py:132
  27.8 3.9 %collective-permute-done.5.rest_6_ = bf16[8,128,128]{2,1,0:T(8,128)(2,1)S(1)} collective-permute-done((bf16[8,128,128]{2,1,0:T(8,128)(2,1)S(1)}, bf16[8,128,128]{2,1,0:T(8,128)(2,1)S(1)}, u32[]{:S(2)}, u32[]{:S(2)}) %collective-permute-start.5) | collective-permute-done | bytes 262176 | tf_op jit(solution)/shard_map/ppermute | solution.py:32
  31.7 8.5 %density.1 = (f32[18,4,256]{2,1,0:T(4,128)S(1)}, f32[18,4,256]{2,1,0:T(4,128)S(1)}, f32[12,4,256]{2,1,0:T(4,128)S(1)}) custom-call(s32[4,4,4,12]{3,2,1,0:T(4,128)S(1)} %bitcast.6, bf16[4,12,512,256]{3,2,1,0:T(8,128)(2,1)S(1)} %transpose.21.turned, f32[12,4,256]{2,1,0:T(4,128)S(1)} %bitcast.9, bf16[8,128,128]{2,1,0:T(8,128)(2,1)S(1)} %get-tuple-element.31.rest_0_, ...), custom_call_target="tpu_custom_call" | custom-call | tf_op jit(solution)/shard_map/density/pallas_call | solution.py:202
  40.8 2.8 %collective-permute-start.7 = (f32[18,4,256]{2,1,0:T(4,128)S(1)}, f32[18,4,256]{2,1,0:T(4,128)S(1)}, u32[]{:S(2)}, u32[]{:S(2)}) collective-permute-start(f32[18,4,256]{2,1,0:T(4,128)S(1)} %get-tuple-element.38), channel_id=1, source_target_pairs={{16,32},{17,33},{18,34},{19,35},{20,36},{21,37},{22,38},{23,39},{2... | collective-permute-start | bytes 221192 | tf_op jit(solution)/shard_map/ppermute | solution.py:32
  44.5 1.9 %collective-permute-done.7.second = f32[18,4,256]{2,1,0:T(4,128)S(1)} collective-permute-done((f32[18,4,256]{2,1,0:T(4,128)S(1)}, f32[18,4,256]{2,1,0:T(4,128)S(1)}, u32[]{:S(2)}, u32[]{:S(2)}) %collective-permute-start.7) | collective-permute-done | bytes 73760 | tf_op jit(solution)/shard_map/ppermute | solution.py:32
  46.6 4.1 %collective-permute-start.9 = (f32[5,8,256]{2,1,0:T(8,128)S(1)}, f32[5,8,256]{2,1,0:T(8,128)S(1)}, u32[]{:S(2)}, u32[]{:S(2)}) collective-permute-start(f32[5,8,256]{2,1,0:T(8,128)S(1)} %get-tuple-element.42), channel_id=1, source_target_pairs={{1,2},{2,1},{3,4},{4,3},{5,6},{6,5},{7,8},{8,7},{9,10},{10,9},{11,... | collective-permute-start | bytes 122888 | tf_op jit(solution)/shard_map/ppermute | solution.py:32
  50.7 5.5 %integrals_inner.1.rest_4_ = f32[73,128,128]{2,1,0:T(8,128)S(1)} custom-call(s32[4,4,4,12]{3,2,1,0:T(4,128)S(1)} %bitcast.7, bf16[4,12,512,256]{3,2,1,0:T(8,128)(2,1)S(1)} %transpose.21.turned, f32[12,4,256]{2,1,0:T(4,128)S(1)} %bitcast.11, f32[12,16,256]{2,1,0:T(8,128)S(1)} %get-tuple-element.39.field_x.rest_0_, ...), custom_call_target="tpu_custom_call", output_to_operand_aliasing={{}: (5, {})} | custom-call | flops 3221225472 | tf_op jit(solution)/shard_map/integrals_inner/pallas_call | solution.py:388
  56.3 6.2 %integrals_outer.1 = (f32[12,4,256]{2,1,0:T(4,128)}, f32[73,128,128]{2,1,0:T(8,128)S(1)}, f32[8,128,128]{2,1,0:T(8,128)S(1)}, bf16[8,128,128]{2,1,0:T(8,128)(2,1...) custom-call(s32[4,4,4,12]{3,2,1,0:T(4,128)S(1)} %bitcast.8, ...), custom_call_target="tpu_custom_call", output_to_operand_aliasing={{1}: (7, {})} | custom-call | flops 3221225472 | tf_op jit(solution)/shard_map/integrals_outer/pallas_call | solution.py:405
  63.4 2.5 %collective-permute-start.15 = (bf16[8,128,128]{2,1,0:T(8,128)(2,1)S(1)}, bf16[8,128,128]{2,1,0:T(8,128)(2,1)S(1)}, u32[]{:S(2)}, u32[]{:S(2)}) collective-permute-start(bf16[8,128,128]{2,1,0:T(8,128)(2,1)S(1)} %get-tuple-element.51), channel_id=1, source_target_pairs={{1,2},{2,1},{3,4},{4,3},{5,6},{6,5},{7,8},{8,7},{9,10},{10,9},{11,... | collective-permute-start | bytes 786440 | tf_op jit(solution)/shard_map/ppermute | solution.py:32
  65.9 1.4 %collective-permute-start.16 = (bf16[8,128,128]{2,1,0:T(8,128)(2,1)S(1)}, bf16[8,128,128]{2,1,0:T(8,128)(2,1)S(1)}, u32[]{:S(2)}, u32[]{:S(2)}) collective-permute-start(bf16[8,128,128]{2,1,0:T(8,128)(2,1)S(1)} %get-tuple-element.52), channel_id=1, source_target_pairs={{0,17},{1,16},{2,19},{3,18},{4,21},{5,20},{6,23},{7,22},{8,25},{9,... | collective-permute-start | bytes 786440 | tf_op jit(solution)/shard_map/ppermute | solution.py:32
  67.3 4.7 %collective-permute-start.17 = (bf16[8,128,128]{2,1,0:T(8,128)(2,1)S(1)}, bf16[8,128,128]{2,1,0:T(8,128)(2,1)S(1)}, u32[]{:S(2)}, u32[]{:S(2)}) collective-permute-start(bf16[8,128,128]{2,1,0:T(8,128)(2,1)S(1)} %get-tuple-element.53), channel_id=1, source_target_pairs={{1,18},{2,17},{3,20},{4,19},{5,22},{6,21},{7,24},{8,23},{9,26},{10... | collective-permute-start | bytes 786440 | tf_op jit(solution)/shard_map/ppermute | solution.py:32
  72.0 2.3 %collective-permute-start.10 = (bf16[8,128,128]{2,1,0:T(8,128)(2,1)S(1)}, bf16[8,128,128]{2,1,0:T(8,128)(2,1)S(1)}, u32[]{:S(2)}, u32[]{:S(2)}) collective-permute-start(bf16[8,128,128]{2,1,0:T(8,128)(2,1)S(1)} %get-tuple-element.45), channel_id=1, source_target_pairs={{16,33},{17,32},{18,35},{19,34},{20,37},{21,36},{22,39},{23,38},{2... | collective-permute-start | bytes 786440 | tf_op jit(solution)/shard_map/ppermute | solution.py:32
  74.4 4.1 %collective-permute-start.11 = (bf16[8,128,128]{2,1,0:T(8,128)(2,1)S(1)}, bf16[8,128,128]{2,1,0:T(8,128)(2,1)S(1)}, u32[]{:S(2)}, u32[]{:S(2)}) collective-permute-start(bf16[8,128,128]{2,1,0:T(8,128)(2,1)S(1)} %get-tuple-element.46), channel_id=1, source_target_pairs={{17,34},{18,33},{19,36},{20,35},{21,38},{22,37},{23,40},{24,39},{2... | collective-permute-start | bytes 786440 | tf_op jit(solution)/shard_map/ppermute | solution.py:32
  78.5 2.1 %collective-permute-start.12 = (bf16[8,128,128]{2,1,0:T(8,128)(2,1)S(1)}, bf16[8,128,128]{2,1,0:T(8,128)(2,1)S(1)}, u32[]{:S(2)}, u32[]{:S(2)}) collective-permute-start(bf16[8,128,128]{2,1,0:T(8,128)(2,1)S(1)} %get-tuple-element.47), channel_id=1, source_target_pairs={{16,32},{17,33},{18,34},{19,35},{20,36},{21,37},{22,38},{23,39},{2... | collective-permute-start | bytes 786440 | tf_op jit(solution)/shard_map/ppermute | solution.py:32
  80.7 1.1 %collective-permute-done.17.rest_4_ = bf16[8,128,128]{2,1,0:T(8,128)(2,1)S(1)} collective-permute-done((bf16[8,128,128]{2,1,0:T(8,128)(2,1)S(1)}, bf16[8,128,128]{2,1,0:T(8,128)(2,1)S(1)}, u32[]{:S(2)}, u32[]{:S(2)}) %collective-permute-start.17) | collective-permute-done | bytes 262176 | tf_op jit(solution)/shard_map/ppermute | solution.py:32
  81.8 3.4 %collect_early.1 = (f32[64,128,128]{2,1,0:T(8,128)S(1)}, f32[64,128,128]{2,1,0:T(8,128)}) custom-call(s32[9,1,8]{2,1,0:T(1,128)S(1)} %bitcast.14, f32[8,128,128]{2,1,0:T(8,128)S(1)} %get-tuple-element.49.rest_0_, bf16[8,128,128]{2,1,0:T(8,128)(2,1)S(1)} %collective-permute-done.14.rest_1_, bf16[8,128,128]{2,1,0:T(8,128)(2,1)S(1)} %collective-permute-done.15.rest_2_, ...), custom_call_target="tpu_custom_call" | custom-call | flops 1000000000 | tf_op jit(solution)/shard_map/collect_early/pallas_call | solution.py:478
  85.2 2.3 %collective-permute-done.11.rest_1_ = bf16[8,128,128]{2,1,0:T(8,128)(2,1)S(1)} collective-permute-done((bf16[8,128,128]{2,1,0:T(8,128)(2,1)S(1)}, bf16[8,128,128]{2,1,0:T(8,128)(2,1)S(1)}, u32[]{:S(2)}, u32[]{:S(2)}) %collective-permute-start.11) | collective-permute-done | bytes 262176 | tf_op jit(solution)/shard_map/ppermute | solution.py:32
  87.7 2.6 %collect_late.1 = (f32[64,128,128]{2,1,0:T(8,128)S(1)}, f32[64,128,128]{2,1,0:T(8,128)}) custom-call(s32[9,1,8]{2,1,0:T(1,128)S(1)} %bitcast.15, bf16[8,128,128]{2,1,0:T(8,128)(2,1)S(1)} %collective-permute-done.10.rest_0_, bf16[8,128,128]{2,1,0:T(8,128)(2,1)S(1)} %collective-permute-done.11.rest_1_, ...), custom_call_target="tpu_custom_call", output_to_operand_aliasing={{0}: (5, {}), {1}: (6, {})} | custom-call | tf_op jit(solution)/shard_map/collect_late/pallas_call | solution.py:488
  (33 shorter events, 3.9 us)
Async XLA Ops:
  2.4 3.9 %collective-permute-start.1 = (bf16[24,128,128]{2,1,0:T(8,128)(2,1)S(1)}, bf16[24,128,128]{2,1,0:T(8,128)(2,1)S(1)}, u32[]{:S(2)}, u32[]{:S(2)}) collective-permute-start(bf16[24,128,128]{2,1,0:T(8,128)(2,1)S(1)} %get-tuple-element.32), channel_id=1, source_target_pairs={{0,16},{1,17},{2,18},{3,19},{4,20},{5,21},{6,22},{7,23},{8,24},{9,... | collective-permute-start | bytes 2359304 | tf_op jit(solution)/shard_map/ppermute | solution.py:32
  3.2 13.6 %collective-permute-start = (bf16[24,128,128]{2,1,0:T(8,128)(2,1)S(1)}, bf16[24,128,128]{2,1,0:T(8,128)(2,1)S(1)}, u32[]{:S(2)}, u32[]{:S(2)}) collective-permute-start(bf16[24,128,128]{2,1,0:T(8,128)(2,1)S(1)} %get-tuple-element.30), channel_id=1, source_target_pairs={{16,32},{17,33},{18,34},{19,35},{20,36},{21,37},{22,38},{23,39},{2... | collective-permute-start | bytes 2359304 | tf_op jit(solution)/shard_map/ppermute | solution.py:32
  6.4 25.2 %collective-permute-start.2 = (bf16[16,128,128]{2,1,0:T(8,128)(2,1)S(1)}, bf16[16,128,128]{2,1,0:T(8,128)(2,1)S(1)}, u32[]{:S(2)}, u32[]{:S(2)}) collective-permute-start(bf16[16,128,128]{2,1,0:T(8,128)(2,1)S(1)} %pad_maximum_fusion), channel_id=1, source_target_pairs={{0,1},{1,0},{2,3},{3,2},{4,5},{5,4},{6,7},{7,6},{8,9},{9,8},{10,11... | collective-permute-start | bytes 1572872 | tf_op jit(solution)/shard_map/ppermute | solution.py:32
  8.2 23.5 %collective-permute-start.3 = (bf16[16,128,128]{2,1,0:T(8,128)(2,1)S(1)}, bf16[16,128,128]{2,1,0:T(8,128)(2,1)S(1)}, u32[]{:S(2)}, u32[]{:S(2)}) collective-permute-start(bf16[16,128,128]{2,1,0:T(8,128)(2,1)S(1)} %pad_maximum_fusion.1), channel_id=1, source_target_pairs={{1,2},{2,1},{3,4},{4,3},{5,6},{6,5},{7,8},{8,7},{9,10},{10,9},{11,... | collective-permute-start | bytes 1572872 | tf_op jit(solution)/shard_map/ppermute | solution.py:32
  16.8 14.8 %collective-permute-start.5 = (bf16[8,128,128]{2,1,0:T(8,128)(2,1)S(1)}, bf16[8,128,128]{2,1,0:T(8,128)(2,1)S(1)}, u32[]{:S(2)}, u32[]{:S(2)}) collective-permute-start(bf16[8,128,128]{2,1,0:T(8,128)(2,1)S(1)} %get-tuple-element.57), channel_id=1, source_target_pairs={{1,2},{2,1},{3,4},{4,3},{5,6},{6,5},{7,8},{8,7},{9,10},{10,9},{11,... | collective-permute-start | bytes 786440 | tf_op jit(solution)/shard_map/ppermute | solution.py:32
  22.4 9.2 %copy-start = (s32[4,12,4,4]{1,3,2,0:T(4,128)S(1)}, s32[4,12,4,4]{1,3,2,0:T(4,128)}, u32[]{:S(2)}) copy-start(s32[4,12,4,4]{1,3,2,0:T(4,128)} %param.8) | copy-start | bytes 9220
  22.5 9.2 %copy-start.1 = (f32[4,12,256]{2,0,1:T(4,128)S(1)}, f32[4,12,256]{2,0,1:T(4,128)}, u32[]{:S(2)}) copy-start(f32[4,12,256]{2,0,1:T(4,128)} %param.10) | copy-start | bytes 147460
  22.5 9.2 %collective-permute-start.4 = (bf16[8,128,128]{2,1,0:T(8,128)(2,1)S(1)}, bf16[8,128,128]{2,1,0:T(8,128)(2,1)S(1)}, u32[]{:S(2)}, u32[]{:S(2)}) collective-permute-start(bf16[8,128,128]{2,1,0:T(8,128)(2,1)S(1)} %get-tuple-element.58), channel_id=1, source_target_pairs={{0,1},{1,0},{2,3},{3,2},{4,5},{5,4},{6,7},{7,6},{8,9},{9,8},{10,11... | collective-permute-start | bytes 786440 | tf_op jit(solution)/shard_map/ppermute | solution.py:32
  31.7 19.1 %copy-start.2 = (f32[4,12,256]{2,0,1:T(4,128)S(1)}, f32[4,12,256]{2,0,1:T(4,128)}, u32[]{:S(2)}) copy-start(f32[4,12,256]{2,0,1:T(4,128)} %param.11) | copy-start | bytes 147460
  40.2 4.3 %collective-permute-start.6 = (f32[18,4,256]{2,1,0:T(4,128)S(1)}, f32[18,4,256]{2,1,0:T(4,128)S(1)}, u32[]{:S(2)}, u32[]{:S(2)}) collective-permute-start(f32[18,4,256]{2,1,0:T(4,128)S(1)} %get-tuple-element.37), channel_id=1, source_target_pairs={{0,16},{1,17},{2,18},{3,19},{4,20},{5,21},{6,22},{7,23},{8,24},{9,... | collective-permute-start | bytes 221192 | tf_op jit(solution)/shard_map/ppermute | solution.py:32
  40.8 5.7 %collective-permute-start.7 = (f32[18,4,256]{2,1,0:T(4,128)S(1)}, f32[18,4,256]{2,1,0:T(4,128)S(1)}, u32[]{:S(2)}, u32[]{:S(2)}) collective-permute-start(f32[18,4,256]{2,1,0:T(4,128)S(1)} %get-tuple-element.38), channel_id=1, source_target_pairs={{16,32},{17,33},{18,34},{19,35},{20,36},{21,37},{22,38},{23,39},{2... | collective-permute-start | bytes 221192 | tf_op jit(solution)/shard_map/ppermute | solution.py:32
  46.5 9.8 %collective-permute-start.8 = (f32[5,8,256]{2,1,0:T(8,128)S(1)}, f32[5,8,256]{2,1,0:T(8,128)S(1)}, u32[]{:S(2)}, u32[]{:S(2)}) collective-permute-start(f32[5,8,256]{2,1,0:T(8,128)S(1)} %get-tuple-element.41), channel_id=1, source_target_pairs={{0,1},{1,0},{2,3},{3,2},{4,5},{5,4},{6,7},{7,6},{8,9},{9,8},{10,11... | collective-permute-start | bytes 122888 | tf_op jit(solution)/shard_map/ppermute | solution.py:32
  46.6 9.7 %collective-permute-start.9 = (f32[5,8,256]{2,1,0:T(8,128)S(1)}, f32[5,8,256]{2,1,0:T(8,128)S(1)}, u32[]{:S(2)}, u32[]{:S(2)}) collective-permute-start(f32[5,8,256]{2,1,0:T(8,128)S(1)} %get-tuple-element.42), channel_id=1, source_target_pairs={{1,2},{2,1},{3,4},{4,3},{5,6},{6,5},{7,8},{8,7},{9,10},{10,9},{11,... | collective-permute-start | bytes 122888 | tf_op jit(solution)/shard_map/ppermute | solution.py:32
  56.3 25.6 %copy-start.3 = (s32[1,3,3,8]{3,0,2,1:T(1,128)S(1)}, s32[1,3,3,8]{3,0,2,1:T(1,128)}, u32[]{:S(2)}) copy-start(s32[1,3,3,8]{3,0,2,1:T(1,128)} %param.7) | copy-start | bytes 868
  62.5 11.9 %collective-permute-start.14 = (bf16[8,128,128]{2,1,0:T(8,128)(2,1)S(1)}, bf16[8,128,128]{2,1,0:T(8,128)(2,1)S(1)}, u32[]{:S(2)}, u32[]{:S(2)}) collective-permute-start(bf16[8,128,128]{2,1,0:T(8,128)(2,1)S(1)} %get-tuple-element.50), channel_id=1, source_target_pairs={{0,1},{1,0},{2,3},{3,2},{4,5},{5,4},{6,7},{7,6},{8,9},{9,8},{10,11... | collective-permute-start | bytes 786440 | tf_op jit(solution)/shard_map/ppermute | solution.py:32
  63.4 15.1 %collective-permute-start.15 = (bf16[8,128,128]{2,1,0:T(8,128)(2,1)S(1)}, bf16[8,128,128]{2,1,0:T(8,128)(2,1)S(1)}, u32[]{:S(2)}, u32[]{:S(2)}) collective-permute-start(bf16[8,128,128]{2,1,0:T(8,128)(2,1)S(1)} %get-tuple-element.51), channel_id=1, source_target_pairs={{1,2},{2,1},{3,4},{4,3},{5,6},{6,5},{7,8},{8,7},{9,10},{10,9},{11,... | collective-permute-start | bytes 786440 | tf_op jit(solution)/shard_map/ppermute | solution.py:32
  65.9 14.7 %collective-permute-start.16 = (bf16[8,128,128]{2,1,0:T(8,128)(2,1)S(1)}, bf16[8,128,128]{2,1,0:T(8,128)(2,1)S(1)}, u32[]{:S(2)}, u32[]{:S(2)}) collective-permute-start(bf16[8,128,128]{2,1,0:T(8,128)(2,1)S(1)} %get-tuple-element.52), channel_id=1, source_target_pairs={{0,17},{1,16},{2,19},{3,18},{4,21},{5,20},{6,23},{7,22},{8,25},{9,... | collective-permute-start | bytes 786440 | tf_op jit(solution)/shard_map/ppermute | solution.py:32
  67.3 14.5 %collective-permute-start.17 = (bf16[8,128,128]{2,1,0:T(8,128)(2,1)S(1)}, bf16[8,128,128]{2,1,0:T(8,128)(2,1)S(1)}, u32[]{:S(2)}, u32[]{:S(2)}) collective-permute-start(bf16[8,128,128]{2,1,0:T(8,128)(2,1)S(1)} %get-tuple-element.53), channel_id=1, source_target_pairs={{1,18},{2,17},{3,20},{4,19},{5,22},{6,21},{7,24},{8,23},{9,26},{10... | collective-permute-start | bytes 786440 | tf_op jit(solution)/shard_map/ppermute | solution.py:32
  72.0 13.2 %collective-permute-start.10 = (bf16[8,128,128]{2,1,0:T(8,128)(2,1)S(1)}, bf16[8,128,128]{2,1,0:T(8,128)(2,1)S(1)}, u32[]{:S(2)}, u32[]{:S(2)}) collective-permute-start(bf16[8,128,128]{2,1,0:T(8,128)(2,1)S(1)} %get-tuple-element.45), channel_id=1, source_target_pairs={{16,33},{17,32},{18,35},{19,34},{20,37},{21,36},{22,39},{23,38},{2... | collective-permute-start | bytes 786440 | tf_op jit(solution)/shard_map/ppermute | solution.py:32
  74.4 13.2 %collective-permute-start.11 = (bf16[8,128,128]{2,1,0:T(8,128)(2,1)S(1)}, bf16[8,128,128]{2,1,0:T(8,128)(2,1)S(1)}, u32[]{:S(2)}, u32[]{:S(2)}) collective-permute-start(bf16[8,128,128]{2,1,0:T(8,128)(2,1)S(1)} %get-tuple-element.46), channel_id=1, source_target_pairs={{17,34},{18,33},{19,36},{20,35},{21,38},{22,37},{23,40},{24,39},{2... | collective-permute-start | bytes 786440 | tf_op jit(solution)/shard_map/ppermute | solution.py:32
  78.5 9.2 %collective-permute-start.12 = (bf16[8,128,128]{2,1,0:T(8,128)(2,1)S(1)}, bf16[8,128,128]{2,1,0:T(8,128)(2,1)S(1)}, u32[]{:S(2)}, u32[]{:S(2)}) collective-permute-start(bf16[8,128,128]{2,1,0:T(8,128)(2,1)S(1)} %get-tuple-element.47), channel_id=1, source_target_pairs={{16,32},{17,33},{18,34},{19,35},{20,36},{21,37},{22,38},{23,39},{2... | collective-permute-start | bytes 786440 | tf_op jit(solution)/shard_map/ppermute | solution.py:32
  80.6 7.0 %collective-permute-start.13 = (bf16[8,128,128]{2,1,0:T(8,128)(2,1)S(1)}, bf16[8,128,128]{2,1,0:T(8,128)(2,1)S(1)}, u32[]{:S(2)}, u32[]{:S(2)}) collective-permute-start(bf16[8,128,128]{2,1,0:T(8,128)(2,1)S(1)} %get-tuple-element.48), channel_id=1, source_target_pairs={{0,16},{1,17},{2,18},{3,19},{4,20},{5,21},{6,22},{7,23},{8,24},{9,... | collective-permute-start | bytes 786440 | tf_op jit(solution)/shard_map/ppermute | solution.py:32

commit v5 on v4

--- a/solution.py
+++ b/solution.py
@@ -11,8 +11,8 @@
 CELL_VOLUME = 0.0625
 
 KINDS = ((0, 0), (0, 1), (0, 2), (1, 1), (1, 2), (2, 1), (2, 2), (2, 0), (1, 0))
-SENT = (((0, 0),), ((1, 0), (1, 1), (1, 2)), ((2, 0), (2, 1), (2, 2)), ((0, 1),), ((0, 2),))
-ARRIVED = (((0, 0),), ((1, 0),), ((2, 0),), ((0, 1), (1, 1)), ((0, 2), (1, 2)), ((2, 1),), ((2, 2),))
+SENT = (((0, 0),), ((1, 0), (1, 1), (1, 2)), ((0, 1),), ((0, 2),), ((2, 1),), ((2, 2),), ((2, 0),))
+ARRIVED = (((0, 0),), ((1, 0),), ((0, 1), (1, 1)), ((0, 2), (1, 2)), ((2, 1),), ((2, 2),), ((2, 0),))
 
 
 def partner(index, kind):
@@ -98,14 +98,12 @@
 
 
 def spread(outgoing, depth, sizes):
-    own, to_first, to_second, along_first, along_second = outgoing
+    own, to_first, along_first, along_second, *others = outgoing
     first = swap(to_first, (1, 0), sizes)
-    second = swap(to_second, (2, 0), sizes)
     one = swap(jnp.concatenate([along_first, first[depth : 2 * depth]]), (0, 1), sizes)
     two = swap(jnp.concatenate([along_second, first[2 * depth :]]), (0, 2), sizes)
-    three = swap(second[depth : 2 * depth], (0, 1), sizes)
-    four = swap(second[2 * depth :], (0, 2), sizes)
-    return [own, first, second, one, two, three, four]
+    rest = [swap(blocks, kinds[0], sizes) for blocks, kinds in zip(others, SENT[4:])]
+    return [own, first, one, two, *rest]
 
 
 def transpose_body(basis, after, turned, held, sems):
@@ -160,7 +158,7 @@
 
 
 def density_body(depth, slots, turned, previous, *rest):
-    arrived, (to_first, to_second, kept, blocks) = rest[: len(ARRIVED)], rest[len(ARRIVED) :]
+    arrived, (to_first, to_second, kept, flat, blocks) = rest[: len(ARRIVED)], rest[len(ARRIVED) :]
     brick_x, brick_y, rows, _ = turned.shape
     width = blocks.shape[1]
     per = rows // width
@@ -173,10 +171,11 @@
 
     def step(x, carry):
         for y in range(brick_y):
+            used = [slot_of(slots, x, y, i // per, i % per, empty) for i in range(per * per)]
+            for i, slot in enumerate(used):
+                flat[(x * brick_y + y) * per * per + i] = slot
             lefts = [
-                jnp.concatenate(
-                    [blocks[slot_of(slots, x, y, a, b, empty)] for b in range(per)], axis=1
-                )
+                jnp.concatenate([blocks[slot] for slot in used[a * per : (a + 1) * per]], axis=1)
                 for a in range(per)
             ]
             right = turned[x, y]
@@ -204,8 +203,9 @@
         "density",
         12,
         in_specs=[SMEM] + [VMEM] * (2 + len(arrived)),
-        out_specs=[VMEM] * 3,
-        out_shape=[message, message, pltpu.VMEM(shape, jnp.float32)],
+        out_specs=[VMEM] * 3 + [SMEM],
+        out_shape=[message, message, jax.ShapeDtypeStruct(shape, jnp.float32)]
+        + [jax.ShapeDtypeStruct((brick_x * brick_y * (rows // width) ** 2,), jnp.int32)],
         scratch_shapes=[pltpu.VMEM((len(KINDS) * depth + 1, width, width), turned.dtype)],
     )(slots, turned, previous, *arrived)
 
@@ -327,7 +327,7 @@
 def add_integrals(slots, turned, potential, sums, columns):
     width = sums.shape[1]
     per = turned.shape[2] // width
-    empty = sums.shape[0] - 1
+    brick_y = turned.shape[1]
 
     def step(i, carry):
         for x, y in [(2 * i + j, y) for j in range(2) for y in columns]:
@@ -341,7 +341,7 @@
             )
             for a in range(per):
                 for b in range(per):
-                    slot = slot_of(slots, x, y, a, b, empty)
+                    slot = slots[(x * brick_y + y) * per * per + a * per + b]
                     sums[slot] += product[a * width : (a + 1) * width, b * width : (b + 1) * width]
         return carry
 
@@ -509,15 +509,15 @@
     table_far = pltpu.with_memory_space_constraint(table, pltpu.HBM)
     blocks_far = pltpu.with_memory_space_constraint(density_blocks, pltpu.HBM)
     arrived = spread(gather(table_far, blocks_far), depth, sizes)
-    turned = transposed(basis_values, arrived[2])
-    to_first, to_second, kept = density_of(slots, turned, previous, arrived, depth)
+    turned = transposed(basis_values, arrived[1])
+    to_first, to_second, kept, flat = density_of(slots, turned, previous, arrived, depth)
     second, first = swap(to_second, (2, 0), sizes), swap(to_first, (1, 0), sizes)
     density, sums = copied(kept, (len(KINDS) * depth + 1, width, width))
     field, charge, to_first, to_second = widen(previous, kept, first, second)
     first, second = swap(to_first, (0, 1), sizes), swap(to_second, (0, 2), sizes)
-    sums = integrals_inner(slots, turned, external, field, charge, sums, sizes)
+    sums = integrals_inner(flat, turned, external, field, charge, sums, sizes)
     wide = (field, charge, first, second)
-    hartree, _, *partial = integrals_outer(slots, turned, external, wide, sums, depth, sizes)
+    hartree, _, *partial = integrals_outer(flat, turned, external, wide, sums, depth, sizes)
     returned = [partial[0]] + [swap(m, kind, sizes) for m, kind in zip(partial[1:], KINDS[1:])]
     potential = collect(table, returned, owned)
     return density.transpose(1, 0, 2), hartree.transpose(1, 0, 2), potential

time: 91.4 us -> 90.4 us (0.989)
  waiting for transfers between devices: 13.8 us -> 12.2 us
    ppermute x18, waiting for transfers between devices: 13.8 us -> 12.2 us  [swap(): return lax.ppermute(value, ('gx', 'gy'), pairs)]
  transfers between devices with their start and end apart: 18 -> 18, of which waited for: 6 -> 6; matrix products, arithmetic and copies ran while one was open for 0% -> 0% of each run, Pallas kernels for 17% -> 16%
where the time goes in v5:
time: 90.4 us; the launch traced here: 89.3 us
  starting transfers between devices  42.1 us (47%)
  Pallas kernels  33.8 us (37%)
  waiting for transfers between devices  12.2 us (13%)
  between operations  1.08 us (1%)
    ppermute x18, starting transfers between devices, swap(): return lax.ppermute(value, ('gx', 'gy'), pairs)  42.1 us
    ppermute x18, waiting for transfers between devices, swap(): return lax.ppermute(value, ('gx', 'gy'), pairs)  12.2 us
    pallas_call x1, Pallas kernels, density_of(): call(functools.partial(density_body, depth), 'density', 12, in_specs=[SME...  9.14 us
    pallas_call x1, Pallas kernels, integrals_outer(): call(functools.partial(outer_body, depth, sizes), 'integrals_outer', 12,...  5.69 us
    pallas_call x1, Pallas kernels, transposed(): call(transpose_body, 'transpose', 32, in_specs=[ANY, ANY], out_specs=VMEM...  5.2 us
    pallas_call x1, Pallas kernels, integrals_inner(): call(functools.partial(inner_body, sizes), 'integrals_inner', 8, in_specs...  5.07 us
    pallas_call x1, Pallas kernels, collect(): call(functools.partial(early_body, KINDS[:early]), 'collect_early', 4, in...  3.38 us
    pallas_call x1, Pallas kernels, collect(): call(functools.partial(late_body, KINDS[early:]), 'collect_late', 4, in_s...  2.56 us
  transfers between devices with their start and end apart: 18, of which 6 were waited for; matrix products, arithmetic and copies ran while one was open for 0% of the time, Pallas kernels for 16%

profile of v5, /device:TPU:13, one launch (start us, length us, event | category | flops | bytes accessed | tf_op | source)
XLA Modules:
  0.0 89.3 jit_solution(1673106540318770563)
XLA Ops:
  0.6 1.8 %gather.1 = (bf16[8,128,128]{2,1,0:T(8,128)(2,1)S(1)}, bf16[24,128,128]{2,1,0:T(8,128)(2,1)S(1)}, bf16[8,128,128]{2,1,0:T(8,128)(2,1)S(1)}, bf16[8,128,128]{2,1,...) custom-call(s32[9,1,8]{2,1,0:T(1,128)} %bitcast.11, ...), custom_call_target="tpu_custom_call" | custom-call | tf_op jit(solution)/shard_map/gather/pallas_call | solution.py:82
  3.2 1.9 %collective-permute-done.after.rest_1_ = bf16[24,128,128]{2,1,0:T(8,128)(2,1)S(1)} collective-permute-done((bf16[24,128,128]{2,1,0:T(8,128)(2,1)S(1)}, bf16[24,128,128]{2,1,0:T(8,128)(2,1)S(1)}, u32[]{:S(2)}, u32[]{:S(2)}) %collective-permute-start) | collective-permute-done | bytes 786464 | tf_op jit(solution)/shard_map/ppermute | solution.py:32
  5.2 1.7 %collective-permute-start.1 = (bf16[16,128,128]{2,1,0:T(8,128)(2,1)S(1)}, bf16[16,128,128]{2,1,0:T(8,128)(2,1)S(1)}, u32[]{:S(2)}, u32[]{:S(2)}) collective-permute-start(bf16[16,128,128]{2,1,0:T(8,128)(2,1)S(1)} %pad_maximum_fusion), channel_id=1, source_target_pairs={{0,1},{1,0},{2,3},{3,2},{4,5},{5,4},{6,7},{7,6},{8,9},{9,8},{10,11... | collective-permute-start | bytes 1572872 | tf_op jit(solution)/shard_map/ppermute | solution.py:32
  6.9 4.1 %collective-permute-start.2 = (bf16[16,128,128]{2,1,0:T(8,128)(2,1)S(1)}, bf16[16,128,128]{2,1,0:T(8,128)(2,1)S(1)}, u32[]{:S(2)}, u32[]{:S(2)}) collective-permute-start(bf16[16,128,128]{2,1,0:T(8,128)(2,1)S(1)} %pad_maximum_fusion.1), channel_id=1, source_target_pairs={{1,2},{2,1},{3,4},{4,3},{5,6},{6,5},{7,8},{8,7},{9,10},{10,9},{11,... | collective-permute-start | bytes 1572872 | tf_op jit(solution)/shard_map/ppermute | solution.py:32
  11.1 4.5 %collective-permute-start.3 = (bf16[8,128,128]{2,1,0:T(8,128)(2,1)S(1)}, bf16[8,128,128]{2,1,0:T(8,128)(2,1)S(1)}, u32[]{:S(2)}, u32[]{:S(2)}) collective-permute-start(bf16[8,128,128]{2,1,0:T(8,128)(2,1)S(1)} %get-tuple-element.37), channel_id=1, source_target_pairs={{16,33},{17,32},{18,35},{19,34},{20,37},{21,36},{22,39},{23,38},{2... | collective-permute-start | bytes 786440 | tf_op jit(solution)/shard_map/ppermute | solution.py:32
  15.6 2.5 %collective-permute-start.4 = (bf16[8,128,128]{2,1,0:T(8,128)(2,1)S(1)}, bf16[8,128,128]{2,1,0:T(8,128)(2,1)S(1)}, u32[]{:S(2)}, u32[]{:S(2)}) collective-permute-start(bf16[8,128,128]{2,1,0:T(8,128)(2,1)S(1)} %get-tuple-element.38), channel_id=1, source_target_pairs={{17,34},{18,33},{19,36},{20,35},{21,38},{22,37},{23,40},{24,39},{2... | collective-permute-start | bytes 786440 | tf_op jit(solution)/shard_map/ppermute | solution.py:32
  18.1 3.2 %collective-permute-start.5 = (bf16[8,128,128]{2,1,0:T(8,128)(2,1)S(1)}, bf16[8,128,128]{2,1,0:T(8,128)(2,1)S(1)}, u32[]{:S(2)}, u32[]{:S(2)}) collective-permute-start(bf16[8,128,128]{2,1,0:T(8,128)(2,1)S(1)} %get-tuple-element.39), channel_id=1, source_target_pairs={{16,32},{17,33},{18,34},{19,35},{20,36},{21,37},{22,38},{23,39},{2... | collective-permute-start | bytes 786440 | tf_op jit(solution)/shard_map/ppermute | solution.py:32
  21.4 5.2 %transpose.21.turned = bf16[4,12,512,256]{3,2,1,0:T(8,128)(2,1)S(1)} custom-call(bf16[4,12,4,256,128]{4,3,2,1,0:T(8,128)(2,1)} %basis.1, bf16[24,128,128]{2,1,0:T(8,128)(2,1)S(1)} %collective-permute-done.after.rest_1_), custom_call_target="tpu_custom_call" | custom-call | bytes 25165824 | tf_op jit(solution)/shard_map/transpose/pallas_call | solution.py:130
  26.6 4.7 %collective-permute-done.4.rest_5_ = bf16[8,128,128]{2,1,0:T(8,128)(2,1)S(1)} collective-permute-done((bf16[8,128,128]{2,1,0:T(8,128)(2,1)S(1)}, bf16[8,128,128]{2,1,0:T(8,128)(2,1)S(1)}, u32[]{:S(2)}, u32[]{:S(2)}) %collective-permute-start.4) | collective-permute-done | bytes 262176 | tf_op jit(solution)/shard_map/ppermute | solution.py:32
  31.3 9.1 %density.1 = (f32[18,4,256]{2,1,0:T(4,128)S(1)}, f32[18,4,256]{2,1,0:T(4,128)S(1)}, f32[12,4,256]{2,1,0:T(4,128)S(1)}, s32[768]{0:T(1024)S(1)}) custom-call(s32[4,4,4,12]{3,2,1,0:T(4,128)S(1)} %bitcast.10, bf16[4,12,512,256]{3,2,1,0:T(8,128)(2,1)S(1)} %transpose.21.turned, f32[12,4,256]{2,1,0:T(4,128)S(1)} %bitcast.6, ...), custom_call_target="tpu_custom_call" | custom-call | tf_op jit(solution)/shard_map/density/pallas_call | solution.py:201
  40.5 2.7 %collective-permute-start.7 = (f32[18,4,256]{2,1,0:T(4,128)S(1)}, f32[18,4,256]{2,1,0:T(4,128)S(1)}, u32[]{:S(2)}, u32[]{:S(2)}) collective-permute-start(f32[18,4,256]{2,1,0:T(4,128)S(1)} %get-tuple-element.44), channel_id=1, source_target_pairs={{16,32},{17,33},{18,34},{19,35},{20,36},{21,37},{22,38},{23,39},{2... | collective-permute-start | bytes 221192 | tf_op jit(solution)/shard_map/ppermute | solution.py:32
  44.1 2.1 %collective-permute-done.7.second = f32[18,4,256]{2,1,0:T(4,128)S(1)} collective-permute-done((f32[18,4,256]{2,1,0:T(4,128)S(1)}, f32[18,4,256]{2,1,0:T(4,128)S(1)}, u32[]{:S(2)}, u32[]{:S(2)}) %collective-permute-start.7) | collective-permute-done | bytes 73760 | tf_op jit(solution)/shard_map/ppermute | solution.py:32
  46.4 4.1 %collective-permute-start.9 = (f32[5,8,256]{2,1,0:T(8,128)S(1)}, f32[5,8,256]{2,1,0:T(8,128)S(1)}, u32[]{:S(2)}, u32[]{:S(2)}) collective-permute-start(f32[5,8,256]{2,1,0:T(8,128)S(1)} %get-tuple-element.48), channel_id=1, source_target_pairs={{1,2},{2,1},{3,4},{4,3},{5,6},{6,5},{7,8},{8,7},{9,10},{10,9},{11,... | collective-permute-start | bytes 122888 | tf_op jit(solution)/shard_map/ppermute | solution.py:32
  50.6 5.1 %integrals_inner.1.rest_4_ = f32[73,128,128]{2,1,0:T(8,128)S(1)} custom-call(s32[768]{0:T(1024)S(1)} %get-tuple-element.42.slots, bf16[4,12,512,256]{3,2,1,0:T(8,128)(2,1)S(1)} %transpose.21.turned, f32[12,4,256]{2,1,0:T(4,128)S(1)} %bitcast.8, f32[12,16,256]{2,1,0:T(8,128)S(1)} %get-tuple-element.45.field_x.rest_0_, ...), custom_call_target="tpu_custom_call", output_to_operand_aliasing={{}: (5, {})} | custom-call | flops 3221225472 | tf_op jit(solution)/shard_map/integrals_inner/pallas_call | solution.py:388
  55.7 5.7 %integrals_outer.1 = (f32[12,4,256]{2,1,0:T(4,128)}, f32[73,128,128]{2,1,0:T(8,128)S(1)}, f32[8,128,128]{2,1,0:T(8,128)S(1)}, bf16[8,128,128]{2,1,0:T(8,128)(2,1...) custom-call(s32[768]{0:T(1024)S(1)} %get-tuple-element.42.slots, ...), custom_call_target="tpu_custom_call", output_to_operand_aliasing={{1}: (7, {})} | custom-call | flops 3221225472 | tf_op jit(solution)/shard_map/integrals_outer/pallas_call | solution.py:405
  62.3 2.5 %collective-permute-start.15 = (bf16[8,128,128]{2,1,0:T(8,128)(2,1)S(1)}, bf16[8,128,128]{2,1,0:T(8,128)(2,1)S(1)}, u32[]{:S(2)}, u32[]{:S(2)}) collective-permute-start(bf16[8,128,128]{2,1,0:T(8,128)(2,1)S(1)} %get-tuple-element.57), channel_id=1, source_target_pairs={{1,2},{2,1},{3,4},{4,3},{5,6},{6,5},{7,8},{8,7},{9,10},{10,9},{11,... | collective-permute-start | bytes 786440 | tf_op jit(solution)/shard_map/ppermute | solution.py:32
  64.8 1.7 %collective-permute-start.16 = (bf16[8,128,128]{2,1,0:T(8,128)(2,1)S(1)}, bf16[8,128,128]{2,1,0:T(8,128)(2,1)S(1)}, u32[]{:S(2)}, u32[]{:S(2)}) collective-permute-start(bf16[8,128,128]{2,1,0:T(8,128)(2,1)S(1)} %get-tuple-element.58), channel_id=1, source_target_pairs={{0,17},{1,16},{2,19},{3,18},{4,21},{5,20},{6,23},{7,22},{8,25},{9,... | collective-permute-start | bytes 786440 | tf_op jit(solution)/shard_map/ppermute | solution.py:32
  66.5 4.7 %collective-permute-start.17 = (bf16[8,128,128]{2,1,0:T(8,128)(2,1)S(1)}, bf16[8,128,128]{2,1,0:T(8,128)(2,1)S(1)}, u32[]{:S(2)}, u32[]{:S(2)}) collective-permute-start(bf16[8,128,128]{2,1,0:T(8,128)(2,1)S(1)} %get-tuple-element.59), channel_id=1, source_target_pairs={{1,18},{2,17},{3,20},{4,19},{5,22},{6,21},{7,24},{8,23},{9,26},{10... | collective-permute-start | bytes 786440 | tf_op jit(solution)/shard_map/ppermute | solution.py:32
  71.2 1.9 %collective-permute-start.10 = (bf16[8,128,128]{2,1,0:T(8,128)(2,1)S(1)}, bf16[8,128,128]{2,1,0:T(8,128)(2,1)S(1)}, u32[]{:S(2)}, u32[]{:S(2)}) collective-permute-start(bf16[8,128,128]{2,1,0:T(8,128)(2,1)S(1)} %get-tuple-element.51), channel_id=1, source_target_pairs={{16,33},{17,32},{18,35},{19,34},{20,37},{21,36},{22,39},{23,38},{2... | collective-permute-start | bytes 786440 | tf_op jit(solution)/shard_map/ppermute | solution.py:32
  73.2 4.5 %collective-permute-start.11 = (bf16[8,128,128]{2,1,0:T(8,128)(2,1)S(1)}, bf16[8,128,128]{2,1,0:T(8,128)(2,1)S(1)}, u32[]{:S(2)}, u32[]{:S(2)}) collective-permute-start(bf16[8,128,128]{2,1,0:T(8,128)(2,1)S(1)} %get-tuple-element.52), channel_id=1, source_target_pairs={{17,34},{18,33},{19,36},{20,35},{21,38},{22,37},{23,40},{24,39},{2... | collective-permute-start | bytes 786440 | tf_op jit(solution)/shard_map/ppermute | solution.py:32
  77.7 1.9 %collective-permute-start.12 = (bf16[8,128,128]{2,1,0:T(8,128)(2,1)S(1)}, bf16[8,128,128]{2,1,0:T(8,128)(2,1)S(1)}, u32[]{:S(2)}, u32[]{:S(2)}) collective-permute-start(bf16[8,128,128]{2,1,0:T(8,128)(2,1)S(1)} %get-tuple-element.53), channel_id=1, source_target_pairs={{16,32},{17,33},{18,34},{19,35},{20,36},{21,37},{22,38},{23,39},{2... | collective-permute-start | bytes 786440 | tf_op jit(solution)/shard_map/ppermute | solution.py:32
  80.5 3.4 %collect_early.1 = (f32[64,128,128]{2,1,0:T(8,128)S(1)}, f32[64,128,128]{2,1,0:T(8,128)}) custom-call(s32[9,1,8]{2,1,0:T(1,128)S(1)} %bitcast.12, f32[8,128,128]{2,1,0:T(8,128)S(1)} %get-tuple-element.55.rest_0_, bf16[8,128,128]{2,1,0:T(8,128)(2,1)S(1)} %collective-permute-done.14.rest_1_, bf16[8,128,128]{2,1,0:T(8,128)(2,1)S(1)} %collective-permute-done.15.rest_2_, ...), custom_call_target="tpu_custom_call" | custom-call | flops 1000000000 | tf_op jit(solution)/shard_map/collect_early/pallas_call | solution.py:478
  83.9 2.3 %collective-permute-done.11.rest_1_ = bf16[8,128,128]{2,1,0:T(8,128)(2,1)S(1)} collective-permute-done((bf16[8,128,128]{2,1,0:T(8,128)(2,1)S(1)}, bf16[8,128,128]{2,1,0:T(8,128)(2,1)S(1)}, u32[]{:S(2)}, u32[]{:S(2)}) %collective-permute-start.11) | collective-permute-done | bytes 262176 | tf_op jit(solution)/shard_map/ppermute | solution.py:32
  86.6 2.6 %collect_late.1 = (f32[64,128,128]{2,1,0:T(8,128)S(1)}, f32[64,128,128]{2,1,0:T(8,128)}) custom-call(s32[9,1,8]{2,1,0:T(1,128)S(1)} %bitcast.13, bf16[8,128,128]{2,1,0:T(8,128)(2,1)S(1)} %collective-permute-done.10.rest_0_, bf16[8,128,128]{2,1,0:T(8,128)(2,1)S(1)} %collective-permute-done.11.rest_1_, ...), custom_call_target="tpu_custom_call", output_to_operand_aliasing={{0}: (5, {}), {1}: (6, {})} | custom-call | tf_op jit(solution)/shard_map/collect_late/pallas_call | solution.py:488
  (32 shorter events, 4.4 us)
Async XLA Ops:
  2.4 2.7 %collective-permute-start = (bf16[24,128,128]{2,1,0:T(8,128)(2,1)S(1)}, bf16[24,128,128]{2,1,0:T(8,128)(2,1)S(1)}, u32[]{:S(2)}, u32[]{:S(2)}) collective-permute-start(bf16[24,128,128]{2,1,0:T(8,128)(2,1)S(1)} %get-tuple-element.33), channel_id=1, source_target_pairs={{0,16},{1,17},{2,18},{3,19},{4,20},{5,21},{6,22},{7,23},{8,24},{9,... | collective-permute-start | bytes 2359304 | tf_op jit(solution)/shard_map/ppermute | solution.py:32
  5.2 26.1 %collective-permute-start.1 = (bf16[16,128,128]{2,1,0:T(8,128)(2,1)S(1)}, bf16[16,128,128]{2,1,0:T(8,128)(2,1)S(1)}, u32[]{:S(2)}, u32[]{:S(2)}) collective-permute-start(bf16[16,128,128]{2,1,0:T(8,128)(2,1)S(1)} %pad_maximum_fusion), channel_id=1, source_target_pairs={{0,1},{1,0},{2,3},{3,2},{4,5},{5,4},{6,7},{7,6},{8,9},{9,8},{10,11... | collective-permute-start | bytes 1572872 | tf_op jit(solution)/shard_map/ppermute | solution.py:32
  6.9 24.3 %collective-permute-start.2 = (bf16[16,128,128]{2,1,0:T(8,128)(2,1)S(1)}, bf16[16,128,128]{2,1,0:T(8,128)(2,1)S(1)}, u32[]{:S(2)}, u32[]{:S(2)}) collective-permute-start(bf16[16,128,128]{2,1,0:T(8,128)(2,1)S(1)} %pad_maximum_fusion.1), channel_id=1, source_target_pairs={{1,2},{2,1},{3,4},{4,3},{5,6},{6,5},{7,8},{8,7},{9,10},{10,9},{11,... | collective-permute-start | bytes 1572872 | tf_op jit(solution)/shard_map/ppermute | solution.py:32
  11.1 15.5 %collective-permute-start.3 = (bf16[8,128,128]{2,1,0:T(8,128)(2,1)S(1)}, bf16[8,128,128]{2,1,0:T(8,128)(2,1)S(1)}, u32[]{:S(2)}, u32[]{:S(2)}) collective-permute-start(bf16[8,128,128]{2,1,0:T(8,128)(2,1)S(1)} %get-tuple-element.37), channel_id=1, source_target_pairs={{16,33},{17,32},{18,35},{19,34},{20,37},{21,36},{22,39},{23,38},{2... | collective-permute-start | bytes 786440 | tf_op jit(solution)/shard_map/ppermute | solution.py:32
  15.6 15.6 %collective-permute-start.4 = (bf16[8,128,128]{2,1,0:T(8,128)(2,1)S(1)}, bf16[8,128,128]{2,1,0:T(8,128)(2,1)S(1)}, u32[]{:S(2)}, u32[]{:S(2)}) collective-permute-start(bf16[8,128,128]{2,1,0:T(8,128)(2,1)S(1)} %get-tuple-element.38), channel_id=1, source_target_pairs={{17,34},{18,33},{19,36},{20,35},{21,38},{22,37},{23,40},{24,39},{2... | collective-permute-start | bytes 786440 | tf_op jit(solution)/shard_map/ppermute | solution.py:32
  18.1 13.1 %copy-start = (f32[4,12,256]{2,0,1:T(4,128)S(1)}, f32[4,12,256]{2,0,1:T(4,128)}, u32[]{:S(2)}) copy-start(f32[4,12,256]{2,0,1:T(4,128)} %param.10) | copy-start | bytes 147460
  18.1 13.1 %copy-start.2 = (s32[4,12,4,4]{1,3,2,0:T(4,128)S(1)}, s32[4,12,4,4]{1,3,2,0:T(4,128)}, u32[]{:S(2)}) copy-start(s32[4,12,4,4]{1,3,2,0:T(4,128)} %param.8) | copy-start | bytes 9220
  18.1 13.1 %collective-permute-start.5 = (bf16[8,128,128]{2,1,0:T(8,128)(2,1)S(1)}, bf16[8,128,128]{2,1,0:T(8,128)(2,1)S(1)}, u32[]{:S(2)}, u32[]{:S(2)}) collective-permute-start(bf16[8,128,128]{2,1,0:T(8,128)(2,1)S(1)} %get-tuple-element.39), channel_id=1, source_target_pairs={{16,32},{17,33},{18,34},{19,35},{20,36},{21,37},{22,38},{23,39},{2... | collective-permute-start | bytes 786440 | tf_op jit(solution)/shard_map/ppermute | solution.py:32
  31.3 19.3 %copy-start.1 = (f32[4,12,256]{2,0,1:T(4,128)S(1)}, f32[4,12,256]{2,0,1:T(4,128)}, u32[]{:S(2)}) copy-start(f32[4,12,256]{2,0,1:T(4,128)} %param.11) | copy-start | bytes 147460
  40.4 3.7 %collective-permute-start.6 = (f32[18,4,256]{2,1,0:T(4,128)S(1)}, f32[18,4,256]{2,1,0:T(4,128)S(1)}, u32[]{:S(2)}, u32[]{:S(2)}) collective-permute-start(f32[18,4,256]{2,1,0:T(4,128)S(1)} %get-tuple-element.43), channel_id=1, source_target_pairs={{0,16},{1,17},{2,18},{3,19},{4,20},{5,21},{6,22},{7,23},{8,24},{9,... | collective-permute-start | bytes 221192 | tf_op jit(solution)/shard_map/ppermute | solution.py:32
  40.5 5.8 %collective-permute-start.7 = (f32[18,4,256]{2,1,0:T(4,128)S(1)}, f32[18,4,256]{2,1,0:T(4,128)S(1)}, u32[]{:S(2)}, u32[]{:S(2)}) collective-permute-start(f32[18,4,256]{2,1,0:T(4,128)S(1)} %get-tuple-element.44), channel_id=1, source_target_pairs={{16,32},{17,33},{18,34},{19,35},{20,36},{21,37},{22,38},{23,39},{2... | collective-permute-start | bytes 221192 | tf_op jit(solution)/shard_map/ppermute | solution.py:32
  46.3 9.3 %collective-permute-start.8 = (f32[5,8,256]{2,1,0:T(8,128)S(1)}, f32[5,8,256]{2,1,0:T(8,128)S(1)}, u32[]{:S(2)}, u32[]{:S(2)}) collective-permute-start(f32[5,8,256]{2,1,0:T(8,128)S(1)} %get-tuple-element.47), channel_id=1, source_target_pairs={{0,1},{1,0},{2,3},{3,2},{4,5},{5,4},{6,7},{7,6},{8,9},{9,8},{10,11... | collective-permute-start | bytes 122888 | tf_op jit(solution)/shard_map/ppermute | solution.py:32
  46.4 9.2 %collective-permute-start.9 = (f32[5,8,256]{2,1,0:T(8,128)S(1)}, f32[5,8,256]{2,1,0:T(8,128)S(1)}, u32[]{:S(2)}, u32[]{:S(2)}) collective-permute-start(f32[5,8,256]{2,1,0:T(8,128)S(1)} %get-tuple-element.48), channel_id=1, source_target_pairs={{1,2},{2,1},{3,4},{4,3},{5,6},{6,5},{7,8},{8,7},{9,10},{10,9},{11,... | collective-permute-start | bytes 122888 | tf_op jit(solution)/shard_map/ppermute | solution.py:32
  55.7 24.9 %copy-start.3 = (s32[1,3,3,8]{3,0,2,1:T(1,128)S(1)}, s32[1,3,3,8]{3,0,2,1:T(1,128)}, u32[]{:S(2)}) copy-start(s32[1,3,3,8]{3,0,2,1:T(1,128)} %param.7) | copy-start | bytes 868
  61.4 11.8 %collective-permute-start.14 = (bf16[8,128,128]{2,1,0:T(8,128)(2,1)S(1)}, bf16[8,128,128]{2,1,0:T(8,128)(2,1)S(1)}, u32[]{:S(2)}, u32[]{:S(2)}) collective-permute-start(bf16[8,128,128]{2,1,0:T(8,128)(2,1)S(1)} %get-tuple-element.56), channel_id=1, source_target_pairs={{0,1},{1,0},{2,3},{3,2},{4,5},{5,4},{6,7},{7,6},{8,9},{9,8},{10,11... | collective-permute-start | bytes 786440 | tf_op jit(solution)/shard_map/ppermute | solution.py:32
  62.3 15.4 %collective-permute-start.15 = (bf16[8,128,128]{2,1,0:T(8,128)(2,1)S(1)}, bf16[8,128,128]{2,1,0:T(8,128)(2,1)S(1)}, u32[]{:S(2)}, u32[]{:S(2)}) collective-permute-start(bf16[8,128,128]{2,1,0:T(8,128)(2,1)S(1)} %get-tuple-element.57), channel_id=1, source_target_pairs={{1,2},{2,1},{3,4},{4,3},{5,6},{6,5},{7,8},{8,7},{9,10},{10,9},{11,... | collective-permute-start | bytes 786440 | tf_op jit(solution)/shard_map/ppermute | solution.py:32
  64.8 14.8 %collective-permute-start.16 = (bf16[8,128,128]{2,1,0:T(8,128)(2,1)S(1)}, bf16[8,128,128]{2,1,0:T(8,128)(2,1)S(1)}, u32[]{:S(2)}, u32[]{:S(2)}) collective-permute-start(bf16[8,128,128]{2,1,0:T(8,128)(2,1)S(1)} %get-tuple-element.58), channel_id=1, source_target_pairs={{0,17},{1,16},{2,19},{3,18},{4,21},{5,20},{6,23},{7,22},{8,25},{9,... | collective-permute-start | bytes 786440 | tf_op jit(solution)/shard_map/ppermute | solution.py:32
  66.5 14.0 %collective-permute-start.17 = (bf16[8,128,128]{2,1,0:T(8,128)(2,1)S(1)}, bf16[8,128,128]{2,1,0:T(8,128)(2,1)S(1)}, u32[]{:S(2)}, u32[]{:S(2)}) collective-permute-start(bf16[8,128,128]{2,1,0:T(8,128)(2,1)S(1)} %get-tuple-element.59), channel_id=1, source_target_pairs={{1,18},{2,17},{3,20},{4,19},{5,22},{6,21},{7,24},{8,23},{9,26},{10... | collective-permute-start | bytes 786440 | tf_op jit(solution)/shard_map/ppermute | solution.py:32
  71.2 12.7 %collective-permute-start.10 = (bf16[8,128,128]{2,1,0:T(8,128)(2,1)S(1)}, bf16[8,128,128]{2,1,0:T(8,128)(2,1)S(1)}, u32[]{:S(2)}, u32[]{:S(2)}) collective-permute-start(bf16[8,128,128]{2,1,0:T(8,128)(2,1)S(1)} %get-tuple-element.51), channel_id=1, source_target_pairs={{16,33},{17,32},{18,35},{19,34},{20,37},{21,36},{22,39},{23,38},{2... | collective-permute-start | bytes 786440 | tf_op jit(solution)/shard_map/ppermute | solution.py:32
  73.2 13.0 %collective-permute-start.11 = (bf16[8,128,128]{2,1,0:T(8,128)(2,1)S(1)}, bf16[8,128,128]{2,1,0:T(8,128)(2,1)S(1)}, u32[]{:S(2)}, u32[]{:S(2)}) collective-permute-start(bf16[8,128,128]{2,1,0:T(8,128)(2,1)S(1)} %get-tuple-element.52), channel_id=1, source_target_pairs={{17,34},{18,33},{19,36},{20,35},{21,38},{22,37},{23,40},{24,39},{2... | collective-permute-start | bytes 786440 | tf_op jit(solution)/shard_map/ppermute | solution.py:32
  77.7 8.9 %collective-permute-start.12 = (bf16[8,128,128]{2,1,0:T(8,128)(2,1)S(1)}, bf16[8,128,128]{2,1,0:T(8,128)(2,1)S(1)}, u32[]{:S(2)}, u32[]{:S(2)}) collective-permute-start(bf16[8,128,128]{2,1,0:T(8,128)(2,1)S(1)} %get-tuple-element.53), channel_id=1, source_target_pairs={{16,32},{17,33},{18,34},{19,35},{20,36},{21,37},{22,38},{23,39},{2... | collective-permute-start | bytes 786440 | tf_op jit(solution)/shard_map/ppermute | solution.py:32
  79.6 7.0 %collective-permute-start.13 = (bf16[8,128,128]{2,1,0:T(8,128)(2,1)S(1)}, bf16[8,128,128]{2,1,0:T(8,128)(2,1)S(1)}, u32[]{:S(2)}, u32[]{:S(2)}) collective-permute-start(bf16[8,128,128]{2,1,0:T(8,128)(2,1)S(1)} %get-tuple-element.54), channel_id=1, source_target_pairs={{0,16},{1,17},{2,18},{3,19},{4,20},{5,21},{6,22},{7,23},{8,24},{9,... | collective-permute-start | bytes 786440 | tf_op jit(solution)/shard_map/ppermute | solution.py:32

commit v6 on v5

--- a/solution.py
+++ b/solution.py
@@ -106,7 +106,7 @@
     return [own, first, one, two, *rest]
 
 
-def transpose_body(basis, after, turned, held, sems):
+def transpose_body(empty, basis, after, slots, turned, flat, held, sems):
     brick_x, brick_y, per, _, width = basis.shape
     half = brick_y // 2
     parts = [(x, j) for x in range(brick_x) for j in range(2)]
@@ -123,28 +123,29 @@
         for y in range(j * half, (j + 1) * half):
             for b in range(per):
                 turned[x, y, b * width : (b + 1) * width, :] = held[x, y, b].T
-
-
-def transposed(basis, after):
+            for pair in range(per * per):
+                slot = slots[x, pair // per, pair % per, y]
+                flat[(x * brick_y + y) * per * per + pair] = jnp.where(slot < 0, empty, slot)
+
+
+def transposed(basis, after, slots, empty):
     brick_x, brick_y, per, points, width = basis.shape
     return call(
-        transpose_body,
+        functools.partial(transpose_body, empty),
         "transpose",
         32,
-        in_specs=[ANY, ANY],
-        out_specs=VMEM,
-        out_shape=pltpu.VMEM((brick_x, brick_y, per * width, points), basis.dtype),
+        in_specs=[ANY, ANY, SMEM],
+        out_specs=[VMEM, SMEM],
+        out_shape=[
+            jax.ShapeDtypeStruct((brick_x, brick_y, per * width, points), basis.dtype),
+            jax.ShapeDtypeStruct((brick_x * brick_y * per * per,), jnp.int32),
+        ],
         scratch_shapes=[
             pltpu.VMEM(basis.shape, basis.dtype),
             pltpu.SemaphoreType.DMA((2 * brick_x,)),
         ],
         cost_estimate=pl.CostEstimate(flops=0, bytes_accessed=4 * basis.size, transcendentals=0),
-    )(basis, after)
-
-
-def slot_of(slots, x, y, a, b, empty):
-    slot = slots[x, a, b, y]
-    return jnp.where(slot < 0, empty, slot)
+    )(basis, after, slots)
 
 
 def message_of(out, previous, density, low):
@@ -158,7 +159,7 @@
 
 
 def density_body(depth, slots, turned, previous, *rest):
-    arrived, (to_first, to_second, kept, flat, blocks) = rest[: len(ARRIVED)], rest[len(ARRIVED) :]
+    arrived, (to_first, to_second, kept, blocks) = rest[: len(ARRIVED)], rest[len(ARRIVED) :]
     brick_x, brick_y, rows, _ = turned.shape
     width = blocks.shape[1]
     per = rows // width
@@ -171,9 +172,7 @@
 
     def step(x, carry):
         for y in range(brick_y):
-            used = [slot_of(slots, x, y, i // per, i % per, empty) for i in range(per * per)]
-            for i, slot in enumerate(used):
-                flat[(x * brick_y + y) * per * per + i] = slot
+            used = [slots[(x * brick_y + y) * per * per + i] for i in range(per * per)]
             lefts = [
                 jnp.concatenate([blocks[slot] for slot in used[a * per : (a + 1) * per]], axis=1)
                 for a in range(per)
@@ -203,9 +202,8 @@
         "density",
         12,
         in_specs=[SMEM] + [VMEM] * (2 + len(arrived)),
-        out_specs=[VMEM] * 3 + [SMEM],
-        out_shape=[message, message, jax.ShapeDtypeStruct(shape, jnp.float32)]
-        + [jax.ShapeDtypeStruct((brick_x * brick_y * (rows // width) ** 2,), jnp.int32)],
+        out_specs=[VMEM] * 3,
+        out_shape=[message, message, jax.ShapeDtypeStruct(shape, jnp.float32)],
         scratch_shapes=[pltpu.VMEM((len(KINDS) * depth + 1, width, width), turned.dtype)],
     )(slots, turned, previous, *arrived)
 
@@ -509,8 +507,8 @@
     table_far = pltpu.with_memory_space_constraint(table, pltpu.HBM)
     blocks_far = pltpu.with_memory_space_constraint(density_blocks, pltpu.HBM)
     arrived = spread(gather(table_far, blocks_far), depth, sizes)
-    turned = transposed(basis_values, arrived[1])
-    to_first, to_second, kept, flat = density_of(slots, turned, previous, arrived, depth)
+    turned, flat = transposed(basis_values, arrived[1], slots, len(KINDS) * depth)
+    to_first, to_second, kept = density_of(flat, turned, previous, arrived, depth)
     second, first = swap(to_second, (2, 0), sizes), swap(to_first, (1, 0), sizes)
     density, sums = copied(kept, (len(KINDS) * depth + 1, width, width))
     field, charge, to_first, to_second = widen(previous, kept, first, second)

time: 90.4 us -> 89.2 us (0.987)
  waiting for transfers between devices: 12.2 us -> 10.6 us
    pallas_call x1, Pallas kernels: 5.2 us -> 6.91 us  [transposed(): call(functools.partial(transpose_body, empty), 'transpose', 32, in_specs=...]
    ppermute x18, waiting for transfers between devices: 12.2 us -> 10.6 us  [swap(): return lax.ppermute(value, ('gx', 'gy'), pairs)]
    pallas_call x1, Pallas kernels: 9.14 us -> 8.02 us  [density_of(): call(functools.partial(density_body, depth), 'density', 12, in_specs=[SME...]
  transfers between devices with their start and end apart: 18 -> 18, of which waited for: 6 -> 6; matrix products, arithmetic and copies ran while one was open for 0% -> 0% of each run, Pallas kernels for 16% -> 18%
where the time goes in v6:
time: 89.2 us; the launch traced here: 88.2 us
  starting transfers between devices  42 us (47%)
  Pallas kernels  34.4 us (39%)
  waiting for transfers between devices  10.6 us (12%)
  between operations  1.09 us (1%)
    ppermute x18, starting transfers between devices, swap(): return lax.ppermute(value, ('gx', 'gy'), pairs)  42 us
    ppermute x18, waiting for transfers between devices, swap(): return lax.ppermute(value, ('gx', 'gy'), pairs)  10.6 us
    pallas_call x1, Pallas kernels, density_of(): call(functools.partial(density_body, depth), 'density', 12, in_specs=[SME...  8.02 us
    pallas_call x1, Pallas kernels, transposed(): call(functools.partial(transpose_body, empty), 'transpose', 32, in_specs=...  6.91 us
    pallas_call x1, Pallas kernels, integrals_outer(): call(functools.partial(outer_body, depth, sizes), 'integrals_outer', 12,...  5.69 us
    pallas_call x1, Pallas kernels, integrals_inner(): call(functools.partial(inner_body, sizes), 'integrals_inner', 8, in_specs...  5.06 us
    pallas_call x1, Pallas kernels, collect(): call(functools.partial(early_body, KINDS[:early]), 'collect_early', 4, in...  3.38 us
    pallas_call x1, Pallas kernels, collect(): call(functools.partial(late_body, KINDS[early:]), 'collect_late', 4, in_s...  2.59 us
  transfers between devices with their start and end apart: 18, of which 6 were waited for; matrix products, arithmetic and copies ran while one was open for 0% of the time, Pallas kernels for 18%

profile of v6, /device:TPU:13, one launch (start us, length us, event | category | flops | bytes accessed | tf_op | source)
XLA Modules:
  0.0 88.2 jit_solution(10162555666067032852)
XLA Ops:
  0.6 1.8 %gather.1 = (bf16[8,128,128]{2,1,0:T(8,128)(2,1)S(1)}, bf16[24,128,128]{2,1,0:T(8,128)(2,1)S(1)}, bf16[8,128,128]{2,1,0:T(8,128)(2,1)S(1)}, bf16[8,128,128]{2,1,...) custom-call(s32[9,1,8]{2,1,0:T(1,128)} %bitcast.11, ...), custom_call_target="tpu_custom_call" | custom-call | tf_op jit(solution)/shard_map/gather/pallas_call | solution.py:82
  3.2 1.9 %collective-permute-done.after.rest_1_ = bf16[24,128,128]{2,1,0:T(8,128)(2,1)S(1)} collective-permute-done((bf16[24,128,128]{2,1,0:T(8,128)(2,1)S(1)}, bf16[24,128,128]{2,1,0:T(8,128)(2,1)S(1)}, u32[]{:S(2)}, u32[]{:S(2)}) %collective-permute-start) | collective-permute-done | bytes 786464 | tf_op jit(solution)/shard_map/ppermute | solution.py:32
  5.2 1.7 %collective-permute-start.1 = (bf16[16,128,128]{2,1,0:T(8,128)(2,1)S(1)}, bf16[16,128,128]{2,1,0:T(8,128)(2,1)S(1)}, u32[]{:S(2)}, u32[]{:S(2)}) collective-permute-start(bf16[16,128,128]{2,1,0:T(8,128)(2,1)S(1)} %pad_maximum_fusion), channel_id=1, source_target_pairs={{0,1},{1,0},{2,3},{3,2},{4,5},{5,4},{6,7},{7,6},{8,9},{9,8},{10,11... | collective-permute-start | bytes 1572872 | tf_op jit(solution)/shard_map/ppermute | solution.py:32
  7.0 4.1 %collective-permute-start.2 = (bf16[16,128,128]{2,1,0:T(8,128)(2,1)S(1)}, bf16[16,128,128]{2,1,0:T(8,128)(2,1)S(1)}, u32[]{:S(2)}, u32[]{:S(2)}) collective-permute-start(bf16[16,128,128]{2,1,0:T(8,128)(2,1)S(1)} %pad_maximum_fusion.1), channel_id=1, source_target_pairs={{1,2},{2,1},{3,4},{4,3},{5,6},{6,5},{7,8},{8,7},{9,10},{10,9},{11,... | collective-permute-start | bytes 1572872 | tf_op jit(solution)/shard_map/ppermute | solution.py:32
  11.1 4.5 %collective-permute-start.3 = (bf16[8,128,128]{2,1,0:T(8,128)(2,1)S(1)}, bf16[8,128,128]{2,1,0:T(8,128)(2,1)S(1)}, u32[]{:S(2)}, u32[]{:S(2)}) collective-permute-start(bf16[8,128,128]{2,1,0:T(8,128)(2,1)S(1)} %get-tuple-element.40), channel_id=1, source_target_pairs={{16,33},{17,32},{18,35},{19,34},{20,37},{21,36},{22,39},{23,38},{2... | collective-permute-start | bytes 786440 | tf_op jit(solution)/shard_map/ppermute | solution.py:32
  15.6 2.5 %collective-permute-start.4 = (bf16[8,128,128]{2,1,0:T(8,128)(2,1)S(1)}, bf16[8,128,128]{2,1,0:T(8,128)(2,1)S(1)}, u32[]{:S(2)}, u32[]{:S(2)}) collective-permute-start(bf16[8,128,128]{2,1,0:T(8,128)(2,1)S(1)} %get-tuple-element.41), channel_id=1, source_target_pairs={{17,34},{18,33},{19,36},{20,35},{21,38},{22,37},{23,40},{24,39},{2... | collective-permute-start | bytes 786440 | tf_op jit(solution)/shard_map/ppermute | solution.py:32
  18.1 3.1 %collective-permute-start.5 = (bf16[8,128,128]{2,1,0:T(8,128)(2,1)S(1)}, bf16[8,128,128]{2,1,0:T(8,128)(2,1)S(1)}, u32[]{:S(2)}, u32[]{:S(2)}) collective-permute-start(bf16[8,128,128]{2,1,0:T(8,128)(2,1)S(1)} %get-tuple-element.42), channel_id=1, source_target_pairs={{16,32},{17,33},{18,34},{19,35},{20,36},{21,37},{22,38},{23,39},{2... | collective-permute-start | bytes 786440 | tf_op jit(solution)/shard_map/ppermute | solution.py:32
  21.2 6.9 %transpose.21 = (bf16[4,12,512,256]{3,2,1,0:T(8,128)(2,1)S(1)}, s32[768]{0:T(1024)S(1)}) custom-call(bf16[4,12,4,256,128]{4,3,2,1,0:T(8,128)(2,1)} %basis.1, bf16[24,128,128]{2,1,0:T(8,128)(2,1)S(1)} %collective-permute-done.after.rest_1_, s32[4,4,4,12]{3,2,1,0:T(4,128)S(1)} %bitcast.10), custom_call_target="tpu_custom_call" | custom-call | bytes 25165824 | tf_op jit(solution)/shard_map/transpose/pallas_call | solution.py:133
  28.2 3.1 %collective-permute-done.4.rest_5_ = bf16[8,128,128]{2,1,0:T(8,128)(2,1)S(1)} collective-permute-done((bf16[8,128,128]{2,1,0:T(8,128)(2,1)S(1)}, bf16[8,128,128]{2,1,0:T(8,128)(2,1)S(1)}, u32[]{:S(2)}, u32[]{:S(2)}) %collective-permute-start.4) | collective-permute-done | bytes 262176 | tf_op jit(solution)/shard_map/ppermute | solution.py:32
  31.3 8.0 %density.1 = (f32[18,4,256]{2,1,0:T(4,128)S(1)}, f32[18,4,256]{2,1,0:T(4,128)S(1)}, f32[12,4,256]{2,1,0:T(4,128)S(1)}) custom-call(s32[768]{0:T(1024)S(1)} %get-tuple-element.35.slots, bf16[4,12,512,256]{3,2,1,0:T(8,128)(2,1)S(1)} %get-tuple-element.36.turned, f32[12,4,256]{2,1,0:T(4,128)S(1)} %bitcast.6, ...), custom_call_target="tpu_custom_call" | custom-call | tf_op jit(solution)/shard_map/density/pallas_call | solution.py:200
  39.4 2.7 %collective-permute-start.7 = (f32[18,4,256]{2,1,0:T(4,128)S(1)}, f32[18,4,256]{2,1,0:T(4,128)S(1)}, u32[]{:S(2)}, u32[]{:S(2)}) collective-permute-start(f32[18,4,256]{2,1,0:T(4,128)S(1)} %get-tuple-element.46), channel_id=1, source_target_pairs={{16,32},{17,33},{18,34},{19,35},{20,36},{21,37},{22,38},{23,39},{2... | collective-permute-start | bytes 221192 | tf_op jit(solution)/shard_map/ppermute | solution.py:32
  43.0 2.1 %collective-permute-done.7.second = f32[18,4,256]{2,1,0:T(4,128)S(1)} collective-permute-done((f32[18,4,256]{2,1,0:T(4,128)S(1)}, f32[18,4,256]{2,1,0:T(4,128)S(1)}, u32[]{:S(2)}, u32[]{:S(2)}) %collective-permute-start.7) | collective-permute-done | bytes 73760 | tf_op jit(solution)/shard_map/ppermute | solution.py:32
  45.3 4.1 %collective-permute-start.9 = (f32[5,8,256]{2,1,0:T(8,128)S(1)}, f32[5,8,256]{2,1,0:T(8,128)S(1)}, u32[]{:S(2)}, u32[]{:S(2)}) collective-permute-start(f32[5,8,256]{2,1,0:T(8,128)S(1)} %get-tuple-element.50), channel_id=1, source_target_pairs={{1,2},{2,1},{3,4},{4,3},{5,6},{6,5},{7,8},{8,7},{9,10},{10,9},{11,... | collective-permute-start | bytes 122888 | tf_op jit(solution)/shard_map/ppermute | solution.py:32
  49.5 5.1 %integrals_inner.1.rest_4_ = f32[73,128,128]{2,1,0:T(8,128)S(1)} custom-call(s32[768]{0:T(1024)S(1)} %get-tuple-element.35.slots, bf16[4,12,512,256]{3,2,1,0:T(8,128)(2,1)S(1)} %get-tuple-element.36.turned, f32[12,4,256]{2,1,0:T(4,128)S(1)} %bitcast.8, f32[12,16,256]{2,1,0:T(8,128)S(1)} %get-tuple-element.47.field_x.rest_0_, ...), custom_call_target="tpu_custom_call", output_to_operand_aliasing={{}: (5, {})} | custom-call | flops 3221225472 | tf_op jit(solution)/shard_map/integrals_inner/pallas_call | solution.py:386
  54.6 5.7 %integrals_outer.1 = (f32[12,4,256]{2,1,0:T(4,128)}, f32[73,128,128]{2,1,0:T(8,128)S(1)}, f32[8,128,128]{2,1,0:T(8,128)S(1)}, bf16[8,128,128]{2,1,0:T(8,128)(2,1...) custom-call(s32[768]{0:T(1024)S(1)} %get-tuple-element.35.slots, ...), custom_call_target="tpu_custom_call", output_to_operand_aliasing={{1}: (7, {})} | custom-call | flops 3221225472 | tf_op jit(solution)/shard_map/integrals_outer/pallas_call | solution.py:403
  61.2 2.5 %collective-permute-start.15 = (bf16[8,128,128]{2,1,0:T(8,128)(2,1)S(1)}, bf16[8,128,128]{2,1,0:T(8,128)(2,1)S(1)}, u32[]{:S(2)}, u32[]{:S(2)}) collective-permute-start(bf16[8,128,128]{2,1,0:T(8,128)(2,1)S(1)} %get-tuple-element.59), channel_id=1, source_target_pairs={{1,2},{2,1},{3,4},{4,3},{5,6},{6,5},{7,8},{8,7},{9,10},{10,9},{11,... | collective-permute-start | bytes 786440 | tf_op jit(solution)/shard_map/ppermute | solution.py:32
  63.7 1.7 %collective-permute-start.16 = (bf16[8,128,128]{2,1,0:T(8,128)(2,1)S(1)}, bf16[8,128,128]{2,1,0:T(8,128)(2,1)S(1)}, u32[]{:S(2)}, u32[]{:S(2)}) collective-permute-start(bf16[8,128,128]{2,1,0:T(8,128)(2,1)S(1)} %get-tuple-element.60), channel_id=1, source_target_pairs={{0,17},{1,16},{2,19},{3,18},{4,21},{5,20},{6,23},{7,22},{8,25},{9,... | collective-permute-start | bytes 786440 | tf_op jit(solution)/shard_map/ppermute | solution.py:32
  65.4 4.7 %collective-permute-start.17 = (bf16[8,128,128]{2,1,0:T(8,128)(2,1)S(1)}, bf16[8,128,128]{2,1,0:T(8,128)(2,1)S(1)}, u32[]{:S(2)}, u32[]{:S(2)}) collective-permute-start(bf16[8,128,128]{2,1,0:T(8,128)(2,1)S(1)} %get-tuple-element.61), channel_id=1, source_target_pairs={{1,18},{2,17},{3,20},{4,19},{5,22},{6,21},{7,24},{8,23},{9,26},{10... | collective-permute-start | bytes 786440 | tf_op jit(solution)/shard_map/ppermute | solution.py:32
  70.1 1.9 %collective-permute-start.10 = (bf16[8,128,128]{2,1,0:T(8,128)(2,1)S(1)}, bf16[8,128,128]{2,1,0:T(8,128)(2,1)S(1)}, u32[]{:S(2)}, u32[]{:S(2)}) collective-permute-start(bf16[8,128,128]{2,1,0:T(8,128)(2,1)S(1)} %get-tuple-element.53), channel_id=1, source_target_pairs={{16,33},{17,32},{18,35},{19,34},{20,37},{21,36},{22,39},{23,38},{2... | collective-permute-start | bytes 786440 | tf_op jit(solution)/shard_map/ppermute | solution.py:32
  72.1 4.5 %collective-permute-start.11 = (bf16[8,128,128]{2,1,0:T(8,128)(2,1)S(1)}, bf16[8,128,128]{2,1,0:T(8,128)(2,1)S(1)}, u32[]{:S(2)}, u32[]{:S(2)}) collective-permute-start(bf16[8,128,128]{2,1,0:T(8,128)(2,1)S(1)} %get-tuple-element.54), channel_id=1, source_target_pairs={{17,34},{18,33},{19,36},{20,35},{21,38},{22,37},{23,40},{24,39},{2... | collective-permute-start | bytes 786440 | tf_op jit(solution)/shard_map/ppermute | solution.py:32
  76.6 1.9 %collective-permute-start.12 = (bf16[8,128,128]{2,1,0:T(8,128)(2,1)S(1)}, bf16[8,128,128]{2,1,0:T(8,128)(2,1)S(1)}, u32[]{:S(2)}, u32[]{:S(2)}) collective-permute-start(bf16[8,128,128]{2,1,0:T(8,128)(2,1)S(1)} %get-tuple-element.55), channel_id=1, source_target_pairs={{16,32},{17,33},{18,34},{19,35},{20,36},{21,37},{22,38},{23,39},{2... | collective-permute-start | bytes 786440 | tf_op jit(solution)/shard_map/ppermute | solution.py:32
  79.4 3.4 %collect_early.1 = (f32[64,128,128]{2,1,0:T(8,128)S(1)}, f32[64,128,128]{2,1,0:T(8,128)}) custom-call(s32[9,1,8]{2,1,0:T(1,128)S(1)} %bitcast.12, f32[8,128,128]{2,1,0:T(8,128)S(1)} %get-tuple-element.57.rest_0_, bf16[8,128,128]{2,1,0:T(8,128)(2,1)S(1)} %collective-permute-done.14.rest_1_, bf16[8,128,128]{2,1,0:T(8,128)(2,1)S(1)} %collective-permute-done.15.rest_2_, ...), custom_call_target="tpu_custom_call" | custom-call | flops 1000000000 | tf_op jit(solution)/shard_map/collect_early/pallas_call | solution.py:476
  82.8 2.3 %collective-permute-done.11.rest_1_ = bf16[8,128,128]{2,1,0:T(8,128)(2,1)S(1)} collective-permute-done((bf16[8,128,128]{2,1,0:T(8,128)(2,1)S(1)}, bf16[8,128,128]{2,1,0:T(8,128)(2,1)S(1)}, u32[]{:S(2)}, u32[]{:S(2)}) %collective-permute-start.11) | collective-permute-done | bytes 262176 | tf_op jit(solution)/shard_map/ppermute | solution.py:32
  85.5 2.6 %collect_late.1 = (f32[64,128,128]{2,1,0:T(8,128)S(1)}, f32[64,128,128]{2,1,0:T(8,128)}) custom-call(s32[9,1,8]{2,1,0:T(1,128)S(1)} %bitcast.13, bf16[8,128,128]{2,1,0:T(8,128)(2,1)S(1)} %collective-permute-done.10.rest_0_, bf16[8,128,128]{2,1,0:T(8,128)(2,1)S(1)} %collective-permute-done.11.rest_1_, ...), custom_call_target="tpu_custom_call", output_to_operand_aliasing={{0}: (5, {}), {1}: (6, {})} | custom-call | tf_op jit(solution)/shard_map/collect_late/pallas_call | solution.py:486
  (32 shorter events, 4.3 us)
Async XLA Ops:
  0.6 20.6 %copy-start.2 = (s32[4,12,4,4]{1,3,2,0:T(4,128)S(1)}, s32[4,12,4,4]{1,3,2,0:T(4,128)}, u32[]{:S(2)}) copy-start(s32[4,12,4,4]{1,3,2,0:T(4,128)} %param.8) | copy-start | bytes 9220
  2.4 2.7 %collective-permute-start = (bf16[24,128,128]{2,1,0:T(8,128)(2,1)S(1)}, bf16[24,128,128]{2,1,0:T(8,128)(2,1)S(1)}, u32[]{:S(2)}, u32[]{:S(2)}) collective-permute-start(bf16[24,128,128]{2,1,0:T(8,128)(2,1)S(1)} %get-tuple-element.34), channel_id=1, source_target_pairs={{0,16},{1,17},{2,18},{3,19},{4,20},{5,21},{6,22},{7,23},{8,24},{9,... | collective-permute-start | bytes 2359304 | tf_op jit(solution)/shard_map/ppermute | solution.py:32
  5.2 26.1 %collective-permute-start.1 = (bf16[16,128,128]{2,1,0:T(8,128)(2,1)S(1)}, bf16[16,128,128]{2,1,0:T(8,128)(2,1)S(1)}, u32[]{:S(2)}, u32[]{:S(2)}) collective-permute-start(bf16[16,128,128]{2,1,0:T(8,128)(2,1)S(1)} %pad_maximum_fusion), channel_id=1, source_target_pairs={{0,1},{1,0},{2,3},{3,2},{4,5},{5,4},{6,7},{7,6},{8,9},{9,8},{10,11... | collective-permute-start | bytes 1572872 | tf_op jit(solution)/shard_map/ppermute | solution.py:32
  7.0 24.3 %collective-permute-start.2 = (bf16[16,128,128]{2,1,0:T(8,128)(2,1)S(1)}, bf16[16,128,128]{2,1,0:T(8,128)(2,1)S(1)}, u32[]{:S(2)}, u32[]{:S(2)}) collective-permute-start(bf16[16,128,128]{2,1,0:T(8,128)(2,1)S(1)} %pad_maximum_fusion.1), channel_id=1, source_target_pairs={{1,2},{2,1},{3,4},{4,3},{5,6},{6,5},{7,8},{8,7},{9,10},{10,9},{11,... | collective-permute-start | bytes 1572872 | tf_op jit(solution)/shard_map/ppermute | solution.py:32
  11.1 17.1 %collective-permute-start.3 = (bf16[8,128,128]{2,1,0:T(8,128)(2,1)S(1)}, bf16[8,128,128]{2,1,0:T(8,128)(2,1)S(1)}, u32[]{:S(2)}, u32[]{:S(2)}) collective-permute-start(bf16[8,128,128]{2,1,0:T(8,128)(2,1)S(1)} %get-tuple-element.40), channel_id=1, source_target_pairs={{16,33},{17,32},{18,35},{19,34},{20,37},{21,36},{22,39},{23,38},{2... | collective-permute-start | bytes 786440 | tf_op jit(solution)/shard_map/ppermute | solution.py:32
  15.6 15.6 %collective-permute-start.4 = (bf16[8,128,128]{2,1,0:T(8,128)(2,1)S(1)}, bf16[8,128,128]{2,1,0:T(8,128)(2,1)S(1)}, u32[]{:S(2)}, u32[]{:S(2)}) collective-permute-start(bf16[8,128,128]{2,1,0:T(8,128)(2,1)S(1)} %get-tuple-element.41), channel_id=1, source_target_pairs={{17,34},{18,33},{19,36},{20,35},{21,38},{22,37},{23,40},{24,39},{2... | collective-permute-start | bytes 786440 | tf_op jit(solution)/shard_map/ppermute | solution.py:32
  18.1 13.1 %collective-permute-start.5 = (bf16[8,128,128]{2,1,0:T(8,128)(2,1)S(1)}, bf16[8,128,128]{2,1,0:T(8,128)(2,1)S(1)}, u32[]{:S(2)}, u32[]{:S(2)}) collective-permute-start(bf16[8,128,128]{2,1,0:T(8,128)(2,1)S(1)} %get-tuple-element.42), channel_id=1, source_target_pairs={{16,32},{17,33},{18,34},{19,35},{20,36},{21,37},{22,38},{23,39},{2... | collective-permute-start | bytes 786440 | tf_op jit(solution)/shard_map/ppermute | solution.py:32
  21.2 10.0 %copy-start = (f32[4,12,256]{2,0,1:T(4,128)S(1)}, f32[4,12,256]{2,0,1:T(4,128)}, u32[]{:S(2)}) copy-start(f32[4,12,256]{2,0,1:T(4,128)} %param.10) | copy-start | bytes 147460
  31.3 18.2 %copy-start.1 = (f32[4,12,256]{2,0,1:T(4,128)S(1)}, f32[4,12,256]{2,0,1:T(4,128)}, u32[]{:S(2)}) copy-start(f32[4,12,256]{2,0,1:T(4,128)} %param.11) | copy-start | bytes 147460
  39.3 3.7 %collective-permute-start.6 = (f32[18,4,256]{2,1,0:T(4,128)S(1)}, f32[18,4,256]{2,1,0:T(4,128)S(1)}, u32[]{:S(2)}, u32[]{:S(2)}) collective-permute-start(f32[18,4,256]{2,1,0:T(4,128)S(1)} %get-tuple-element.45), channel_id=1, source_target_pairs={{0,16},{1,17},{2,18},{3,19},{4,20},{5,21},{6,22},{7,23},{8,24},{9,... | collective-permute-start | bytes 221192 | tf_op jit(solution)/shard_map/ppermute | solution.py:32
  39.4 5.8 %collective-permute-start.7 = (f32[18,4,256]{2,1,0:T(4,128)S(1)}, f32[18,4,256]{2,1,0:T(4,128)S(1)}, u32[]{:S(2)}, u32[]{:S(2)}) collective-permute-start(f32[18,4,256]{2,1,0:T(4,128)S(1)} %get-tuple-element.46), channel_id=1, source_target_pairs={{16,32},{17,33},{18,34},{19,35},{20,36},{21,37},{22,38},{23,39},{2... | collective-permute-start | bytes 221192 | tf_op jit(solution)/shard_map/ppermute | solution.py:32
  45.2 9.3 %collective-permute-start.8 = (f32[5,8,256]{2,1,0:T(8,128)S(1)}, f32[5,8,256]{2,1,0:T(8,128)S(1)}, u32[]{:S(2)}, u32[]{:S(2)}) collective-permute-start(f32[5,8,256]{2,1,0:T(8,128)S(1)} %get-tuple-element.49), channel_id=1, source_target_pairs={{0,1},{1,0},{2,3},{3,2},{4,5},{5,4},{6,7},{7,6},{8,9},{9,8},{10,11... | collective-permute-start | bytes 122888 | tf_op jit(solution)/shard_map/ppermute | solution.py:32
  45.3 9.2 %collective-permute-start.9 = (f32[5,8,256]{2,1,0:T(8,128)S(1)}, f32[5,8,256]{2,1,0:T(8,128)S(1)}, u32[]{:S(2)}, u32[]{:S(2)}) collective-permute-start(f32[5,8,256]{2,1,0:T(8,128)S(1)} %get-tuple-element.50), channel_id=1, source_target_pairs={{1,2},{2,1},{3,4},{4,3},{5,6},{6,5},{7,8},{8,7},{9,10},{10,9},{11,... | collective-permute-start | bytes 122888 | tf_op jit(solution)/shard_map/ppermute | solution.py:32
  54.5 24.9 %copy-start.3 = (s32[1,3,3,8]{3,0,2,1:T(1,128)S(1)}, s32[1,3,3,8]{3,0,2,1:T(1,128)}, u32[]{:S(2)}) copy-start(s32[1,3,3,8]{3,0,2,1:T(1,128)} %param.7) | copy-start | bytes 868
  60.3 11.8 %collective-permute-start.14 = (bf16[8,128,128]{2,1,0:T(8,128)(2,1)S(1)}, bf16[8,128,128]{2,1,0:T(8,128)(2,1)S(1)}, u32[]{:S(2)}, u32[]{:S(2)}) collective-permute-start(bf16[8,128,128]{2,1,0:T(8,128)(2,1)S(1)} %get-tuple-element.58), channel_id=1, source_target_pairs={{0,1},{1,0},{2,3},{3,2},{4,5},{5,4},{6,7},{7,6},{8,9},{9,8},{10,11... | collective-permute-start | bytes 786440 | tf_op jit(solution)/shard_map/ppermute | solution.py:32
  61.2 15.4 %collective-permute-start.15 = (bf16[8,128,128]{2,1,0:T(8,128)(2,1)S(1)}, bf16[8,128,128]{2,1,0:T(8,128)(2,1)S(1)}, u32[]{:S(2)}, u32[]{:S(2)}) collective-permute-start(bf16[8,128,128]{2,1,0:T(8,128)(2,1)S(1)} %get-tuple-element.59), channel_id=1, source_target_pairs={{1,2},{2,1},{3,4},{4,3},{5,6},{6,5},{7,8},{8,7},{9,10},{10,9},{11,... | collective-permute-start | bytes 786440 | tf_op jit(solution)/shard_map/ppermute | solution.py:32
  63.7 14.9 %collective-permute-start.16 = (bf16[8,128,128]{2,1,0:T(8,128)(2,1)S(1)}, bf16[8,128,128]{2,1,0:T(8,128)(2,1)S(1)}, u32[]{:S(2)}, u32[]{:S(2)}) collective-permute-start(bf16[8,128,128]{2,1,0:T(8,128)(2,1)S(1)} %get-tuple-element.60), channel_id=1, source_target_pairs={{0,17},{1,16},{2,19},{3,18},{4,21},{5,20},{6,23},{7,22},{8,25},{9,... | collective-permute-start | bytes 786440 | tf_op jit(solution)/shard_map/ppermute | solution.py:32
  65.4 14.0 %collective-permute-start.17 = (bf16[8,128,128]{2,1,0:T(8,128)(2,1)S(1)}, bf16[8,128,128]{2,1,0:T(8,128)(2,1)S(1)}, u32[]{:S(2)}, u32[]{:S(2)}) collective-permute-start(bf16[8,128,128]{2,1,0:T(8,128)(2,1)S(1)} %get-tuple-element.61), channel_id=1, source_target_pairs={{1,18},{2,17},{3,20},{4,19},{5,22},{6,21},{7,24},{8,23},{9,26},{10... | collective-permute-start | bytes 786440 | tf_op jit(solution)/shard_map/ppermute | solution.py:32
  70.1 12.6 %collective-permute-start.10 = (bf16[8,128,128]{2,1,0:T(8,128)(2,1)S(1)}, bf16[8,128,128]{2,1,0:T(8,128)(2,1)S(1)}, u32[]{:S(2)}, u32[]{:S(2)}) collective-permute-start(bf16[8,128,128]{2,1,0:T(8,128)(2,1)S(1)} %get-tuple-element.53), channel_id=1, source_target_pairs={{16,33},{17,32},{18,35},{19,34},{20,37},{21,36},{22,39},{23,38},{2... | collective-permute-start | bytes 786440 | tf_op jit(solution)/shard_map/ppermute | solution.py:32
  72.1 13.0 %collective-permute-start.11 = (bf16[8,128,128]{2,1,0:T(8,128)(2,1)S(1)}, bf16[8,128,128]{2,1,0:T(8,128)(2,1)S(1)}, u32[]{:S(2)}, u32[]{:S(2)}) collective-permute-start(bf16[8,128,128]{2,1,0:T(8,128)(2,1)S(1)} %get-tuple-element.54), channel_id=1, source_target_pairs={{17,34},{18,33},{19,36},{20,35},{21,38},{22,37},{23,40},{24,39},{2... | collective-permute-start | bytes 786440 | tf_op jit(solution)/shard_map/ppermute | solution.py:32
  76.6 8.9 %collective-permute-start.12 = (bf16[8,128,128]{2,1,0:T(8,128)(2,1)S(1)}, bf16[8,128,128]{2,1,0:T(8,128)(2,1)S(1)}, u32[]{:S(2)}, u32[]{:S(2)}) collective-permute-start(bf16[8,128,128]{2,1,0:T(8,128)(2,1)S(1)} %get-tuple-element.55), channel_id=1, source_target_pairs={{16,32},{17,33},{18,34},{19,35},{20,36},{21,37},{22,38},{23,39},{2... | collective-permute-start | bytes 786440 | tf_op jit(solution)/shard_map/ppermute | solution.py:32
  78.6 6.9 %collective-permute-start.13 = (bf16[8,128,128]{2,1,0:T(8,128)(2,1)S(1)}, bf16[8,128,128]{2,1,0:T(8,128)(2,1)S(1)}, u32[]{:S(2)}, u32[]{:S(2)}) collective-permute-start(bf16[8,128,128]{2,1,0:T(8,128)(2,1)S(1)} %get-tuple-element.56), channel_id=1, source_target_pairs={{0,16},{1,17},{2,18},{3,19},{4,20},{5,21},{6,22},{7,23},{8,24},{9,... | collective-permute-start | bytes 786440 | tf_op jit(solution)/shard_map/ppermute | solution.py:32

commit v7 on v6

--- a/solution.py
+++ b/solution.py
@@ -100,8 +100,8 @@
 def spread(outgoing, depth, sizes):
     own, to_first, along_first, along_second, *others = outgoing
     first = swap(to_first, (1, 0), sizes)
+    two = swap(jnp.concatenate([along_second, first[2 * depth :]]), (0, 2), sizes)
     one = swap(jnp.concatenate([along_first, first[depth : 2 * depth]]), (0, 1), sizes)
-    two = swap(jnp.concatenate([along_second, first[2 * depth :]]), (0, 2), sizes)
     rest = [swap(blocks, kinds[0], sizes) for blocks, kinds in zip(others, SENT[4:])]
     return [own, first, one, two, *rest]
 

time: 89.2 us -> 89.3 us (level)
  no operation moved by 1% of the time
where the time goes in v7:
time: 89.3 us; the launch traced here: 88.2 us
  starting transfers between devices  41.9 us (47%)
  Pallas kernels  34.4 us (39%)
  waiting for transfers between devices  10.6 us (12%)
  between operations  1.09 us (1%)
    ppermute x18, starting transfers between devices, swap(): return lax.ppermute(value, ('gx', 'gy'), pairs)  41.9 us
    ppermute x18, waiting for transfers between devices, swap(): return lax.ppermute(value, ('gx', 'gy'), pairs)  10.6 us
    pallas_call x1, Pallas kernels, density_of(): call(functools.partial(density_body, depth), 'density', 12, in_specs=[SME...  8.02 us
    pallas_call x1, Pallas kernels, transposed(): call(functools.partial(transpose_body, empty), 'transpose', 32, in_specs=...  6.91 us
    pallas_call x1, Pallas kernels, integrals_outer(): call(functools.partial(outer_body, depth, sizes), 'integrals_outer', 12,...  5.69 us
    pallas_call x1, Pallas kernels, integrals_inner(): call(functools.partial(inner_body, sizes), 'integrals_inner', 8, in_specs...  5.07 us
    pallas_call x1, Pallas kernels, collect(): call(functools.partial(early_body, KINDS[:early]), 'collect_early', 4, in...  3.38 us
    pallas_call x1, Pallas kernels, collect(): call(functools.partial(late_body, KINDS[early:]), 'collect_late', 4, in_s...  2.59 us
  transfers between devices with their start and end apart: 18, of which 6 were waited for; matrix products, arithmetic and copies ran while one was open for 0% of the time, Pallas kernels for 18%

profile of v7, /device:TPU:13, one launch (start us, length us, event | category | flops | bytes accessed | tf_op | source)
XLA Modules:
  0.0 88.2 jit_solution(10162555666067032852)
XLA Ops:
  0.6 1.8 %gather.1 = (bf16[8,128,128]{2,1,0:T(8,128)(2,1)S(1)}, bf16[24,128,128]{2,1,0:T(8,128)(2,1)S(1)}, bf16[8,128,128]{2,1,0:T(8,128)(2,1)S(1)}, bf16[8,128,128]{2,1,...) custom-call(s32[9,1,8]{2,1,0:T(1,128)} %bitcast.11, ...), custom_call_target="tpu_custom_call" | custom-call | tf_op jit(solution)/shard_map/gather/pallas_call | solution.py:82
  3.2 1.9 %collective-permute-done.after.rest_1_ = bf16[24,128,128]{2,1,0:T(8,128)(2,1)S(1)} collective-permute-done((bf16[24,128,128]{2,1,0:T(8,128)(2,1)S(1)}, bf16[24,128,128]{2,1,0:T(8,128)(2,1)S(1)}, u32[]{:S(2)}, u32[]{:S(2)}) %collective-permute-start) | collective-permute-done | bytes 786464 | tf_op jit(solution)/shard_map/ppermute | solution.py:32
  5.2 1.7 %collective-permute-start.1 = (bf16[16,128,128]{2,1,0:T(8,128)(2,1)S(1)}, bf16[16,128,128]{2,1,0:T(8,128)(2,1)S(1)}, u32[]{:S(2)}, u32[]{:S(2)}) collective-permute-start(bf16[16,128,128]{2,1,0:T(8,128)(2,1)S(1)} %pad_maximum_fusion), channel_id=1, source_target_pairs={{0,1},{1,0},{2,3},{3,2},{4,5},{5,4},{6,7},{7,6},{8,9},{9,8},{10,11... | collective-permute-start | bytes 1572872 | tf_op jit(solution)/shard_map/ppermute | solution.py:32
  7.0 4.1 %collective-permute-start.2 = (bf16[16,128,128]{2,1,0:T(8,128)(2,1)S(1)}, bf16[16,128,128]{2,1,0:T(8,128)(2,1)S(1)}, u32[]{:S(2)}, u32[]{:S(2)}) collective-permute-start(bf16[16,128,128]{2,1,0:T(8,128)(2,1)S(1)} %pad_maximum_fusion.1), channel_id=1, source_target_pairs={{1,2},{2,1},{3,4},{4,3},{5,6},{6,5},{7,8},{8,7},{9,10},{10,9},{11,... | collective-permute-start | bytes 1572872 | tf_op jit(solution)/shard_map/ppermute | solution.py:32
  11.1 4.5 %collective-permute-start.3 = (bf16[8,128,128]{2,1,0:T(8,128)(2,1)S(1)}, bf16[8,128,128]{2,1,0:T(8,128)(2,1)S(1)}, u32[]{:S(2)}, u32[]{:S(2)}) collective-permute-start(bf16[8,128,128]{2,1,0:T(8,128)(2,1)S(1)} %get-tuple-element.40), channel_id=1, source_target_pairs={{16,33},{17,32},{18,35},{19,34},{20,37},{21,36},{22,39},{23,38},{2... | collective-permute-start | bytes 786440 | tf_op jit(solution)/shard_map/ppermute | solution.py:32
  15.6 2.5 %collective-permute-start.4 = (bf16[8,128,128]{2,1,0:T(8,128)(2,1)S(1)}, bf16[8,128,128]{2,1,0:T(8,128)(2,1)S(1)}, u32[]{:S(2)}, u32[]{:S(2)}) collective-permute-start(bf16[8,128,128]{2,1,0:T(8,128)(2,1)S(1)} %get-tuple-element.41), channel_id=1, source_target_pairs={{17,34},{18,33},{19,36},{20,35},{21,38},{22,37},{23,40},{24,39},{2... | collective-permute-start | bytes 786440 | tf_op jit(solution)/shard_map/ppermute | solution.py:32
  18.1 3.1 %collective-permute-start.5 = (bf16[8,128,128]{2,1,0:T(8,128)(2,1)S(1)}, bf16[8,128,128]{2,1,0:T(8,128)(2,1)S(1)}, u32[]{:S(2)}, u32[]{:S(2)}) collective-permute-start(bf16[8,128,128]{2,1,0:T(8,128)(2,1)S(1)} %get-tuple-element.42), channel_id=1, source_target_pairs={{16,32},{17,33},{18,34},{19,35},{20,36},{21,37},{22,38},{23,39},{2... | collective-permute-start | bytes 786440 | tf_op jit(solution)/shard_map/ppermute | solution.py:32
  21.2 6.9 %transpose.21 = (bf16[4,12,512,256]{3,2,1,0:T(8,128)(2,1)S(1)}, s32[768]{0:T(1024)S(1)}) custom-call(bf16[4,12,4,256,128]{4,3,2,1,0:T(8,128)(2,1)} %basis.1, bf16[24,128,128]{2,1,0:T(8,128)(2,1)S(1)} %collective-permute-done.after.rest_1_, s32[4,4,4,12]{3,2,1,0:T(4,128)S(1)} %bitcast.10), custom_call_target="tpu_custom_call" | custom-call | bytes 25165824 | tf_op jit(solution)/shard_map/transpose/pallas_call | solution.py:133
  28.2 3.1 %collective-permute-done.4.rest_5_ = bf16[8,128,128]{2,1,0:T(8,128)(2,1)S(1)} collective-permute-done((bf16[8,128,128]{2,1,0:T(8,128)(2,1)S(1)}, bf16[8,128,128]{2,1,0:T(8,128)(2,1)S(1)}, u32[]{:S(2)}, u32[]{:S(2)}) %collective-permute-start.4) | collective-permute-done | bytes 262176 | tf_op jit(solution)/shard_map/ppermute | solution.py:32
  31.3 8.0 %density.1 = (f32[18,4,256]{2,1,0:T(4,128)S(1)}, f32[18,4,256]{2,1,0:T(4,128)S(1)}, f32[12,4,256]{2,1,0:T(4,128)S(1)}) custom-call(s32[768]{0:T(1024)S(1)} %get-tuple-element.35.slots, bf16[4,12,512,256]{3,2,1,0:T(8,128)(2,1)S(1)} %get-tuple-element.36.turned, f32[12,4,256]{2,1,0:T(4,128)S(1)} %bitcast.6, ...), custom_call_target="tpu_custom_call" | custom-call | tf_op jit(solution)/shard_map/density/pallas_call | solution.py:200
  39.4 2.7 %collective-permute-start.7 = (f32[18,4,256]{2,1,0:T(4,128)S(1)}, f32[18,4,256]{2,1,0:T(4,128)S(1)}, u32[]{:S(2)}, u32[]{:S(2)}) collective-permute-start(f32[18,4,256]{2,1,0:T(4,128)S(1)} %get-tuple-element.46), channel_id=1, source_target_pairs={{16,32},{17,33},{18,34},{19,35},{20,36},{21,37},{22,38},{23,39},{2... | collective-permute-start | bytes 221192 | tf_op jit(solution)/shard_map/ppermute | solution.py:32
  43.0 2.1 %collective-permute-done.7.second = f32[18,4,256]{2,1,0:T(4,128)S(1)} collective-permute-done((f32[18,4,256]{2,1,0:T(4,128)S(1)}, f32[18,4,256]{2,1,0:T(4,128)S(1)}, u32[]{:S(2)}, u32[]{:S(2)}) %collective-permute-start.7) | collective-permute-done | bytes 73760 | tf_op jit(solution)/shard_map/ppermute | solution.py:32
  45.3 4.1 %collective-permute-start.9 = (f32[5,8,256]{2,1,0:T(8,128)S(1)}, f32[5,8,256]{2,1,0:T(8,128)S(1)}, u32[]{:S(2)}, u32[]{:S(2)}) collective-permute-start(f32[5,8,256]{2,1,0:T(8,128)S(1)} %get-tuple-element.50), channel_id=1, source_target_pairs={{1,2},{2,1},{3,4},{4,3},{5,6},{6,5},{7,8},{8,7},{9,10},{10,9},{11,... | collective-permute-start | bytes 122888 | tf_op jit(solution)/shard_map/ppermute | solution.py:32
  49.5 5.1 %integrals_inner.1.rest_4_ = f32[73,128,128]{2,1,0:T(8,128)S(1)} custom-call(s32[768]{0:T(1024)S(1)} %get-tuple-element.35.slots, bf16[4,12,512,256]{3,2,1,0:T(8,128)(2,1)S(1)} %get-tuple-element.36.turned, f32[12,4,256]{2,1,0:T(4,128)S(1)} %bitcast.8, f32[12,16,256]{2,1,0:T(8,128)S(1)} %get-tuple-element.47.field_x.rest_0_, ...), custom_call_target="tpu_custom_call", output_to_operand_aliasing={{}: (5, {})} | custom-call | flops 3221225472 | tf_op jit(solution)/shard_map/integrals_inner/pallas_call | solution.py:386
  54.6 5.7 %integrals_outer.1 = (f32[12,4,256]{2,1,0:T(4,128)}, f32[73,128,128]{2,1,0:T(8,128)S(1)}, f32[8,128,128]{2,1,0:T(8,128)S(1)}, bf16[8,128,128]{2,1,0:T(8,128)(2,1...) custom-call(s32[768]{0:T(1024)S(1)} %get-tuple-element.35.slots, ...), custom_call_target="tpu_custom_call", output_to_operand_aliasing={{1}: (7, {})} | custom-call | flops 3221225472 | tf_op jit(solution)/shard_map/integrals_outer/pallas_call | solution.py:403
  61.3 2.5 %collective-permute-start.15 = (bf16[8,128,128]{2,1,0:T(8,128)(2,1)S(1)}, bf16[8,128,128]{2,1,0:T(8,128)(2,1)S(1)}, u32[]{:S(2)}, u32[]{:S(2)}) collective-permute-start(bf16[8,128,128]{2,1,0:T(8,128)(2,1)S(1)} %get-tuple-element.59), channel_id=1, source_target_pairs={{1,2},{2,1},{3,4},{4,3},{5,6},{6,5},{7,8},{8,7},{9,10},{10,9},{11,... | collective-permute-start | bytes 786440 | tf_op jit(solution)/shard_map/ppermute | solution.py:32
  63.7 1.7 %collective-permute-start.16 = (bf16[8,128,128]{2,1,0:T(8,128)(2,1)S(1)}, bf16[8,128,128]{2,1,0:T(8,128)(2,1)S(1)}, u32[]{:S(2)}, u32[]{:S(2)}) collective-permute-start(bf16[8,128,128]{2,1,0:T(8,128)(2,1)S(1)} %get-tuple-element.60), channel_id=1, source_target_pairs={{0,17},{1,16},{2,19},{3,18},{4,21},{5,20},{6,23},{7,22},{8,25},{9,... | collective-permute-start | bytes 786440 | tf_op jit(solution)/shard_map/ppermute | solution.py:32
  65.4 4.7 %collective-permute-start.17 = (bf16[8,128,128]{2,1,0:T(8,128)(2,1)S(1)}, bf16[8,128,128]{2,1,0:T(8,128)(2,1)S(1)}, u32[]{:S(2)}, u32[]{:S(2)}) collective-permute-start(bf16[8,128,128]{2,1,0:T(8,128)(2,1)S(1)} %get-tuple-element.61), channel_id=1, source_target_pairs={{1,18},{2,17},{3,20},{4,19},{5,22},{6,21},{7,24},{8,23},{9,26},{10... | collective-permute-start | bytes 786440 | tf_op jit(solution)/shard_map/ppermute | solution.py:32
  70.1 1.9 %collective-permute-start.10 = (bf16[8,128,128]{2,1,0:T(8,128)(2,1)S(1)}, bf16[8,128,128]{2,1,0:T(8,128)(2,1)S(1)}, u32[]{:S(2)}, u32[]{:S(2)}) collective-permute-start(bf16[8,128,128]{2,1,0:T(8,128)(2,1)S(1)} %get-tuple-element.53), channel_id=1, source_target_pairs={{16,33},{17,32},{18,35},{19,34},{20,37},{21,36},{22,39},{23,38},{2... | collective-permute-start | bytes 786440 | tf_op jit(solution)/shard_map/ppermute | solution.py:32
  72.0 4.5 %collective-permute-start.11 = (bf16[8,128,128]{2,1,0:T(8,128)(2,1)S(1)}, bf16[8,128,128]{2,1,0:T(8,128)(2,1)S(1)}, u32[]{:S(2)}, u32[]{:S(2)}) collective-permute-start(bf16[8,128,128]{2,1,0:T(8,128)(2,1)S(1)} %get-tuple-element.54), channel_id=1, source_target_pairs={{17,34},{18,33},{19,36},{20,35},{21,38},{22,37},{23,40},{24,39},{2... | collective-permute-start | bytes 786440 | tf_op jit(solution)/shard_map/ppermute | solution.py:32
  76.6 1.9 %collective-permute-start.12 = (bf16[8,128,128]{2,1,0:T(8,128)(2,1)S(1)}, bf16[8,128,128]{2,1,0:T(8,128)(2,1)S(1)}, u32[]{:S(2)}, u32[]{:S(2)}) collective-permute-start(bf16[8,128,128]{2,1,0:T(8,128)(2,1)S(1)} %get-tuple-element.55), channel_id=1, source_target_pairs={{16,32},{17,33},{18,34},{19,35},{20,36},{21,37},{22,38},{23,39},{2... | collective-permute-start | bytes 786440 | tf_op jit(solution)/shard_map/ppermute | solution.py:32
  79.5 3.4 %collect_early.1 = (f32[64,128,128]{2,1,0:T(8,128)S(1)}, f32[64,128,128]{2,1,0:T(8,128)}) custom-call(s32[9,1,8]{2,1,0:T(1,128)S(1)} %bitcast.12, f32[8,128,128]{2,1,0:T(8,128)S(1)} %get-tuple-element.57.rest_0_, bf16[8,128,128]{2,1,0:T(8,128)(2,1)S(1)} %collective-permute-done.14.rest_1_, bf16[8,128,128]{2,1,0:T(8,128)(2,1)S(1)} %collective-permute-done.15.rest_2_, ...), custom_call_target="tpu_custom_call" | custom-call | flops 1000000000 | tf_op jit(solution)/shard_map/collect_early/pallas_call | solution.py:476
  82.9 2.2 %collective-permute-done.11.rest_1_ = bf16[8,128,128]{2,1,0:T(8,128)(2,1)S(1)} collective-permute-done((bf16[8,128,128]{2,1,0:T(8,128)(2,1)S(1)}, bf16[8,128,128]{2,1,0:T(8,128)(2,1)S(1)}, u32[]{:S(2)}, u32[]{:S(2)}) %collective-permute-start.11) | collective-permute-done | bytes 262176 | tf_op jit(solution)/shard_map/ppermute | solution.py:32
  85.5 2.6 %collect_late.1 = (f32[64,128,128]{2,1,0:T(8,128)S(1)}, f32[64,128,128]{2,1,0:T(8,128)}) custom-call(s32[9,1,8]{2,1,0:T(1,128)S(1)} %bitcast.13, bf16[8,128,128]{2,1,0:T(8,128)(2,1)S(1)} %collective-permute-done.10.rest_0_, bf16[8,128,128]{2,1,0:T(8,128)(2,1)S(1)} %collective-permute-done.11.rest_1_, ...), custom_call_target="tpu_custom_call", output_to_operand_aliasing={{0}: (5, {}), {1}: (6, {})} | custom-call | tf_op jit(solution)/shard_map/collect_late/pallas_call | solution.py:486
  (32 shorter events, 4.4 us)
Async XLA Ops:
  0.6 20.6 %copy-start.2 = (s32[4,12,4,4]{1,3,2,0:T(4,128)S(1)}, s32[4,12,4,4]{1,3,2,0:T(4,128)}, u32[]{:S(2)}) copy-start(s32[4,12,4,4]{1,3,2,0:T(4,128)} %param.8) | copy-start | bytes 9220
  2.4 2.7 %collective-permute-start = (bf16[24,128,128]{2,1,0:T(8,128)(2,1)S(1)}, bf16[24,128,128]{2,1,0:T(8,128)(2,1)S(1)}, u32[]{:S(2)}, u32[]{:S(2)}) collective-permute-start(bf16[24,128,128]{2,1,0:T(8,128)(2,1)S(1)} %get-tuple-element.34), channel_id=1, source_target_pairs={{0,16},{1,17},{2,18},{3,19},{4,20},{5,21},{6,22},{7,23},{8,24},{9,... | collective-permute-start | bytes 2359304 | tf_op jit(solution)/shard_map/ppermute | solution.py:32
  5.2 26.1 %collective-permute-start.1 = (bf16[16,128,128]{2,1,0:T(8,128)(2,1)S(1)}, bf16[16,128,128]{2,1,0:T(8,128)(2,1)S(1)}, u32[]{:S(2)}, u32[]{:S(2)}) collective-permute-start(bf16[16,128,128]{2,1,0:T(8,128)(2,1)S(1)} %pad_maximum_fusion), channel_id=1, source_target_pairs={{0,1},{1,0},{2,3},{3,2},{4,5},{5,4},{6,7},{7,6},{8,9},{9,8},{10,11... | collective-permute-start | bytes 1572872 | tf_op jit(solution)/shard_map/ppermute | solution.py:32
  7.0 24.3 %collective-permute-start.2 = (bf16[16,128,128]{2,1,0:T(8,128)(2,1)S(1)}, bf16[16,128,128]{2,1,0:T(8,128)(2,1)S(1)}, u32[]{:S(2)}, u32[]{:S(2)}) collective-permute-start(bf16[16,128,128]{2,1,0:T(8,128)(2,1)S(1)} %pad_maximum_fusion.1), channel_id=1, source_target_pairs={{1,2},{2,1},{3,4},{4,3},{5,6},{6,5},{7,8},{8,7},{9,10},{10,9},{11,... | collective-permute-start | bytes 1572872 | tf_op jit(solution)/shard_map/ppermute | solution.py:32
  11.1 17.1 %collective-permute-start.3 = (bf16[8,128,128]{2,1,0:T(8,128)(2,1)S(1)}, bf16[8,128,128]{2,1,0:T(8,128)(2,1)S(1)}, u32[]{:S(2)}, u32[]{:S(2)}) collective-permute-start(bf16[8,128,128]{2,1,0:T(8,128)(2,1)S(1)} %get-tuple-element.40), channel_id=1, source_target_pairs={{16,33},{17,32},{18,35},{19,34},{20,37},{21,36},{22,39},{23,38},{2... | collective-permute-start | bytes 786440 | tf_op jit(solution)/shard_map/ppermute | solution.py:32
  15.6 15.6 %collective-permute-start.4 = (bf16[8,128,128]{2,1,0:T(8,128)(2,1)S(1)}, bf16[8,128,128]{2,1,0:T(8,128)(2,1)S(1)}, u32[]{:S(2)}, u32[]{:S(2)}) collective-permute-start(bf16[8,128,128]{2,1,0:T(8,128)(2,1)S(1)} %get-tuple-element.41), channel_id=1, source_target_pairs={{17,34},{18,33},{19,36},{20,35},{21,38},{22,37},{23,40},{24,39},{2... | collective-permute-start | bytes 786440 | tf_op jit(solution)/shard_map/ppermute | solution.py:32
  18.1 13.1 %collective-permute-start.5 = (bf16[8,128,128]{2,1,0:T(8,128)(2,1)S(1)}, bf16[8,128,128]{2,1,0:T(8,128)(2,1)S(1)}, u32[]{:S(2)}, u32[]{:S(2)}) collective-permute-start(bf16[8,128,128]{2,1,0:T(8,128)(2,1)S(1)} %get-tuple-element.42), channel_id=1, source_target_pairs={{16,32},{17,33},{18,34},{19,35},{20,36},{21,37},{22,38},{23,39},{2... | collective-permute-start | bytes 786440 | tf_op jit(solution)/shard_map/ppermute | solution.py:32
  21.2 10.0 %copy-start = (f32[4,12,256]{2,0,1:T(4,128)S(1)}, f32[4,12,256]{2,0,1:T(4,128)}, u32[]{:S(2)}) copy-start(f32[4,12,256]{2,0,1:T(4,128)} %param.10) | copy-start | bytes 147460
  31.3 18.2 %copy-start.1 = (f32[4,12,256]{2,0,1:T(4,128)S(1)}, f32[4,12,256]{2,0,1:T(4,128)}, u32[]{:S(2)}) copy-start(f32[4,12,256]{2,0,1:T(4,128)} %param.11) | copy-start | bytes 147460
  39.3 3.7 %collective-permute-start.6 = (f32[18,4,256]{2,1,0:T(4,128)S(1)}, f32[18,4,256]{2,1,0:T(4,128)S(1)}, u32[]{:S(2)}, u32[]{:S(2)}) collective-permute-start(f32[18,4,256]{2,1,0:T(4,128)S(1)} %get-tuple-element.45), channel_id=1, source_target_pairs={{0,16},{1,17},{2,18},{3,19},{4,20},{5,21},{6,22},{7,23},{8,24},{9,... | collective-permute-start | bytes 221192 | tf_op jit(solution)/shard_map/ppermute | solution.py:32
  39.4 5.8 %collective-permute-start.7 = (f32[18,4,256]{2,1,0:T(4,128)S(1)}, f32[18,4,256]{2,1,0:T(4,128)S(1)}, u32[]{:S(2)}, u32[]{:S(2)}) collective-permute-start(f32[18,4,256]{2,1,0:T(4,128)S(1)} %get-tuple-element.46), channel_id=1, source_target_pairs={{16,32},{17,33},{18,34},{19,35},{20,36},{21,37},{22,38},{23,39},{2... | collective-permute-start | bytes 221192 | tf_op jit(solution)/shard_map/ppermute | solution.py:32
  45.2 9.3 %collective-permute-start.8 = (f32[5,8,256]{2,1,0:T(8,128)S(1)}, f32[5,8,256]{2,1,0:T(8,128)S(1)}, u32[]{:S(2)}, u32[]{:S(2)}) collective-permute-start(f32[5,8,256]{2,1,0:T(8,128)S(1)} %get-tuple-element.49), channel_id=1, source_target_pairs={{0,1},{1,0},{2,3},{3,2},{4,5},{5,4},{6,7},{7,6},{8,9},{9,8},{10,11... | collective-permute-start | bytes 122888 | tf_op jit(solution)/shard_map/ppermute | solution.py:32
  45.3 9.2 %collective-permute-start.9 = (f32[5,8,256]{2,1,0:T(8,128)S(1)}, f32[5,8,256]{2,1,0:T(8,128)S(1)}, u32[]{:S(2)}, u32[]{:S(2)}) collective-permute-start(f32[5,8,256]{2,1,0:T(8,128)S(1)} %get-tuple-element.50), channel_id=1, source_target_pairs={{1,2},{2,1},{3,4},{4,3},{5,6},{6,5},{7,8},{8,7},{9,10},{10,9},{11,... | collective-permute-start | bytes 122888 | tf_op jit(solution)/shard_map/ppermute | solution.py:32
  54.5 24.9 %copy-start.3 = (s32[1,3,3,8]{3,0,2,1:T(1,128)S(1)}, s32[1,3,3,8]{3,0,2,1:T(1,128)}, u32[]{:S(2)}) copy-start(s32[1,3,3,8]{3,0,2,1:T(1,128)} %param.7) | copy-start | bytes 868
  60.3 11.8 %collective-permute-start.14 = (bf16[8,128,128]{2,1,0:T(8,128)(2,1)S(1)}, bf16[8,128,128]{2,1,0:T(8,128)(2,1)S(1)}, u32[]{:S(2)}, u32[]{:S(2)}) collective-permute-start(bf16[8,128,128]{2,1,0:T(8,128)(2,1)S(1)} %get-tuple-element.58), channel_id=1, source_target_pairs={{0,1},{1,0},{2,3},{3,2},{4,5},{5,4},{6,7},{7,6},{8,9},{9,8},{10,11... | collective-permute-start | bytes 786440 | tf_op jit(solution)/shard_map/ppermute | solution.py:32
  61.3 15.3 %collective-permute-start.15 = (bf16[8,128,128]{2,1,0:T(8,128)(2,1)S(1)}, bf16[8,128,128]{2,1,0:T(8,128)(2,1)S(1)}, u32[]{:S(2)}, u32[]{:S(2)}) collective-permute-start(bf16[8,128,128]{2,1,0:T(8,128)(2,1)S(1)} %get-tuple-element.59), channel_id=1, source_target_pairs={{1,2},{2,1},{3,4},{4,3},{5,6},{6,5},{7,8},{8,7},{9,10},{10,9},{11,... | collective-permute-start | bytes 786440 | tf_op jit(solution)/shard_map/ppermute | solution.py:32
  63.7 14.8 %collective-permute-start.16 = (bf16[8,128,128]{2,1,0:T(8,128)(2,1)S(1)}, bf16[8,128,128]{2,1,0:T(8,128)(2,1)S(1)}, u32[]{:S(2)}, u32[]{:S(2)}) collective-permute-start(bf16[8,128,128]{2,1,0:T(8,128)(2,1)S(1)} %get-tuple-element.60), channel_id=1, source_target_pairs={{0,17},{1,16},{2,19},{3,18},{4,21},{5,20},{6,23},{7,22},{8,25},{9,... | collective-permute-start | bytes 786440 | tf_op jit(solution)/shard_map/ppermute | solution.py:32
  65.4 14.0 %collective-permute-start.17 = (bf16[8,128,128]{2,1,0:T(8,128)(2,1)S(1)}, bf16[8,128,128]{2,1,0:T(8,128)(2,1)S(1)}, u32[]{:S(2)}, u32[]{:S(2)}) collective-permute-start(bf16[8,128,128]{2,1,0:T(8,128)(2,1)S(1)} %get-tuple-element.61), channel_id=1, source_target_pairs={{1,18},{2,17},{3,20},{4,19},{5,22},{6,21},{7,24},{8,23},{9,26},{10... | collective-permute-start | bytes 786440 | tf_op jit(solution)/shard_map/ppermute | solution.py:32
  70.1 12.7 %collective-permute-start.10 = (bf16[8,128,128]{2,1,0:T(8,128)(2,1)S(1)}, bf16[8,128,128]{2,1,0:T(8,128)(2,1)S(1)}, u32[]{:S(2)}, u32[]{:S(2)}) collective-permute-start(bf16[8,128,128]{2,1,0:T(8,128)(2,1)S(1)} %get-tuple-element.53), channel_id=1, source_target_pairs={{16,33},{17,32},{18,35},{19,34},{20,37},{21,36},{22,39},{23,38},{2... | collective-permute-start | bytes 786440 | tf_op jit(solution)/shard_map/ppermute | solution.py:32
  72.0 13.0 %collective-permute-start.11 = (bf16[8,128,128]{2,1,0:T(8,128)(2,1)S(1)}, bf16[8,128,128]{2,1,0:T(8,128)(2,1)S(1)}, u32[]{:S(2)}, u32[]{:S(2)}) collective-permute-start(bf16[8,128,128]{2,1,0:T(8,128)(2,1)S(1)} %get-tuple-element.54), channel_id=1, source_target_pairs={{17,34},{18,33},{19,36},{20,35},{21,38},{22,37},{23,40},{24,39},{2... | collective-permute-start | bytes 786440 | tf_op jit(solution)/shard_map/ppermute | solution.py:32
  76.6 8.9 %collective-permute-start.12 = (bf16[8,128,128]{2,1,0:T(8,128)(2,1)S(1)}, bf16[8,128,128]{2,1,0:T(8,128)(2,1)S(1)}, u32[]{:S(2)}, u32[]{:S(2)}) collective-permute-start(bf16[8,128,128]{2,1,0:T(8,128)(2,1)S(1)} %get-tuple-element.55), channel_id=1, source_target_pairs={{16,32},{17,33},{18,34},{19,35},{20,36},{21,37},{22,38},{23,39},{2... | collective-permute-start | bytes 786440 | tf_op jit(solution)/shard_map/ppermute | solution.py:32
  78.5 7.0 %collective-permute-start.13 = (bf16[8,128,128]{2,1,0:T(8,128)(2,1)S(1)}, bf16[8,128,128]{2,1,0:T(8,128)(2,1)S(1)}, u32[]{:S(2)}, u32[]{:S(2)}) collective-permute-start(bf16[8,128,128]{2,1,0:T(8,128)(2,1)S(1)} %get-tuple-element.56), channel_id=1, source_target_pairs={{0,16},{1,17},{2,18},{3,19},{4,20},{5,21},{6,22},{7,23},{8,24},{9,... | collective-permute-start | bytes 786440 | tf_op jit(solution)/shard_map/ppermute | solution.py:32
